TPU v7x, 256 devices: a whole 4x4x8 slice. The times are simulated.
256 devices in a mesh: leaf: 64 (over x_lo, z, y), rhs: 4 (over x_hi, core).
Axes of the slice: x: 4 (x_hi: 2, x_lo: 2; x = x_hi * 2 + x_lo), y: 4, z: 8, core: 2. Of those that a mesh axis runs over, the one named last changes fastest.
Arguments:
- rhs_block: bfloat16 [128, 262144], P('rhs', 'leaf'), may hold values from -6 to 6
- col_basis: bfloat16 [64, 262144], P(None, 'leaf'), may hold values from -0.25 to 0.25
- row_basis: bfloat16 [64, 262144], P(None, 'leaf'), may hold values from -0.75 to 0.75
- leaf_transfer: float32 [512, 64, 64], P('leaf'), may hold values from -0.5 to 0.5
- leaf_coupling: float32 [512, 64, 64], P('leaf'), may hold values from -0.75 to 0.75
- inner_transfer: float32 [64, 6, 64, 64], P('leaf'), may hold values from -0.5 to 0.5
- inner_coupling: float32 [64, 6, 64, 64], P('leaf'), may hold values from -0.75 to 0.75
- tree_transfer: float32 [126, 64, 64], replicated, may hold values from -0.5 to 0.5
- tree_coupling: float32 [126, 64, 64], replicated, may hold values from -0.75 to 0.75
- diag_blocks: bfloat16 [512, 512, 512], P('leaf', 'rhs'), may hold values from -0.25 to 0.25
- near_blocks: bfloat16 [512, 2, 512, 512], P('leaf', None, 'rhs'), may hold values from -0.25 to 0.25
- near_leaves: int32 [512, 2], P('leaf'), may hold values from 0 to 511, as said below
Outputs:
- product: float32 [128, 262144], P('rhs', 'leaf')
Inputs may be any that keep to these rules, and one draw needn't show every extreme that they name: `near_leaves`: each entry names another leaf that lies at most 2 leaves from its own leaf; the 2 entries of a leaf differ unless the grid's end folds them together.
All inputs are finite; a program needn't handle non-finite values.
Results may differ from a plain program's by a relative error of at most 0.0021.
Values may be sent and summed in bfloat16 or wider, within the bound.
No kernel may reach another device: no remote copies, remote signals or barrier semaphores. Data moves between devices by JAX's collectives and lax.ppermute only.
A program may use at most 128 MiB of HBM per device.

v0:
```python
import jax
import jax.numpy as jnp
from jax import lax
from jax.sharding import PartitionSpec as P

HIGH = lax.Precision.HIGHEST


def from_partner(block, axis, stride):
    count = lax.axis_size(axis)
    route = []
    for low in range(count):
        high = low | 1 << stride
        if high != low and high < count:
            route += [(low, high), (high, low)]
    return lax.ppermute(block, axis, route)


def extended(array, sides, width):
    for axis, dim in sides:
        size, length = (lax.axis_size(axis), array.shape[dim])
        up = [(i, (i + 1) % size) for i in range(size - 1)]
        down = [(j, i) for i, j in up]
        last = lax.slice_in_dim(array, length - width, length, axis=dim)
        leading = lax.slice_in_dim(array, 0, width, axis=dim)
        before = lax.ppermute(last, axis, up)
        after = lax.ppermute(leading, axis, down)
        array = jnp.concatenate([before, array, after], axis=dim)
    return array


def flip_pairs(values):
    count = values.shape[0]
    return values.reshape((count // 2, 2) + values.shape[1:])[:, ::-1].reshape(values.shape)


def local_mats(table, count):
    return table[0, count - 2 : 2 * count - 2]


def near_terms(grid, count, local_index, diag_part, near_part):
    own = grid[:, 2 : 2 + count]
    slots = jnp.arange(grid.shape[1], dtype=jnp.int32)
    select = (local_index[:, :, None] == slots[None, None, :]).astype(grid.dtype)
    picked = jnp.einsum("ljs,rsn->ljrn", select, grid, preferred_element_type=jnp.float32).astype(
        grid.dtype
    )
    total = jnp.einsum("lmn,rln->lrm", diag_part, own, preferred_element_type=jnp.float32)
    return total + jnp.einsum(
        "ljmn,ljrn->lrm", near_part, picked, preferred_element_type=jnp.float32
    )


def pick_matrix(table, index):
    return lax.dynamic_index_in_dim(table, index, 0, keepdims=False)


def local(
    rhs_block,
    col_basis,
    row_basis,
    leaf_transfer,
    leaf_coupling,
    inner_transfer,
    inner_coupling,
    tree_transfer,
    tree_coupling,
    diag_blocks,
    near_blocks,
    near_leaves,
):
    rows, width = rhs_block.shape
    count = leaf_transfer.shape[0]
    size = width // count
    skel = col_basis.shape[0]
    leaves = rhs_block.reshape(rows, count, size)
    coeffs = jnp.einsum(
        "rlm,klm->lrk",
        leaves,
        col_basis.reshape(skel, count, size),
        preferred_element_type=jnp.float32,
    )
    leaf_terms = jnp.einsum("lrj,lkj->lrk", flip_pairs(coeffs), leaf_coupling, precision=HIGH)
    lifted = jnp.einsum("lrk,lkj->lrj", coeffs, leaf_transfer, precision=HIGH)
    current = lifted.reshape(count // 2, 2, rows, skel).sum(1)
    nodes_here = count // 2
    inner_terms = []
    while nodes_here > 1:
        couple = local_mats(inner_coupling, nodes_here)
        inner_terms.append(jnp.einsum("nrj,nkj->nrk", flip_pairs(current), couple, precision=HIGH))
        transfers = local_mats(inner_transfer, nodes_here)
        lifted = jnp.einsum("nrk,nkj->nrj", current, transfers, precision=HIGH)
        current = lifted.reshape(nodes_here // 2, 2, rows, skel).sum(1)
        nodes_here = nodes_here // 2
    block = current[0]
    device = lax.axis_index("leaf")
    span = lax.axis_size("leaf")
    depth = span.bit_length() - 1
    heap = span + device
    selves = []
    others = []
    current = block
    for bit in range(depth):
        node = heap >> bit
        other = from_partner(current, "leaf", bit)
        selves.append(node)
        others.append(other)
        if bit + 1 < depth:
            mine = pick_matrix(tree_transfer, node - 2)
            theirs = pick_matrix(tree_transfer, (node ^ 1) - 2)
            current = jnp.dot(current, mine, precision=HIGH) + jnp.dot(
                other, theirs, precision=HIGH
            )
    down = None
    for bit in range(depth - 1, -1, -1):
        node = selves[bit]
        term = jnp.einsum(
            "rj,kj->rk", others[bit], pick_matrix(tree_coupling, node - 2), precision=HIGH
        )
        if down is not None:
            term = term + jnp.einsum(
                "rj,kj->rk", down, pick_matrix(tree_transfer, node - 2), precision=HIGH
            )
        down = term
    above = down[None]
    nodes_here = 2
    for terms in reversed(inner_terms):
        transfers = local_mats(inner_transfer, nodes_here)
        above = terms + jnp.einsum(
            "nrj,nkj->nrk", jnp.repeat(above, 2, axis=0), transfers, precision=HIGH
        )
        nodes_here = nodes_here * 2
    leaf_down = leaf_terms + jnp.einsum(
        "lrj,lkj->lrk", jnp.repeat(above, 2, axis=0), leaf_transfer, precision=HIGH
    )
    far = jnp.einsum(
        "lrk,klm->lrm",
        leaf_down.astype(jnp.bfloat16),
        row_basis.reshape(skel, count, size),
        preferred_element_type=jnp.float32,
    )
    padded = extended(rhs_block, (("leaf", 1),), 2 * size)
    local_index = near_leaves - device * count + 2
    piece = lax.all_gather(padded, "rhs", axis=0, tiled=True)
    grid = piece.reshape(piece.shape[0], count + 4, size)
    partial_value = near_terms(grid, count, local_index, diag_blocks, near_blocks)
    close = lax.all_to_all(partial_value, "rhs", split_axis=1, concat_axis=2, tiled=True)
    return jnp.transpose(far + close, (1, 0, 2)).reshape(rows, width)


def solution(mesh):
    in_specs = (
        P("rhs", "leaf"),
        P(None, "leaf"),
        P(None, "leaf"),
        P("leaf", None, None),
        P("leaf", None, None),
        P("leaf", None, None, None),
        P("leaf", None, None, None),
        P(),
        P(),
        P("leaf", "rhs", None),
        P("leaf", None, "rhs", None),
        P("leaf", None),
    )
    out_specs = P("rhs", "leaf")
    return jax.shard_map(local, mesh=mesh, in_specs=in_specs, out_specs=out_specs, check_vma=False)
```

profile of v0, /device:TPU:1, one launch (start us, length us, event | category | flops | bytes accessed | tf_op | source)
XLA Modules:
  0.0 181.1 jit_solution(14342302699608538878)
XLA Ops:
  18.0 18.4 %constant_dynamic-slice_fusion.1 = (f32[1,64,64]{0,2,1:T(8,128)}, f32[1,64,64]{0,2,1:T(8,128)}, f32[1,64,64]{0,2,1:T(8,128)}, f32[1,64,64]{0,2,1:T(8,128)}, f32[...) fusion(f32[126,64,64]{0,2,1:T(8,128)} %param.19, ...), kind=kLoop, calls=%fused_computation.87 | loop fusion | bytes 327720 | tf_op jit(solution)/shard_map/jit(dynamic_index_in_dim)/dynamic_slice | solution.py:55
  36.4 2.3 %copy.73 = f32[1,64,64]{2,1,0:T(8,128)S(1)} copy(f32[1,64,64]{0,2,1:T(8,128)} %get-tuple-element.20) | data formatting | bytes 32768
  39.4 13.3 %constant_dynamic-slice_fusion.15 = (f32[1,64,64]{0,2,1:T(8,128)}, f32[1,64,64]{0,2,1:T(8,128)}, f32[1,64,64]{0,2,1:T(8,128)}, f32[1,64,64]{0,2,1:T(8,128)}, f32[1,64,64]{0,2,1:T(8,128)}, /*index=5*/f32[1,64,64]{0,2,1:T(8,128)}) fusion(f32[126,64,64]{0,2,1:T(8,128)} %param.20, s32[]{:T(128)S(6)} %select_n.44, s32[]{:T(128)S(6)} %select_n.52, ...), kind=kLoop, calls=%fused_computation.101 | loop fusion | bytes 196632 | tf_op jit(solution)/shard_map/jit(dynamic_index_in_dim)/dynamic_slice | solution.py:55
  55.6 2.3 %copy.76 = f32[1,64,64]{2,1,0:T(8,128)S(1)} copy(f32[1,64,64]{0,2,1:T(8,128)} %get-tuple-element.18) | data formatting | bytes 32768
  60.2 2.3 %copy.79 = f32[1,64,64]{2,1,0:T(8,128)S(1)} copy(f32[1,64,64]{0,2,1:T(8,128)} %get-tuple-element.16) | data formatting | bytes 32768
  62.5 2.3 %copy.80 = f32[1,64,64]{2,1,0:T(8,128)S(1)} copy(f32[1,64,64]{0,2,1:T(8,128)} %get-tuple-element.15) | data formatting | bytes 32768
  64.8 2.3 %copy.82 = f32[1,64,64]{2,1,0:T(8,128)S(1)} copy(f32[1,64,64]{0,2,1:T(8,128)} %get-tuple-element.14) | data formatting | bytes 32768
  67.1 2.3 %copy.83 = f32[1,64,64]{2,1,0:T(8,128)S(1)} copy(f32[1,64,64]{0,2,1:T(8,128)} %get-tuple-element.13) | data formatting | bytes 32768
  69.3 2.3 %copy.85 = f32[1,64,64]{2,1,0:T(8,128)S(1)} copy(f32[1,64,64]{0,2,1:T(8,128)} %get-tuple-element.12) | data formatting | bytes 32768
  71.6 2.3 %copy.86 = f32[1,64,64]{2,1,0:T(8,128)S(1)} copy(f32[1,64,64]{0,2,1:T(8,128)} %get-tuple-element.11) | data formatting | bytes 32768
  74.1 4.8 %collective-permute-start.1 = (f32[32,64]{1,0:T(8,128)S(1)}, f32[32,64]{1,0:T(8,128)S(1)}, u32[]{:S(2)}, u32[]{:S(2)}) collective-permute-start(f32[32,64]{1,0:T(8,128)S(1)} %convolution_add_fusion.12), channel_id=1, source_target_pairs={{0,8},{8,0},{4,12},{12,4},{16,24},{24,16},{20,28},{28,20},{32,40},... | collective-permute-start | bytes 24584 | tf_op jit(solution)/shard_map/ppermute | solution.py:16
  80.1 4.2 %collective-permute-start.2 = (f32[32,64]{1,0:T(8,128)S(1)}, f32[32,64]{1,0:T(8,128)S(1)}, u32[]{:S(2)}, u32[]{:S(2)}) collective-permute-start(f32[32,64]{1,0:T(8,128)S(1)} %convolution_add_fusion.10), channel_id=1, source_target_pairs={{0,16},{16,0},{4,20},{20,4},{8,24},{24,8},{12,28},{28,12},{32,48},... | collective-permute-start | bytes 24584 | tf_op jit(solution)/shard_map/ppermute | solution.py:16
  85.6 3.3 %collective-permute-start.3 = (f32[32,64]{1,0:T(8,128)S(1)}, f32[32,64]{1,0:T(8,128)S(1)}, u32[]{:S(2)}, u32[]{:S(2)}) collective-permute-start(f32[32,64]{1,0:T(8,128)S(1)} %convolution_add_fusion.8), channel_id=1, source_target_pairs={{0,32},{32,0},{4,36},{36,4},{8,40},{40,8},{12,44},{44,12},{16,48},... | collective-permute-start | bytes 24584 | tf_op jit(solution)/shard_map/ppermute | solution.py:16
  90.1 7.4 %collective-permute-start.4 = (f32[32,64]{1,0:T(8,128)S(1)}, f32[32,64]{1,0:T(8,128)S(1)}, u32[]{:S(2)}, u32[]{:S(2)}) collective-permute-start(f32[32,64]{1,0:T(8,128)S(1)} %convolution_add_fusion.6), channel_id=1, source_target_pairs={{0,64},{64,0},{4,68},{68,4},{8,72},{72,8},{12,76},{76,12},{16,80},... | collective-permute-start | bytes 24584 | tf_op jit(solution)/shard_map/ppermute | solution.py:16
  103.2 2.3 %copy.84 = f32[1,64,64]{2,1,0:T(8,128)S(1)} copy(f32[1,64,64]{0,2,1:T(8,128)} %get-tuple-element.6) | data formatting | bytes 32768
  105.5 2.3 %copy.81 = f32[1,64,64]{2,1,0:T(8,128)S(1)} copy(f32[1,64,64]{0,2,1:T(8,128)} %get-tuple-element.7) | data formatting | bytes 32768
  107.8 2.3 %copy.78 = f32[1,64,64]{2,1,0:T(8,128)S(1)} copy(f32[1,64,64]{0,2,1:T(8,128)} %get-tuple-element.8) | data formatting | bytes 32768
  110.1 2.3 %copy.75 = f32[1,64,64]{2,1,0:T(8,128)S(1)} copy(f32[1,64,64]{0,2,1:T(8,128)} %get-tuple-element.9) | data formatting | bytes 32768
  112.4 2.3 %copy.72 = f32[1,64,64]{2,1,0:T(8,128)S(1)} copy(f32[1,64,64]{0,2,1:T(8,128)} %get-tuple-element.5) | data formatting | bytes 32768
  118.4 27.6 %all-gather.2.cloned.1.call-done = bf16[128,6144]{1,0:T(8,128)(2,1)} async-done(((bf16[32,6144]{1,0:T(8,128)(2,1)}), bf16[128,6144]{1,0:T(8,128)(2,1)}) %all-gather.2.cloned.1.call-update) | async-done | bytes 1572880 | tf_op jit(solution)/shard_map/all_gather | solution.py:144
  145.9 2.6 %copy.63 = bf16[128,6144]{0,1:T(8,128)(2,1)} copy(bf16[128,6144]{1,0:T(8,128)(2,1)} %all-gather.2.cloned.1.call-done) | data formatting | bytes 3145728 | tf_op jit(solution)/shard_map/all_gather | solution.py:144
  148.5 4.6 %copy.65 = bf16[128,12,512]{2,1,0:T(8,128)(2,1)} copy(bf16[128,12,512]{0,2,1:T(8,128)(2,1)} %bitcast.160) | data formatting | bytes 3145728 | tf_op jit(solution)/shard_map/reshape | solution.py:145
  158.4 3.7 %all-to-all-start = ((f32[8,128,128]{2,0,1:T(8,128)}), f32[8,128,128]{2,0,1:T(8,128)S(1)}, u32[]{:S(2)}, u32[]{:S(2)}) async-start(f32[8,128,128]{2,0,1:T(8,128)} %copy.67), calls=%async_computation | async-start | bytes 1048576 | tf_op jit(solution)/shard_map/all_to_all | solution.py:147
  163.0 8.6 %all-to-all-done = f32[8,128,128]{2,0,1:T(8,128)S(1)} async-done(((f32[8,128,128]{2,0,1:T(8,128)}), f32[8,128,128]{2,0,1:T(8,128)S(1)}, u32[]{:S(2)}, u32[]{:S(2)}) %all-to-all-start) | async-done | bytes 524320 | tf_op jit(solution)/shard_map/all_to_all | solution.py:147
  (84 shorter events, 39.0 us)
Async XLA Ops:
  6.5 149.2 %copy-start = (bf16[8,2,128,512]{3,2,1,0:T(8,128)(2,1)S(1)}, bf16[8,2,128,512]{3,2,1,0:T(8,128)(2,1)}, u32[]{:S(2)}) copy-start(bf16[8,2,128,512]{3,2,1,0:T(8,128)(2,1)} %param.22) | copy-start | bytes 6291460
  6.5 139.4 %all-gather.2.cloned.1.call-start = ((), (), s32[]{:S(2)}) async-start(), calls=%async_computation.1 | async-start | bytes 1966080 | tf_op jit(solution)/shard_map/all_gather | solution.py:144
  11.6 62.3 %collective-permute-start = (f32[32,64]{1,0:T(8,128)S(1)}, f32[32,64]{1,0:T(8,128)S(1)}, u32[]{:S(2)}, u32[]{:S(2)}) collective-permute-start(f32[32,64]{1,0:T(8,128)S(1)} %convolution_bitcast_fusion), channel_id=1, source_target_pairs={{0,4},{4,0},{8,12},{12,8},{16,20},{20,16},{24,28},{28,24},{32,36},... | collective-permute-start | bytes 24584 | tf_op jit(solution)/shard_map/ppermute | solution.py:16
  14.7 100.2 %collective-permute-start.6 = (bf16[32,1024]{1,0:T(8,128)(2,1)S(1)}, bf16[32,1024]{1,0:T(8,128)(2,1)S(1)}, u32[]{:S(2)}, u32[]{:S(2)}) collective-permute-start(bf16[32,1024]{1,0:T(8,128)(2,1)S(1)} %get-tuple-element.21), channel_id=1, source_target_pairs={{0,4},{4,8},{8,12},{12,16},{16,20},{20,24},{24,28},{28,32},{32,36}... | collective-permute-start | bytes 196616 | tf_op jit(solution)/shard_map/ppermute | solution.py:26
  16.6 98.3 %collective-permute-start.7 = (bf16[32,1024]{1,0:T(8,128)(2,1)S(1)}, bf16[32,1024]{1,0:T(8,128)(2,1)S(1)}, u32[]{:S(2)}, u32[]{:S(2)}) collective-permute-start(bf16[32,1024]{1,0:T(8,128)(2,1)S(1)} %get-tuple-element.22), channel_id=1, source_target_pairs={{4,0},{8,4},{12,8},{16,12},{20,16},{24,20},{28,24},{32,28},{36,32}... | collective-permute-start | bytes 196616 | tf_op jit(solution)/shard_map/ppermute | solution.py:27
  36.4 2.3 %copy-start.7 = (f32[1,6,64,64]{3,2,1,0:T(8,128)S(1)}, f32[1,6,64,64]{3,2,1,0:T(8,128)}, u32[]{:S(2)}) copy-start(f32[1,6,64,64]{3,2,1,0:T(8,128)} %param.18) | copy-start | bytes 294916
  39.3 13.3 %copy-start.6 = (f32[8,64,64]{2,1,0:T(8,128)S(1)}, f32[8,64,64]{2,1,0:T(8,128)}, u32[]{:S(2)}) copy-start(f32[8,64,64]{2,1,0:T(8,128)} %param.16) | copy-start | bytes 393220
  69.3 31.6 %copy-start.9 = (s32[8,2]{0,1:T(2,128)S(1)}, s32[8,2]{0,1:T(2,128)}, u32[]{:S(2)}) copy-start(s32[8,2]{0,1:T(2,128)} %param.23) | copy-start | bytes 196
  74.1 5.9 %collective-permute-start.1 = (f32[32,64]{1,0:T(8,128)S(1)}, f32[32,64]{1,0:T(8,128)S(1)}, u32[]{:S(2)}, u32[]{:S(2)}) collective-permute-start(f32[32,64]{1,0:T(8,128)S(1)} %convolution_add_fusion.12), channel_id=1, source_target_pairs={{0,8},{8,0},{4,12},{12,4},{16,24},{24,16},{20,28},{28,20},{32,40},... | collective-permute-start | bytes 24584 | tf_op jit(solution)/shard_map/ppermute | solution.py:16
  80.1 5.3 %collective-permute-start.2 = (f32[32,64]{1,0:T(8,128)S(1)}, f32[32,64]{1,0:T(8,128)S(1)}, u32[]{:S(2)}, u32[]{:S(2)}) collective-permute-start(f32[32,64]{1,0:T(8,128)S(1)} %convolution_add_fusion.10), channel_id=1, source_target_pairs={{0,16},{16,0},{4,20},{20,4},{8,24},{24,8},{12,28},{28,12},{32,48},... | collective-permute-start | bytes 24584 | tf_op jit(solution)/shard_map/ppermute | solution.py:16
  85.6 4.4 %collective-permute-start.3 = (f32[32,64]{1,0:T(8,128)S(1)}, f32[32,64]{1,0:T(8,128)S(1)}, u32[]{:S(2)}, u32[]{:S(2)}) collective-permute-start(f32[32,64]{1,0:T(8,128)S(1)} %convolution_add_fusion.8), channel_id=1, source_target_pairs={{0,32},{32,0},{4,36},{36,4},{8,40},{40,8},{12,44},{44,12},{16,48},... | collective-permute-start | bytes 24584 | tf_op jit(solution)/shard_map/ppermute | solution.py:16
  90.1 8.5 %collective-permute-start.4 = (f32[32,64]{1,0:T(8,128)S(1)}, f32[32,64]{1,0:T(8,128)S(1)}, u32[]{:S(2)}, u32[]{:S(2)}) collective-permute-start(f32[32,64]{1,0:T(8,128)S(1)} %convolution_add_fusion.6), channel_id=1, source_target_pairs={{0,64},{64,0},{4,68},{68,4},{8,72},{72,8},{12,76},{76,12},{16,80},... | collective-permute-start | bytes 24584 | tf_op jit(solution)/shard_map/ppermute | solution.py:16
  98.8 15.9 %collective-permute-start.5 = (f32[32,64]{1,0:T(8,128)S(1)}, f32[32,64]{1,0:T(8,128)S(1)}, u32[]{:S(2)}, u32[]{:S(2)}) collective-permute-start(f32[32,64]{1,0:T(8,128)S(1)} %convolution_add_fusion.4), channel_id=1, source_target_pairs={{0,128},{128,0},{4,132},{132,4},{8,136},{136,8},{12,140},{140,12},... | collective-permute-start | bytes 24584 | tf_op jit(solution)/shard_map/ppermute | solution.py:16
  110.1 4.9 %copy-start.5 = (bf16[32,4096]{1,0:T(8,128)(2,1)S(1)}, bf16[32,4096]{1,0:T(8,128)(2,1)}, u32[]{:S(2)}) copy-start(bf16[32,4096]{1,0:T(8,128)(2,1)} %param.12) | copy-start | bytes 786436
  112.4 5.1 %copy-start.4 = (f32[1,6,64,64]{3,2,1,0:T(8,128)S(1)}, f32[1,6,64,64]{3,2,1,0:T(8,128)}, u32[]{:S(2)}) copy-start(f32[1,6,64,64]{3,2,1,0:T(8,128)} %param.17) | copy-start | bytes 294916
  148.5 4.6 %copy-start.2 = (bf16[8,128,512]{2,1,0:T(8,128)(2,1)S(1)}, bf16[8,128,512]{2,1,0:T(8,128)(2,1)}, u32[]{:S(2)}) copy-start(bf16[8,128,512]{2,1,0:T(8,128)(2,1)} %param.21) | copy-start | bytes 3145732
  153.1 1.9 %copy-start.1 = (bf16[128,12,512]{2,1,0:T(8,128)(2,1)S(1)}, bf16[128,12,512]{2,1,0:T(8,128)(2,1)}, u32[]{:S(2)}) copy-start(bf16[128,12,512]{2,1,0:T(8,128)(2,1)} %copy.65) | copy-start | bytes 4718596
  157.2 4.8 %copy-start.8 = (f32[2,32,64]{2,1,0:T(8,128)S(1)}, f32[2,32,64]{2,1,0:T(8,128)}, u32[]{:S(2)}) copy-start(f32[2,32,64]{2,1,0:T(8,128)} %convolution_add_fusion.3) | copy-start | bytes 49156
  157.2 5.2 %copy-start.3 = (f32[8,64,64]{2,1,0:T(8,128)S(1)}, f32[8,64,64]{2,1,0:T(8,128)}, u32[]{:S(2)}) copy-start(f32[8,64,64]{2,1,0:T(8,128)} %param.15) | copy-start | bytes 393220
  158.4 13.2 %all-to-all-start = ((f32[8,128,128]{2,0,1:T(8,128)}), f32[8,128,128]{2,0,1:T(8,128)S(1)}, u32[]{:S(2)}, u32[]{:S(2)}) async-start(f32[8,128,128]{2,0,1:T(8,128)} %copy.67), calls=%async_computation | async-start | bytes 1048576 | tf_op jit(solution)/shard_map/all_to_all | solution.py:147
Sparse Core Ops, SparseCore 0:
  115.9 30.0 all-gather.1
where the time goes:
time: 182 us; the launch traced here: 181 us
  local copies, waits for them, and re-layouts  79 us (43%)
  waiting for transfers between devices  40.1 us (22%)
  starting transfers between devices  30.9 us (17%)
  matrix products  16.4 us (9%)
  between operations  13.9 us (8%)
    unnamed x36, local copies, waits for them, and re-layouts  36.7 us
    dynamic_slice x2, local copies, waits for them, and re-layouts, pick_matrix(): return lax.dynamic_index_in_dim(table, index, 0, keepdims=False)  31.8 us
    all_gather x1, waiting for transfers between devices, local(): piece = lax.all_gather(padded, 'rhs', axis=0, tiled=True)  27.6 us
    ppermute x6, starting transfers between devices, from_partner(): return lax.ppermute(block, axis, route)  24 us
    all_to_all x1, waiting for transfers between devices, local(): lax.all_to_all(partial_value, 'rhs', split_axis=1, concat_axis=2, tiled=T...  8.6 us
    reshape x1, local copies, waits for them, and re-layouts, local(): grid = piece.reshape(piece.shape[0], count + 4, size)  4.56 us
    ppermute x6, waiting for transfers between devices, from_partner(): return lax.ppermute(block, axis, route)  3.95 us
    all_to_all x1, starting transfers between devices, local(): lax.all_to_all(partial_value, 'rhs', split_axis=1, concat_axis=2, tiled=T...  3.71 us
  transfers between devices with their start and end apart: 10, of which 6 were waited for; matrix products, arithmetic and copies ran while one was open for 42% of the time, Pallas kernels for 0%

commit v1 on v0

v1 whole, which is shorter than its diff:
```python
import functools

import jax
import jax.numpy as jnp
from jax import lax
from jax.experimental import pallas as pl
from jax.experimental.pallas import tpu as pltpu
from jax.sharding import PartitionSpec as P

HIGH = lax.Precision.HIGHEST
F32 = jnp.float32
BF16 = jnp.bfloat16
VMEM = pl.BlockSpec(memory_space=pltpu.VMEM)
ANY = pl.BlockSpec(memory_space=pl.ANY)
PLAIN = (((1,), (0,)), ((), ()))
TURNED = (((1,), (1,)), ((), ()))


def halves(x):
    top = x.astype(BF16)
    return top, (x - top.astype(F32)).astype(BF16)


def dot3(a, b, dims=PLAIN):
    ah, al = halves(a)
    bh, bl = halves(b)
    dot = functools.partial(lax.dot_general, dimension_numbers=dims, preferred_element_type=F32)
    return dot(ah, bh) + (dot(ah, bl) + dot(al, bh))


def swapped(x, axis, bit):
    count = lax.axis_size(axis)
    return lax.ppermute(x, axis, [(i, i ^ bit) for i in range(count)])


def limit(mib):
    return pltpu.CompilerParams(vmem_limit_bytes=mib << 20)


def in_hbm(x):
    return pltpu.with_memory_space_constraint(x, pltpu.HBM)


def fetched(pairs, sems):
    copies = []
    for at, (source, target) in enumerate(pairs):
        copy = pltpu.make_async_copy(source, target, sems.at[at])
        copy.start()
        copies.append(copy)
    return copies


def up_kernel(
    rhs_hbm, cols_hbm, leaf_hbm, inner_hbm, coeffs, second, first, block, rhs, cols, leaf_tr, inner_tr, sems
):
    half = rhs.shape[1] // 2
    size = rhs.shape[1] // 8
    pairs = []
    for side in range(2):
        span = pl.ds(side * half, half)
        pairs += [(rhs_hbm.at[:, span], rhs.at[:, span]), (cols_hbm.at[:, span], cols.at[:, span])]
    pairs += [(leaf_hbm, leaf_tr), (inner_hbm, inner_tr)]
    copies = fetched(pairs, sems)
    parts = []
    for leaf in range(8):
        if leaf % 4 == 0:
            copies[leaf // 2].wait()
            copies[leaf // 2 + 1].wait()
        span = slice(leaf * size, (leaf + 1) * size)
        parts.append(
            lax.dot_general(rhs[:, span], cols[:, span], TURNED, preferred_element_type=F32)
        )
    copies[4].wait()
    copies[5].wait()
    ups = []
    for pair in range(4):
        both = jnp.concatenate(parts[2 * pair : 2 * pair + 2], axis=1)
        coeffs[:, pair * 128 : (pair + 1) * 128] = both
        ups.append(dot3(both, leaf_tr[pair]))
    left = jnp.concatenate(ups[:2], axis=1)
    right = jnp.concatenate(ups[2:], axis=1)
    second[:, :128] = left
    second[:, 128:] = right
    both = jnp.concatenate([dot3(left, inner_tr[1]), dot3(right, inner_tr[2])], axis=1)
    first[...] = both
    block[...] = dot3(both, inner_tr[0])


def run_up(rhs, cols, leaf_tr, inner_tr):
    rows = rhs.shape[0]
    skel = cols.shape[0]
    return pl.pallas_call(
        up_kernel,
        in_specs=[ANY] * 4,
        out_specs=[VMEM] * 4,
        out_shape=[
            pltpu.VMEM((rows, 8 * skel), F32),
            pltpu.VMEM((rows, 4 * skel), F32),
            pltpu.VMEM((rows, 2 * skel), F32),
            pltpu.VMEM((rows, skel), F32),
        ],
        scratch_shapes=[pltpu.VMEM(x.shape, x.dtype) for x in (rhs, cols, leaf_tr, inner_tr)]
        + [pltpu.SemaphoreType.DMA((6,))],
        compiler_params=limit(4),
        cost_estimate=pl.CostEstimate(flops=200_000_000, bytes_accessed=2_000_000, transcendentals=0),
        name="up",
    )(*map(in_hbm, (rhs, cols, leaf_tr, inner_tr)))


def sides_kernel(own, mate, after, out, sems):
    del after
    wide = out.shape[1] // 2
    core = lax.rem(lax.axis_index("rhs"), 2)
    start = pl.multiple_of((1 - core) * (own.shape[1] - wide), wide)
    pairs = [
        (ref.at[:, pl.ds(start, wide)], out.at[:, pl.ds(at * wide, wide)])
        for at, ref in enumerate((own, mate))
    ]
    for copy in fetched(pairs, sems):
        copy.wait()


def run_sides(own, mate, wide, after):
    return pl.pallas_call(
        sides_kernel,
        in_specs=[ANY] * 3,
        out_specs=VMEM,
        out_shape=pltpu.VMEM((own.shape[0], 2 * wide), own.dtype),
        scratch_shapes=[pltpu.SemaphoreType.DMA((2,))],
        compiler_params=limit(1),
        cost_estimate=pl.CostEstimate(flops=0, bytes_accessed=400_000, transcendentals=0),
        name="sides",
    )(in_hbm(own), mate, after)


def join_kernel(*refs):
    parts, (after, out, sems) = refs[:-3], refs[-3:]
    del after
    pairs = []
    column = 0
    for part in parts:
        width = part.shape[1]
        pairs.append((part, out.at[:, pl.ds(column, width)]))
        column += width
    for copy in fetched(pairs, sems):
        copy.wait()


def run_join(parts, after):
    rows = parts[0].shape[0]
    width = sum(part.shape[1] for part in parts)
    return pl.pallas_call(
        join_kernel,
        in_specs=[ANY] * (len(parts) + 1),
        out_specs=VMEM,
        out_shape=pltpu.VMEM((rows, width), parts[0].dtype),
        scratch_shapes=[pltpu.SemaphoreType.DMA((len(parts),))],
        compiler_params=limit(1),
        cost_estimate=pl.CostEstimate(flops=0, bytes_accessed=1_000_000, transcendentals=0),
        name="join",
    )(*parts, after)


def chosen(table_hbm, table, wanted, picked, sems):
    skel, _, nodes = table.shape
    lane = lax.broadcasted_iota(jnp.int32, (16, nodes), 1)
    select = (wanted == lane).astype(BF16)
    chunk = 8
    copies = fetched(
        [
            (table_hbm.at[pl.ds(at, chunk)], table.at[pl.ds(at, chunk)])
            for at in range(0, skel, chunk)
        ],
        sems,
    )

    def finish():
        dot = functools.partial(
            lax.dot_general, select, dimension_numbers=TURNED, preferred_element_type=F32
        )
        group = 4
        for k in range(0, skel, group):
            if k % chunk == 0:
                copies[k // chunk].wait()
            top, low = halves(table[k : k + group].reshape(group * skel, nodes))
            rows = dot(top) + dot(low)
            for at in range(group):
                picked[pl.ds(16 * (k + at), 16), :] = rows[:, at * skel : (at + 1) * skel]

    return finish


def node_rows(nodes):
    return lax.broadcasted_iota(jnp.int32, (16, nodes), 0)


def pick_kernel(depth, tree_hbm, after, out, tree, picked, sems):
    del after
    skel, _, nodes = tree.shape
    heap = lax.axis_size("leaf") + lax.axis_index("leaf")
    row = node_rows(nodes)
    wanted = (lax.shift_right_logical(heap, row >> 1) ^ (row & 1)) - 2
    chosen(tree_hbm, tree, wanted, picked, sems)()
    for bit in range(depth - 1):
        for side in range(2):
            out[bit, side * skel : (side + 1) * skel, :] = picked[
                pl.ds(2 * bit + side, skel, stride=16), :
            ]


def run_pick(depth, tree_tr, after):
    skel = tree_tr.shape[0]
    return pl.pallas_call(
        functools.partial(pick_kernel, depth),
        in_specs=[ANY] * 2,
        out_specs=VMEM,
        out_shape=pltpu.VMEM((depth - 1, 2 * skel, skel), F32),
        scratch_shapes=[
            pltpu.VMEM(tree_tr.shape, F32),
            pltpu.VMEM((16 * skel, skel), F32),
            pltpu.SemaphoreType.DMA((skel // 8,)),
        ],
        compiler_params=limit(6),
        cost_estimate=pl.CostEstimate(flops=200_000_000, bytes_accessed=2_000_000, transcendentals=0),
        name="pick",
    )(in_hbm(tree_tr), after)


def lift_kernel(bit, current, other, mats, *rest):
    out = rest[-1]
    out[...] = dot3(jnp.concatenate([current[...], other[...]], axis=1), mats[bit])


def run_lift(bit, current, other, mats, after):
    return pl.pallas_call(
        functools.partial(lift_kernel, bit),
        in_specs=[VMEM] * 3 + [ANY] * len(after),
        out_specs=VMEM,
        out_shape=pltpu.VMEM(current.shape, F32),
        compiler_params=limit(1),
        cost_estimate=pl.CostEstimate(flops=2_000_000, bytes_accessed=100_000, transcendentals=0),
        name="lift",
    )(current, other, mats, *after)


def prep_kernel(
    coeffs,
    second,
    first,
    after,
    leaf_tr_hbm,
    leaf_cp_hbm,
    inner_tr_hbm,
    inner_cp_hbm,
    local_ref,
    reach_ref,
    leaf_tr,
    leaf_cp,
    inner_tr,
    inner_cp,
    sems,
):
    del after
    copies = fetched(
        [
            (inner_cp_hbm, inner_cp),
            (inner_tr_hbm, inner_tr),
            (leaf_cp_hbm, leaf_cp),
            (leaf_tr_hbm, leaf_tr),
        ],
        sems,
    )

    def coupled(values, table):
        a = dot3(values[:, 64:], table[:64], TURNED)
        b = dot3(values[:, :64], table[64:], TURNED)
        return jnp.concatenate([a, b], axis=1)

    for copy in copies:
        copy.wait()
    tops = coupled(first[...], inner_cp[0])
    mids = []
    for side in range(2):
        own = coupled(second[:, side * 128 : (side + 1) * 128], inner_cp[1 + side])
        mids.append(own + dot3(tops[:, side * 64 : (side + 1) * 64], inner_tr[1 + side], TURNED))
    reach_top = inner_tr[0]
    for pair in range(4):
        side = pair // 2
        low = (pair % 2) * 64
        own = coupled(coeffs[:, pair * 128 : (pair + 1) * 128], leaf_cp[pair])
        own = own + dot3(mids[side][:, low : low + 64], leaf_tr[pair], TURNED)
        local_ref[:, pair * 128 : (pair + 1) * 128] = own
        if pair % 2 == 0:
            reach_mid = dot3(inner_tr[1 + side], reach_top[side * 64 : (side + 1) * 64])
        reach_ref[pair * 128 : (pair + 1) * 128, :] = dot3(leaf_tr[pair], reach_mid[low : low + 64])


def run_prep(coeffs, second, first, leaf_tr, leaf_cp, inner_tr, inner_cp, after):
    rows = coeffs.shape[0]
    skel = first.shape[1] // 2
    tables = (leaf_tr, leaf_cp, inner_tr, inner_cp)
    return pl.pallas_call(
        prep_kernel,
        in_specs=[VMEM] * 3 + [ANY] * 5,
        out_specs=[VMEM] * 2,
        out_shape=[pltpu.VMEM((rows, 8 * skel), F32), pltpu.VMEM((8 * skel, skel), F32)],
        scratch_shapes=[pltpu.VMEM(x.shape, F32) for x in tables] + [pltpu.SemaphoreType.DMA((4,))],
        compiler_params=limit(4),
        cost_estimate=pl.CostEstimate(flops=200_000_000, bytes_accessed=1_000_000, transcendentals=0),
        name="prep",
    )(coeffs, second, first, after, *map(in_hbm, tables))


def turn_kernel(depth, mats, after, tree_hbm, out, tree, picked, sems):
    del after
    skel, _, nodes = tree.shape
    heap = lax.axis_size("leaf") + lax.axis_index("leaf")
    wanted = lax.shift_right_logical(heap, node_rows(nodes)) - 2
    finish = chosen(tree_hbm, tree, wanted, picked, sems)
    chains = [mats[0, :skel]]
    for bit in range(1, depth - 1):
        chains.append(dot3(chains[-1], mats[bit, :skel]))
    finish()
    for bit in range(depth):
        couple = picked[pl.ds(bit, skel, stride=16), :]
        out[bit] = dot3(chains[bit - 1], couple) if bit else couple


def run_turn(depth, mats, tree_cp, after):
    skel = tree_cp.shape[0]
    return pl.pallas_call(
        functools.partial(turn_kernel, depth),
        in_specs=[VMEM] + [ANY] * 2,
        out_specs=VMEM,
        out_shape=pltpu.VMEM((depth, skel, skel), F32),
        scratch_shapes=[
            pltpu.VMEM(tree_cp.shape, F32),
            pltpu.VMEM((16 * skel, skel), F32),
            pltpu.SemaphoreType.DMA((skel // 8,)),
        ],
        compiler_params=limit(6),
        cost_estimate=pl.CostEstimate(flops=200_000_000, bytes_accessed=2_000_000, transcendentals=0),
        name="turn",
    )(mats, after, in_hbm(tree_cp))


def near_kernel(index, own, mate, far, edge, edge_far, relay, diag, near, after, *rest):
    del after
    kept, beside, across, grid = rest
    rows, width = own.shape
    count, part, size = diag.shape
    wide = 2 * size
    core = lax.rem(lax.axis_index("rhs"), 2)
    here = pl.multiple_of(core * (width + wide), wide)
    there = pl.multiple_of((1 - core) * (width + wide), wide)

    def place(source, start, length, group, column):
        target = (pl.ds(group * rows, rows), pl.ds(column, length))
        grid[target] = source[:, start : start + length]

    place(own, 0, width, 0, wide)
    place(mate, 0, width, 1, wide)
    place(far, 0, width, 2, wide)
    place(relay, 0, width, 3, wide)
    place(edge, 0, wide, 0, here)
    place(edge, wide, wide, 1, here)
    place(edge_far, 0, wide, 2, here)
    place(edge_far, wide, wide, 3, here)
    place(relay, width, wide, 1, there)
    place(relay, width + wide, wide, 0, there)
    place(relay, width + 2 * wide, wide, 3, there)
    place(relay, width + 3 * wide, wide, 2, there)
    base = lax.axis_index("leaf") * count - 2
    dot = functools.partial(
        lax.dot_general, dimension_numbers=TURNED, preferred_element_type=F32
    )
    for leaf in range(count):
        total = dot(grid[:, (leaf + 2) * size : (leaf + 3) * size], diag[leaf])
        for j in range(near.shape[1]):
            column = pl.multiple_of((index[j, leaf] - base) * size, size)
            total = total + dot(grid[:, pl.ds(column, size)], near[leaf, j])
        here = slice(leaf * part, (leaf + 1) * part)
        kept[:, here] = total[:rows]
        beside[:, here] = total[rows : 2 * rows].astype(BF16)
        across[:, here] = total[2 * rows : 3 * rows].astype(BF16)
        here = slice((count + leaf) * part, (count + leaf + 1) * part)
        across[:, here] = total[3 * rows :].astype(BF16)


def run_near(index, own, mate, far, edge, edge_far, relay, diag, near, after):
    rows, width = own.shape
    count, part, size = diag.shape
    return pl.pallas_call(
        near_kernel,
        in_specs=[pl.BlockSpec(memory_space=pltpu.SMEM)] + [VMEM] * 8 + [ANY],
        out_specs=[VMEM] * 3,
        out_shape=[
            pltpu.VMEM((rows, count * part), F32),
            pltpu.VMEM((rows, count * part), BF16),
            pltpu.VMEM((rows, 2 * count * part), BF16),
        ],
        scratch_shapes=[pltpu.VMEM((4 * rows, width + 4 * size), BF16)],
        compiler_params=limit(12),
        cost_estimate=pl.CostEstimate(flops=800_000_000, bytes_accessed=6_000_000, transcendentals=0),
        name="near",
    )(index, own, mate, far, edge, edge_far, relay, diag, near, after)


def last_kernel(*refs):
    others, (turn, reach, local, basis, kept, across, beside, out) = refs[:-8], refs[-8:]
    rows = local.shape[0]
    skel = turn.shape[1]
    count = local.shape[1] // skel
    size = basis.shape[1] // count
    part = kept.shape[1] // count
    half = count * part
    total = None
    for bit, other in enumerate(others):
        term = dot3(other[...], turn[bit], TURNED)
        total = term if total is None else total + term
    leaf = (local[...] + dot3(total, reach[...], TURNED)).astype(BF16)
    place = lax.axis_index("rhs")
    for at in range(count):
        span = slice(at * size, (at + 1) * size)
        out[:, span] = lax.dot_general(
            leaf[:, at * skel : (at + 1) * skel], basis[:, span], PLAIN, preferred_element_type=F32
        )
        for group, (close, start) in enumerate(((kept, 0), (beside, 0), (across, 0), (beside, half))):
            column = pl.multiple_of(at * size + (place ^ group) * part, part)
            here = pl.ds(column, part)
            start += at * part
            out[:, here] = out[:, here] + close[:, start : start + part].astype(F32)


def run_last(others, turn, reach, local, basis, kept, across, beside):
    rows = local.shape[0]
    return pl.pallas_call(
        last_kernel,
        in_specs=[VMEM] * (len(others) + 7),
        out_specs=VMEM,
        out_shape=jax.ShapeDtypeStruct((rows, basis.shape[1]), F32),
        compiler_params=limit(6),
        cost_estimate=pl.CostEstimate(flops=200_000_000, bytes_accessed=2_000_000, transcendentals=0),
        name="last",
    )(*others, turn, reach, local, basis, kept, across, beside)


def local(
    rhs_block,
    col_basis,
    row_basis,
    leaf_transfer,
    leaf_coupling,
    inner_transfer,
    inner_coupling,
    tree_transfer,
    tree_coupling,
    diag_blocks,
    near_blocks,
    near_leaves,
):
    width = rhs_block.shape[1]
    count = leaf_transfer.shape[0]
    wide = 2 * (width // count)
    skel = col_basis.shape[0]
    span = lax.axis_size("leaf")
    ranks = lax.axis_size("rhs")
    depth = span.bit_length() - 1
    leaf_tr = leaf_transfer.reshape(count // 2, 2 * skel, skel)
    leaf_cp = leaf_coupling.reshape(count // 2, 2 * skel, skel)
    inner_tr = inner_transfer.reshape(count // 2 - 1, 2 * skel, skel)
    inner_cp = inner_coupling.reshape(count // 2 - 1, 2 * skel, skel)

    mate = swapped(rhs_block, "rhs", 1)
    far = swapped(rhs_block, "rhs", 2)

    coeffs, second, first, block = run_up(rhs_block, col_basis, leaf_tr, inner_tr)
    mats = run_pick(depth, jnp.transpose(tree_transfer, (1, 2, 0)), block)
    sides = run_sides(rhs_block, mate, wide, block)
    same, across = [], []
    for i in range(span):
        for q in range(ranks):
            to = i + 1 if q % 2 == 0 else i - 1
            if 0 <= to < span:
                same.append((i * ranks + q, to * ranks + q))
                across.append((i * ranks + q, to * ranks + (q ^ 2)))
    edge = lax.ppermute(sides, ("leaf", "rhs"), same)
    edge_far = lax.ppermute(sides, ("leaf", "rhs"), across)

    others = []

    def step(current, beside):
        bit = len(others)
        others.append(swapped(current, "leaf", 1 << bit))
        return run_lift(bit, current, others[-1], mats, beside)

    current = step(block, [sides])
    local_part, reach = run_prep(
        coeffs, second, first, leaf_tr, leaf_cp, inner_tr, inner_cp, current
    )
    current = step(current, [reach])
    joined = run_join([far, edge, edge_far], current)
    relay = swapped(joined, "rhs", 1)
    current = step(current, [joined])
    kept, beside, passed = run_near(
        near_leaves.T, rhs_block, mate, far, edge, edge_far, relay, diag_blocks, near_blocks, current
    )
    passed = swapped(passed, "rhs", 2)
    current = step(current, [kept])
    turn = run_turn(depth, mats, jnp.transpose(tree_coupling, (1, 2, 0)), current)
    half = passed.shape[1] // 2
    joined = run_join([beside, passed[:, half:]], current)
    beside = swapped(joined, "rhs", 1)
    current = step(current, [turn, joined])
    others.append(swapped(current, "leaf", 1 << len(others)))
    return run_last(others, turn, reach, local_part, row_basis, kept, passed, beside)


def solution(mesh):
    in_specs = (
        P("rhs", "leaf"),
        P(None, "leaf"),
        P(None, "leaf"),
        P("leaf", None, None),
        P("leaf", None, None),
        P("leaf", None, None, None),
        P("leaf", None, None, None),
        P(),
        P(),
        P("leaf", "rhs", None),
        P("leaf", None, "rhs", None),
        P("leaf", None),
    )
    out_specs = P("rhs", "leaf")
    return jax.shard_map(local, mesh=mesh, in_specs=in_specs, out_specs=out_specs, check_vma=False)
```

time: 182 us -> 55.3 us (0.30)
  the two profiles are of different devices: /device:TPU:1 before, /device:TPU:2 now
where the time goes in v1:
time: 55.3 us; the launch traced here: 55.1 us
  starting transfers between devices  23.9 us (43%)
  Pallas kernels  16.7 us (30%)
  waiting for transfers between devices  14.2 us (26%)
    ppermute x11, starting transfers between devices, swapped(): return lax.ppermute(x, axis, [(i, i ^ bit) for i in range(count)])  16.1 us
    ppermute x11, waiting for transfers between devices, swapped(): return lax.ppermute(x, axis, [(i, i ^ bit) for i in range(count)])  14.2 us
    ppermute x1, starting transfers between devices, local(): edge_far = lax.ppermute(sides, ('leaf', 'rhs'), across)  4.33 us
    ppermute x1, starting transfers between devices, local(): edge = lax.ppermute(sides, ('leaf', 'rhs'), same)  3.49 us
    pallas_call x1, Pallas kernels, run_turn(): pl.pallas_call(functools.partial(turn_kernel, depth), in_specs=[VMEM] + [...  3.34 us
    pallas_call x1, Pallas kernels, run_pick(): pl.pallas_call(functools.partial(pick_kernel, depth), in_specs=[ANY] * 2,...  3.22 us
    pallas_call x1, Pallas kernels, run_prep(): pl.pallas_call(prep_kernel, in_specs=[VMEM] * 3 + [ANY] * 5, out_specs=[V...  2.41 us
    pallas_call x1, Pallas kernels, run_up(): pl.pallas_call(up_kernel, in_specs=[ANY] * 4, out_specs=[VMEM] * 4, out_s...  2.2 us
  transfers between devices with their start and end apart: 13, of which 4 were waited for; matrix products, arithmetic and copies ran while one was open for 0% of the time, Pallas kernels for 24%

profile of v1, /device:TPU:2, one launch (start us, length us, event | category | flops | bytes accessed | tf_op | source)
XLA Modules:
  0.0 55.1 jit_solution(9202428121892493333)
XLA Ops:
  0.0 2.1 %collective-permute-start.4 = (bf16[32,4096]{1,0:T(8,128)(2,1)}, bf16[32,4096]{1,0:T(8,128)(2,1)S(1)}, u32[]{:S(2)}, u32[]{:S(2)}) collective-permute-start(bf16[32,4096]{1,0:T(8,128)(2,1)} %own.3), channel_id=1, source_target_pairs={{0,2},{1,3},{2,0},{3,1},{4,6},{5,7},{6,4},{7,5},{8,10},{9,11},{10,... | collective-permute-start | bytes 786440 | tf_op jit(solution)/shard_map/ppermute | solution.py:33
  2.1 2.2 %up.1 = (f32[32,512]{1,0:T(8,128)S(1)}, f32[32,256]{1,0:T(8,128)S(1)}, f32[32,128]{1,0:T(8,128)S(1)}, f32[32,64]{1,0:T(8,128)S(1)}) custom-call(bf16[32,4096]{1,0:T(8,128)(2,1)} %own.3, bf16[64,4096]{1,0:T(8,128)(2,1)} %cols_hbm.1, f32[4,128,64]{2,1,0:T(8,128)} %bitcast.10, f32[3,128,64]{2,1,0:T(8,128)} %bitcast.12), custom_call_target="tpu_custom_call" | custom-call | flops 200000000 | bytes 2000000 | tf_op jit(solution)/shard_map/up/pallas_call | solution.py:92
  4.4 0.9 %sides.1.rest_0_ = bf16[32,2048]{1,0:T(8,128)(2,1)S(1)} custom-call(bf16[32,4096]{1,0:T(8,128)(2,1)} %own.3, bf16[32,4096]{1,0:T(8,128)(2,1)S(1)} %collective-permute-done.1.mate, f32[32,64]{1,0:T(8,128)S(1)} %get-tuple-element.14.after.current), custom_call_target="tpu_custom_call" | custom-call | bytes 400000 | tf_op jit(solution)/shard_map/sides/pallas_call | solution.py:124
  5.2 3.5 %collective-permute-start.5 = (bf16[32,2048]{1,0:T(8,128)(2,1)S(1)}, bf16[32,2048]{1,0:T(8,128)(2,1)S(1)}, u32[]{:S(2)}, u32[]{:S(2)}) collective-permute-start(bf16[32,2048]{1,0:T(8,128)(2,1)S(1)} %sides.1.rest_0_), channel_id=1, source_target_pairs={{0,4},{2,6},{4,8},{5,1},{6,10},{7,3},{8,12},{9,5},{10,14},{11,7},{... | collective-permute-start | bytes 393224 | tf_op jit(solution)/shard_map/ppermute | solution.py:487
  8.7 4.3 %collective-permute-start.6 = (bf16[32,2048]{1,0:T(8,128)(2,1)S(1)}, bf16[32,2048]{1,0:T(8,128)(2,1)S(1)}, u32[]{:S(2)}, u32[]{:S(2)}) collective-permute-start(bf16[32,2048]{1,0:T(8,128)(2,1)S(1)} %sides.1.rest_0_), channel_id=1, source_target_pairs={{0,6},{2,4},{4,10},{5,3},{6,8},{7,1},{8,14},{9,7},{10,12},{11,5},{... | collective-permute-start | bytes 393224 | tf_op jit(solution)/shard_map/ppermute | solution.py:488
  13.1 1.4 %collective-permute-start = (f32[32,64]{1,0:T(8,128)S(1)}, f32[32,64]{1,0:T(8,128)S(1)}, u32[]{:S(2)}, u32[]{:S(2)}) collective-permute-start(f32[32,64]{1,0:T(8,128)S(1)} %get-tuple-element.14.after.current), channel_id=1, source_target_pairs={{0,4},{4,0},{8,12},{12,8},{16,20},{20,16},{24,28},{28,24},{32,36},... | collective-permute-start | bytes 24584 | tf_op jit(solution)/shard_map/ppermute | solution.py:33
  14.4 3.2 %pick.1.mats = f32[5,128,64]{2,1,0:T(8,128)S(1)} custom-call(f32[64,64,126]{2,1,0:T(8,128)} %bitcast.9, f32[32,64]{1,0:T(8,128)S(1)} %get-tuple-element.14.after.current), custom_call_target="tpu_custom_call" | custom-call | flops 200000000 | bytes 2000000 | tf_op jit(solution)/shard_map/pick/pallas_call | solution.py:213
  17.7 0.2 lift.5.after.current
  17.9 3.2 %collective-permute-start.2 = (f32[32,64]{1,0:T(8,128)S(1)}, f32[32,64]{1,0:T(8,128)S(1)}, u32[]{:S(2)}, u32[]{:S(2)}) collective-permute-start(f32[32,64]{1,0:T(8,128)S(1)} %lift.5.after.current), channel_id=1, source_target_pairs={{0,8},{4,12},{8,0},{12,4},{16,24},{20,28},{24,16},{28,20},{32,40},... | collective-permute-start | bytes 24584 | tf_op jit(solution)/shard_map/ppermute | solution.py:33
  21.1 2.4 %prep.1 = (f32[32,512]{1,0:T(8,128)S(1)}, f32[512,64]{1,0:T(8,128)S(1)}) custom-call(f32[32,512]{1,0:T(8,128)S(1)} %get-tuple-element.15.coeffs, f32[32,256]{1,0:T(8,128)S(1)} %get-tuple-element.16.second, f32[32,128]{1,0:T(8,128)S(1)} %get-tuple-element.17.first, f32[32,64]{1,0:T(8,128)S(1)} %lift.5.after.current, f32[4,128,64]{2,1,0:T(8,128)} %bitcast.11, ...), custom_call_target="tpu_custom_call" | custom-call | flops 200000000 | bytes 1000000 | tf_op jit(solution)/shard_map/prep/pallas_call | solution.py:302
  23.5 0.2 lift.6.refs_3_.current
  23.9 3.2 %collective-permute-start.8 = (bf16[32,8192]{1,0:T(8,128)(2,1)S(1)}, bf16[32,8192]{1,0:T(8,128)(2,1)S(1)}, u32[]{:S(2)}, u32[]{:S(2)}) collective-permute-start(bf16[32,8192]{1,0:T(8,128)(2,1)S(1)} %join.2.rest_0_), channel_id=1, source_target_pairs={{0,1},{1,0},{2,3},{3,2},{4,5},{5,4},{6,7},{7,6},{8,9},{9,8},{10,11... | collective-permute-start | bytes 1572872 | tf_op jit(solution)/shard_map/ppermute | solution.py:33
  27.1 3.7 %collective-permute-done.3.other.refs_2_ = f32[32,64]{1,0:T(8,128)S(1)} collective-permute-done((f32[32,64]{1,0:T(8,128)S(1)}, f32[32,64]{1,0:T(8,128)S(1)}, u32[]{:S(2)}, u32[]{:S(2)}) %collective-permute-start.3) | collective-permute-done | bytes 8224 | tf_op jit(solution)/shard_map/ppermute | solution.py:33
  30.9 0.2 lift.7.after.current
  31.1 1.7 %near.2 = (f32[32,1024]{1,0:T(8,128)S(1)}, bf16[32,1024]{1,0:T(8,128)(2,1)S(1)}, bf16[32,2048]{1,0:T(8,128)(2,1)S(1)}) custom-call(s32[2,8]{1,0:T(2,128)S(1)} %bitcast.7, bf16[32,4096]{1,0:T(8,128)(2,1)S(1)} %copy-done, bf16[32,4096]{1,0:T(8,128)(2,1)S(1)} %collective-permute-done.1.mate, bf16[32,4096]{1,0:T(8,128)(2,1)S(1)} %collective-permute-done.4.refs_0_.far, ...), custom_call_target="tpu_custom_call" | custom-call | flops 800000000 | bytes 6000000 | tf_op jit(solution)/shard_map/near/pallas_call | solution.py:393
  32.8 3.7 %collective-permute-start.10 = (bf16[32,2048]{1,0:T(8,128)(2,1)S(1)}, bf16[32,2048]{1,0:T(8,128)(2,1)S(1)}, u32[]{:S(2)}, u32[]{:S(2)}) collective-permute-start(bf16[32,2048]{1,0:T(8,128)(2,1)S(1)} %get-tuple-element.21), channel_id=1, source_target_pairs={{0,2},{1,3},{2,0},{3,1},{4,6},{5,7},{6,4},{7,5},{8,10},{9,11},{10,... | collective-permute-start | bytes 393224 | tf_op jit(solution)/shard_map/ppermute | solution.py:33
  36.5 4.6 %collective-permute-done.7.other.refs_3_ = f32[32,64]{1,0:T(8,128)S(1)} collective-permute-done((f32[32,64]{1,0:T(8,128)S(1)}, f32[32,64]{1,0:T(8,128)S(1)}, u32[]{:S(2)}, u32[]{:S(2)}) %collective-permute-start.7) | collective-permute-done | bytes 8224 | tf_op jit(solution)/shard_map/ppermute | solution.py:33
  41.1 0.2 lift.8.after.refs_2_.current
  41.5 2.4 %collective-permute-start.9 = (f32[32,64]{1,0:T(8,128)S(1)}, f32[32,64]{1,0:T(8,128)S(1)}, u32[]{:S(2)}, u32[]{:S(2)}) collective-permute-start(f32[32,64]{1,0:T(8,128)S(1)} %lift.8.after.refs_2_.current), channel_id=1, source_target_pairs={{0,64},{4,68},{8,72},{12,76},{16,80},{20,84},{24,88},{28,92},{32,9... | collective-permute-start | bytes 24584 | tf_op jit(solution)/shard_map/ppermute | solution.py:33
  43.9 3.3 %turn.1.rest_0_.refs_6_ = f32[6,64,64]{2,1,0:T(8,128)S(1)} custom-call(f32[5,128,64]{2,1,0:T(8,128)S(1)} %pick.1.mats, f32[32,64]{1,0:T(8,128)S(1)} %lift.8.after.refs_2_.current, f32[64,64,126]{2,1,0:T(8,128)} %bitcast.8), custom_call_target="tpu_custom_call" | custom-call | flops 200000000 | bytes 2000000 | tf_op jit(solution)/shard_map/turn/pallas_call | solution.py:331
  47.3 2.0 %collective-permute-done.9.other.refs_4_ = f32[32,64]{1,0:T(8,128)S(1)} collective-permute-done((f32[32,64]{1,0:T(8,128)S(1)}, f32[32,64]{1,0:T(8,128)S(1)}, u32[]{:S(2)}, u32[]{:S(2)}) %collective-permute-start.9) | collective-permute-done | bytes 8224 | tf_op jit(solution)/shard_map/ppermute | solution.py:33
  49.3 0.2 lift.9
  49.5 3.7 %collective-permute-done.11.refs_5_ = f32[32,64]{1,0:T(8,128)S(1)} collective-permute-done((f32[32,64]{1,0:T(8,128)S(1)}, f32[32,64]{1,0:T(8,128)S(1)}, u32[]{:S(2)}, u32[]{:S(2)}) %collective-permute-start.11) | collective-permute-done | bytes 8224 | tf_op jit(solution)/shard_map/ppermute | solution.py:33
  53.2 1.8 %last.1 = f32[32,4096]{1,0:T(8,128)} custom-call(f32[32,64]{1,0:T(8,128)S(1)} %collective-permute-done.other.refs_0_, f32[32,64]{1,0:T(8,128)S(1)} %collective-permute-done.2.other.refs_1_, f32[32,64]{1,0:T(8,128)S(1)} %collective-permute-done.3.other.refs_2_, f32[32,64]{1,0:T(8,128)S(1)} %collective-permute-done.7.other.refs_3_, ...), custom_call_target="tpu_custom_call" | custom-call | flops 200000000 | bytes 2000000 | tf_op jit(solution)/shard_map/last/pallas_call | solution.py:437
  (27 shorter events, 0.4 us)
Async XLA Ops:
  0.0 4.3 %collective-permute-start.1 = (bf16[32,4096]{1,0:T(8,128)(2,1)}, bf16[32,4096]{1,0:T(8,128)(2,1)S(1)}, u32[]{:S(2)}, u32[]{:S(2)}) collective-permute-start(bf16[32,4096]{1,0:T(8,128)(2,1)} %own.3), channel_id=1, source_target_pairs={{0,1},{1,0},{2,3},{3,2},{4,5},{5,4},{6,7},{7,6},{8,9},{9,8},{10,11... | collective-permute-start | bytes 786440 | tf_op jit(solution)/shard_map/ppermute | solution.py:33
  0.0 23.7 %collective-permute-start.4 = (bf16[32,4096]{1,0:T(8,128)(2,1)}, bf16[32,4096]{1,0:T(8,128)(2,1)S(1)}, u32[]{:S(2)}, u32[]{:S(2)}) collective-permute-start(bf16[32,4096]{1,0:T(8,128)(2,1)} %own.3), channel_id=1, source_target_pairs={{0,2},{1,3},{2,0},{3,1},{4,6},{5,7},{6,4},{7,5},{8,10},{9,11},{10,... | collective-permute-start | bytes 786440 | tf_op jit(solution)/shard_map/ppermute | solution.py:33
  5.2 18.5 %collective-permute-start.5 = (bf16[32,2048]{1,0:T(8,128)(2,1)S(1)}, bf16[32,2048]{1,0:T(8,128)(2,1)S(1)}, u32[]{:S(2)}, u32[]{:S(2)}) collective-permute-start(bf16[32,2048]{1,0:T(8,128)(2,1)S(1)} %sides.1.rest_0_), channel_id=1, source_target_pairs={{0,4},{2,6},{4,8},{5,1},{6,10},{7,3},{8,12},{9,5},{10,14},{11,7},{... | collective-permute-start | bytes 393224 | tf_op jit(solution)/shard_map/ppermute | solution.py:487
  8.7 15.0 %collective-permute-start.6 = (bf16[32,2048]{1,0:T(8,128)(2,1)S(1)}, bf16[32,2048]{1,0:T(8,128)(2,1)S(1)}, u32[]{:S(2)}, u32[]{:S(2)}) collective-permute-start(bf16[32,2048]{1,0:T(8,128)(2,1)S(1)} %sides.1.rest_0_), channel_id=1, source_target_pairs={{0,6},{2,4},{4,10},{5,3},{6,8},{7,1},{8,14},{9,7},{10,12},{11,5},{... | collective-permute-start | bytes 393224 | tf_op jit(solution)/shard_map/ppermute | solution.py:488
  13.1 4.6 %collective-permute-start = (f32[32,64]{1,0:T(8,128)S(1)}, f32[32,64]{1,0:T(8,128)S(1)}, u32[]{:S(2)}, u32[]{:S(2)}) collective-permute-start(f32[32,64]{1,0:T(8,128)S(1)} %get-tuple-element.14.after.current), channel_id=1, source_target_pairs={{0,4},{4,0},{8,12},{12,8},{16,20},{20,16},{24,28},{28,24},{32,36},... | collective-permute-start | bytes 24584 | tf_op jit(solution)/shard_map/ppermute | solution.py:33
  17.7 13.4 %copy-start = (bf16[32,4096]{1,0:T(8,128)(2,1)S(1)}, bf16[32,4096]{1,0:T(8,128)(2,1)}, u32[]{:S(2)}) copy-start(bf16[32,4096]{1,0:T(8,128)(2,1)} %own.3) | copy-start | bytes 786436
  17.7 13.4 %copy-start.1 = (bf16[8,2,128,512]{3,2,1,0:T(8,128)(2,1)S(1)}, bf16[8,2,128,512]{3,2,1,0:T(8,128)(2,1)}, u32[]{:S(2)}) copy-start(bf16[8,2,128,512]{3,2,1,0:T(8,128)(2,1)} %near.3) | copy-start | bytes 6291460
  17.7 13.4 %copy-start.2 = (bf16[8,128,512]{2,1,0:T(8,128)(2,1)S(1)}, bf16[8,128,512]{2,1,0:T(8,128)(2,1)}, u32[]{:S(2)}) copy-start(bf16[8,128,512]{2,1,0:T(8,128)(2,1)} %diag.1) | copy-start | bytes 3145732
  17.7 13.4 %copy-start.4 = (s32[8,2]{0,1:T(2,128)S(1)}, s32[8,2]{0,1:T(2,128)}, u32[]{:S(2)}) copy-start(s32[8,2]{0,1:T(2,128)} %param.23) | copy-start | bytes 196
  17.9 5.6 %collective-permute-start.2 = (f32[32,64]{1,0:T(8,128)S(1)}, f32[32,64]{1,0:T(8,128)S(1)}, u32[]{:S(2)}, u32[]{:S(2)}) collective-permute-start(f32[32,64]{1,0:T(8,128)S(1)} %lift.5.after.current), channel_id=1, source_target_pairs={{0,8},{4,12},{8,0},{12,4},{16,24},{20,28},{24,16},{28,20},{32,40},... | collective-permute-start | bytes 24584 | tf_op jit(solution)/shard_map/ppermute | solution.py:33
  23.9 7.1 %collective-permute-start.8 = (bf16[32,8192]{1,0:T(8,128)(2,1)S(1)}, bf16[32,8192]{1,0:T(8,128)(2,1)S(1)}, u32[]{:S(2)}, u32[]{:S(2)}) collective-permute-start(bf16[32,8192]{1,0:T(8,128)(2,1)S(1)} %join.2.rest_0_), channel_id=1, source_target_pairs={{0,1},{1,0},{2,3},{3,2},{4,5},{5,4},{6,7},{7,6},{8,9},{9,8},{10,11... | collective-permute-start | bytes 1572872 | tf_op jit(solution)/shard_map/ppermute | solution.py:33
  27.1 3.7 %collective-permute-start.3 = (f32[32,64]{1,0:T(8,128)S(1)}, f32[32,64]{1,0:T(8,128)S(1)}, u32[]{:S(2)}, u32[]{:S(2)}) collective-permute-start(f32[32,64]{1,0:T(8,128)S(1)} %lift.6.refs_3_.current), channel_id=1, source_target_pairs={{0,16},{4,20},{8,24},{12,28},{16,0},{20,4},{24,8},{28,12},{32,48},... | collective-permute-start | bytes 24584 | tf_op jit(solution)/shard_map/ppermute | solution.py:33
  32.8 8.5 %collective-permute-start.10 = (bf16[32,2048]{1,0:T(8,128)(2,1)S(1)}, bf16[32,2048]{1,0:T(8,128)(2,1)S(1)}, u32[]{:S(2)}, u32[]{:S(2)}) collective-permute-start(bf16[32,2048]{1,0:T(8,128)(2,1)S(1)} %get-tuple-element.21), channel_id=1, source_target_pairs={{0,2},{1,3},{2,0},{3,1},{4,6},{5,7},{6,4},{7,5},{8,10},{9,11},{10,... | collective-permute-start | bytes 393224 | tf_op jit(solution)/shard_map/ppermute | solution.py:33
  36.5 4.6 %collective-permute-start.7 = (f32[32,64]{1,0:T(8,128)S(1)}, f32[32,64]{1,0:T(8,128)S(1)}, u32[]{:S(2)}, u32[]{:S(2)}) collective-permute-start(f32[32,64]{1,0:T(8,128)S(1)} %lift.7.after.current), channel_id=1, source_target_pairs={{0,32},{4,36},{8,40},{12,44},{16,48},{20,52},{24,56},{28,60},{32,0... | collective-permute-start | bytes 24584 | tf_op jit(solution)/shard_map/ppermute | solution.py:33
  41.1 12.1 %copy-start.3 = (bf16[64,4096]{1,0:T(8,128)(2,1)S(1)}, bf16[64,4096]{1,0:T(8,128)(2,1)}, u32[]{:S(2)}) copy-start(bf16[64,4096]{1,0:T(8,128)(2,1)} %refs_9_.1) | copy-start | bytes 1572868
  41.4 11.8 %collective-permute-start.12 = (bf16[32,2048]{1,0:T(8,128)(2,1)S(1)}, bf16[32,2048]{1,0:T(8,128)(2,1)S(1)}, u32[]{:S(2)}, u32[]{:S(2)}) collective-permute-start(bf16[32,2048]{1,0:T(8,128)(2,1)S(1)} %join.3.rest_1_), channel_id=1, source_target_pairs={{0,1},{1,0},{2,3},{3,2},{4,5},{5,4},{6,7},{7,6},{8,9},{9,8},{10,11... | collective-permute-start | bytes 393224 | tf_op jit(solution)/shard_map/ppermute | solution.py:33
  41.5 7.7 %collective-permute-start.9 = (f32[32,64]{1,0:T(8,128)S(1)}, f32[32,64]{1,0:T(8,128)S(1)}, u32[]{:S(2)}, u32[]{:S(2)}) collective-permute-start(f32[32,64]{1,0:T(8,128)S(1)} %lift.8.after.refs_2_.current), channel_id=1, source_target_pairs={{0,64},{4,68},{8,72},{12,76},{16,80},{20,84},{24,88},{28,92},{32,9... | collective-permute-start | bytes 24584 | tf_op jit(solution)/shard_map/ppermute | solution.py:33
  49.4 3.8 %collective-permute-start.11 = (f32[32,64]{1,0:T(8,128)S(1)}, f32[32,64]{1,0:T(8,128)S(1)}, u32[]{:S(2)}, u32[]{:S(2)}) collective-permute-start(f32[32,64]{1,0:T(8,128)S(1)} %lift.9), channel_id=1, source_target_pairs={{0,128},{4,132},{8,136},{12,140},{16,144},{20,148},{24,152},{28,15... | collective-permute-start | bytes 24584 | tf_op jit(solution)/shard_map/ppermute | solution.py:33

commit v2 on v1

v2 whole, which is shorter than its diff:
```python
import functools

import jax
import jax.numpy as jnp
from jax import lax
from jax.experimental import pallas as pl
from jax.experimental.pallas import tpu as pltpu
from jax.sharding import PartitionSpec as P

HIGH = lax.Precision.HIGHEST
F32 = jnp.float32
BF16 = jnp.bfloat16
VMEM = pl.BlockSpec(memory_space=pltpu.VMEM)
ANY = pl.BlockSpec(memory_space=pl.ANY)
LIGHT = pl.CostEstimate(flops=0, bytes_accessed=0, transcendentals=0)
HEAVY = pl.CostEstimate(flops=20_000_000_000, bytes_accessed=60_000_000, transcendentals=0)
MIDDLE = pl.CostEstimate(flops=0, bytes_accessed=11_000_000, transcendentals=0)
PLAIN = (((1,), (0,)), ((), ()))
TURNED = (((1,), (1,)), ((), ()))


def halves(x):
    top = x.astype(BF16)
    return top, (x - top.astype(F32)).astype(BF16)


def dot3(a, b, dims=PLAIN):
    ah, al = halves(a)
    bh, bl = halves(b)
    dot = functools.partial(lax.dot_general, dimension_numbers=dims, preferred_element_type=F32)
    return dot(ah, bh) + (dot(ah, bl) + dot(al, bh))


def swapped(x, axis, bit):
    count = lax.axis_size(axis)
    return lax.ppermute(x, axis, [(i, i ^ bit) for i in range(count)])


def limit(mib):
    return pltpu.CompilerParams(vmem_limit_bytes=mib << 20)


def in_hbm(x):
    return pltpu.with_memory_space_constraint(x, pltpu.HBM)


def fetched(pairs, sems):
    copies = []
    for at, (source, target) in enumerate(pairs):
        copy = pltpu.make_async_copy(source, target, sems.at[at])
        copy.start()
        copies.append(copy)
    return copies


def up_kernel(
    rhs_hbm,
    cols_hbm,
    leaf_hbm,
    inner_hbm,
    tree_hbm,
    rhs,
    tree,
    coeffs,
    second,
    first,
    block,
    packet,
    outward,
    cols,
    leaf_tr,
    inner_tr,
    sems,
):
    half = rhs.shape[1] // 2
    size = rhs.shape[1] // 8
    wide = 2 * size
    pairs = []
    for side in range(2):
        span = pl.ds(side * half, half)
        pairs += [(rhs_hbm.at[:, span], rhs.at[:, span]), (cols_hbm.at[:, span], cols.at[:, span])]
    pairs += [(leaf_hbm, leaf_tr), (inner_hbm, inner_tr), (tree_hbm, tree)]
    copies = fetched(pairs, sems)
    parts = []
    for leaf in range(8):
        if leaf % 4 == 0:
            copies[leaf // 2].wait()
            copies[leaf // 2 + 1].wait()
        span = slice(leaf * size, (leaf + 1) * size)
        parts.append(
            lax.dot_general(rhs[:, span], cols[:, span], TURNED, preferred_element_type=F32)
        )
    copies[4].wait()
    copies[5].wait()
    ups = []
    for pair in range(4):
        both = jnp.concatenate(parts[2 * pair : 2 * pair + 2], axis=1)
        coeffs[:, pair * 128 : (pair + 1) * 128] = both
        ups.append(dot3(both, leaf_tr[pair]))
    left = jnp.concatenate(ups[:2], axis=1)
    right = jnp.concatenate(ups[2:], axis=1)
    second[:, :128] = left
    second[:, 128:] = right
    both = jnp.concatenate([dot3(left, inner_tr[1]), dot3(right, inner_tr[2])], axis=1)
    first[...] = both
    total = dot3(both, inner_tr[0])
    block[...] = total
    packet[:, :128] = jnp.concatenate(halves(total), axis=1)
    odd = lax.rem(lax.axis_index("leaf"), 2)
    inner_side = pl.multiple_of((1 - odd) * (rhs.shape[1] - wide), wide)
    outer_side = pl.multiple_of(odd * (rhs.shape[1] - wide), wide)
    packet[:, 128:] = rhs[:, pl.ds(inner_side, wide)]
    outward[...] = rhs[:, pl.ds(outer_side, wide)]
    copies[6].wait()


def run_up(rhs, cols, leaf_tr, inner_tr, tree_tr):
    rows, width = rhs.shape
    skel = cols.shape[0]
    wide = width // 4
    tables = (cols, leaf_tr, inner_tr)
    return pl.pallas_call(
        up_kernel,
        in_specs=[ANY] * 5,
        out_specs=[VMEM] * 8,
        out_shape=[
            pltpu.VMEM(rhs.shape, rhs.dtype),
            pltpu.VMEM(tree_tr.shape, F32),
            pltpu.VMEM((rows, 8 * skel), F32),
            pltpu.VMEM((rows, 4 * skel), F32),
            pltpu.VMEM((rows, 2 * skel), F32),
            pltpu.VMEM((rows, skel), F32),
            pltpu.VMEM((rows, 2 * skel + wide), BF16),
            pltpu.VMEM((rows, wide), BF16),
        ],
        scratch_shapes=[pltpu.VMEM(x.shape, x.dtype) for x in tables]
        + [pltpu.SemaphoreType.DMA((7,))],
        compiler_params=limit(8),
        cost_estimate=LIGHT,
        name="up",
    )(*map(in_hbm, (rhs, cols, leaf_tr, inner_tr, tree_tr)))


def join_kernel(spans, *refs):
    refs, (out, sems) = refs[:-2], refs[-2:]
    pairs = []
    column = 0
    for part, (start, width) in zip(refs, spans):
        pairs.append((part.at[:, pl.ds(start, width)], out.at[:, pl.ds(column, width)]))
        column += width
    for copy in fetched(pairs, sems):
        copy.wait()


def run_join(parts, after=()):
    spans = [part[1:] for part in parts]
    arrays = [part[0] for part in parts]
    return pl.pallas_call(
        functools.partial(join_kernel, spans),
        in_specs=[ANY] * (len(parts) + len(after)),
        out_specs=VMEM,
        out_shape=pltpu.VMEM((arrays[0].shape[0], sum(w for _, w in spans)), arrays[0].dtype),
        scratch_shapes=[pltpu.SemaphoreType.DMA((len(parts),))],
        compiler_params=limit(1),
        cost_estimate=LIGHT,
        name="join",
    )(*arrays, *after)


def choose(table, wanted, picked):
    skel, _, nodes = table.shape
    select = (wanted == lax.broadcasted_iota(jnp.int32, (16, nodes), 1)).astype(BF16)
    dot = functools.partial(
        lax.dot_general, select, dimension_numbers=TURNED, preferred_element_type=F32
    )
    group = 4
    for k in range(0, skel, group):
        top, low = halves(table[k : k + group].reshape(group * skel, nodes))
        rows = dot(top) + dot(low)
        for at in range(group):
            picked[pl.ds(16 * (k + at), 16), :] = rows[:, at * skel : (at + 1) * skel]


def node_rows(nodes):
    return lax.broadcasted_iota(jnp.int32, (16, nodes), 0)


def pick_kernel(depth, tree, out, picked):
    skel, _, nodes = tree.shape
    heap = lax.axis_size("leaf") + lax.axis_index("leaf")
    row = node_rows(nodes)
    choose(tree, (lax.shift_right_logical(heap, row >> 1) ^ (row & 1)) - 2, picked)
    for bit in range(depth - 1):
        for side in range(2):
            out[bit, side * skel : (side + 1) * skel, :] = picked[
                pl.ds(2 * bit + side, skel, stride=16), :
            ]


def run_pick(depth, tree):
    skel = tree.shape[0]
    return pl.pallas_call(
        functools.partial(pick_kernel, depth),
        in_specs=[VMEM],
        out_specs=VMEM,
        out_shape=pltpu.VMEM((depth - 1, 2 * skel, skel), F32),
        scratch_shapes=[pltpu.VMEM((16 * skel, skel), F32)],
        compiler_params=limit(6),
        cost_estimate=LIGHT,
        name="pick",
    )(tree)


def first_lift_kernel(current, packet, mats, *rest):
    out, other = rest[-2:]
    skel = current.shape[1]
    sibling = packet[:, :skel].astype(F32) + packet[:, skel : 2 * skel].astype(F32)
    other[...] = sibling
    out[...] = dot3(jnp.concatenate([current[...], sibling], axis=1), mats[0])


def run_first_lift(current, packet, mats, after):
    return pl.pallas_call(
        first_lift_kernel,
        in_specs=[VMEM] * 3 + [ANY] * len(after),
        out_specs=[VMEM] * 2,
        out_shape=[pltpu.VMEM(current.shape, F32)] * 2,
        compiler_params=limit(1),
        cost_estimate=HEAVY,
        name="lift",
    )(current, packet, mats, *after)


def lift_kernel(bit, current, other, mats, *rest):
    out = rest[-1]
    skel = mats.shape[-1]
    both = jnp.concatenate([current[:, :skel], other[:, :skel]], axis=1)
    if out.shape[1] > skel:
        out[...] = jnp.zeros_like(out)
    out[:, :skel] = dot3(both, mats[bit])


def run_lift(bit, current, other, mats, after, width):
    return pl.pallas_call(
        functools.partial(lift_kernel, bit),
        in_specs=[VMEM] * 3 + [ANY] * len(after),
        out_specs=VMEM,
        out_shape=pltpu.VMEM((current.shape[0], width), F32),
        compiler_params=limit(1),
        cost_estimate=(HEAVY, LIGHT, MIDDLE, HEAVY, HEAVY)[bit],
        name="lift",
    )(current, other, mats, *after)


def prep_kernel(
    coeffs,
    second,
    first,
    after,
    leaf_tr_hbm,
    leaf_cp_hbm,
    inner_tr_hbm,
    inner_cp_hbm,
    tree_hbm,
    local_ref,
    reach_ref,
    tree,
    leaf_tr,
    leaf_cp,
    inner_tr,
    inner_cp,
    sems,
):
    del after
    copies = fetched(
        [
            (inner_cp_hbm, inner_cp),
            (inner_tr_hbm, inner_tr),
            (leaf_cp_hbm, leaf_cp),
            (leaf_tr_hbm, leaf_tr),
            (tree_hbm, tree),
        ],
        sems,
    )

    def coupled(values, table):
        a = dot3(values[:, 64:], table[:64], TURNED)
        b = dot3(values[:, :64], table[64:], TURNED)
        return jnp.concatenate([a, b], axis=1)

    for copy in copies[:4]:
        copy.wait()
    tops = coupled(first[...], inner_cp[0])
    mids = []
    for side in range(2):
        own = coupled(second[:, side * 128 : (side + 1) * 128], inner_cp[1 + side])
        mids.append(own + dot3(tops[:, side * 64 : (side + 1) * 64], inner_tr[1 + side], TURNED))
    reach_top = inner_tr[0]
    for pair in range(4):
        side = pair // 2
        low = (pair % 2) * 64
        own = coupled(coeffs[:, pair * 128 : (pair + 1) * 128], leaf_cp[pair])
        own = own + dot3(mids[side][:, low : low + 64], leaf_tr[pair], TURNED)
        local_ref[:, pair * 128 : (pair + 1) * 128] = own
        if pair % 2 == 0:
            reach_mid = dot3(inner_tr[1 + side], reach_top[side * 64 : (side + 1) * 64])
        reach_ref[pair * 128 : (pair + 1) * 128, :] = dot3(leaf_tr[pair], reach_mid[low : low + 64])
    copies[4].wait()


def run_prep(coeffs, second, first, leaf_tr, leaf_cp, inner_tr, inner_cp, tree_cp, after):
    rows = coeffs.shape[0]
    skel = first.shape[1] // 2
    tables = (leaf_tr, leaf_cp, inner_tr, inner_cp)
    return pl.pallas_call(
        prep_kernel,
        in_specs=[VMEM] * 3 + [ANY] * 6,
        out_specs=[VMEM] * 3,
        out_shape=[
            pltpu.VMEM((rows, 8 * skel), F32),
            pltpu.VMEM((8 * skel, skel), F32),
            pltpu.VMEM(tree_cp.shape, F32),
        ],
        scratch_shapes=[pltpu.VMEM(x.shape, F32) for x in tables] + [pltpu.SemaphoreType.DMA((5,))],
        compiler_params=limit(6),
        cost_estimate=LIGHT,
        name="prep",
    )(coeffs, second, first, after, *map(in_hbm, (*tables, tree_cp)))


def turn_kernel(depth, mats, tree, after, out, picked):
    del after
    skel, _, nodes = tree.shape
    heap = lax.axis_size("leaf") + lax.axis_index("leaf")
    choose(tree, lax.shift_right_logical(heap, node_rows(nodes)) - 2, picked)
    chain = None
    for bit in range(depth):
        couple = picked[pl.ds(bit, skel, stride=16), :]
        out[bit] = couple if chain is None else dot3(chain, couple)
        if bit + 1 < depth:
            step = mats[bit, :skel]
            chain = step if chain is None else dot3(chain, step)


def run_turn(depth, mats, tree, after):
    skel = tree.shape[0]
    return pl.pallas_call(
        functools.partial(turn_kernel, depth),
        in_specs=[VMEM] * 2 + [ANY],
        out_specs=VMEM,
        out_shape=pltpu.VMEM((depth, skel, skel), F32),
        scratch_shapes=[pltpu.VMEM((16 * skel, skel), F32)],
        compiler_params=limit(6),
        cost_estimate=LIGHT,
        name="turn",
    )(mats, tree, after)


def near_kernel(index, own, far, edge, edge_far, relay, diag, near, after, *rest):
    del after
    outs, grid = rest[:4], rest[4]
    rows, width = own.shape
    count, part, size = diag.shape
    wide = 2 * size
    odd = lax.rem(lax.axis_index("leaf"), 2)
    inner = pl.multiple_of((1 - odd) * (width + wide), wide)
    outer = pl.multiple_of(odd * (width + wide), wide)

    def place(source, start, length, group, column):
        target = (pl.ds(group * rows, rows), pl.ds(column, length))
        grid[target] = source[:, start : start + length]

    place(own, 0, width, 0, wide)
    place(relay, 0, width, 1, wide)
    place(far, 0, width, 2, wide)
    place(relay, width, width, 3, wide)
    for group, (source, start) in enumerate(
        ((edge, 0), (relay, 2 * width), (edge_far, 0), (relay, 2 * width + 2 * wide))
    ):
        place(source, start, wide, group, inner)
        place(source, start + wide, wide, group, outer)
    base = lax.axis_index("leaf") * count - 2
    dot = functools.partial(
        lax.dot_general, dimension_numbers=TURNED, preferred_element_type=F32
    )
    for leaf in range(count):
        total = dot(grid[:, (leaf + 2) * size : (leaf + 3) * size], diag[leaf])
        for j in range(near.shape[1]):
            column = pl.multiple_of((index[j, leaf] - base) * size, size)
            total = total + dot(grid[:, pl.ds(column, size)], near[leaf, j])
        for group, out in enumerate(outs):
            block = total[group * rows : (group + 1) * rows]
            out[:, leaf * part : (leaf + 1) * part] = block.astype(out.dtype)


def run_near(index, own, far, edge, edge_far, relay, diag, near, after):
    rows, width = own.shape
    count, part, size = diag.shape
    return pl.pallas_call(
        near_kernel,
        in_specs=[pl.BlockSpec(memory_space=pltpu.SMEM)] + [VMEM] * 7 + [ANY],
        out_specs=[VMEM] * 4,
        out_shape=[pltpu.VMEM((rows, count * part), F32)]
        + [pltpu.VMEM((rows, count * part), BF16)] * 3,
        scratch_shapes=[pltpu.VMEM((4 * rows, width + 4 * size), BF16)],
        compiler_params=limit(12),
        cost_estimate=LIGHT,
        name="near",
    )(index, own, far, edge, edge_far, relay, diag, near, after)


def settle_kernel(*refs):
    others, (turn, reach, local, leaf, final) = refs[:-5], refs[-5:]
    skel = turn.shape[1]
    total = None
    for bit, other in enumerate(others):
        term = dot3(other[:, :skel], turn[bit], TURNED)
        total = term if total is None else total + term
    leaf[...] = local[...] + dot3(total, reach[...], TURNED)
    final[...] = dot3(reach[...], turn[len(others)])


def run_settle(others, turn, reach, local):
    return pl.pallas_call(
        settle_kernel,
        in_specs=[VMEM] * (len(others) + 3),
        out_specs=[VMEM] * 2,
        out_shape=[pltpu.VMEM(local.shape, F32), pltpu.VMEM(reach.shape, F32)],
        compiler_params=limit(2),
        cost_estimate=LIGHT,
        name="settle",
    )(*others, turn, reach, local)


def last_kernel(other, final, local, basis, *rest):
    close, out = rest[:-1], rest[-1]
    skel = other.shape[1]
    count = local.shape[1] // skel
    size = basis.shape[1] // count
    part = close[0].shape[1] // count
    leaf = (local[...] + dot3(other[...], final[...], TURNED)).astype(BF16)
    place = lax.axis_index("rhs")
    for at in range(count):
        span = slice(at * size, (at + 1) * size)
        out[:, span] = lax.dot_general(
            leaf[:, at * skel : (at + 1) * skel], basis[:, span], PLAIN, preferred_element_type=F32
        )
        for group, block in enumerate(close):
            column = pl.multiple_of(at * size + (place ^ group) * part, part)
            here = pl.ds(column, part)
            out[:, here] = out[:, here] + block[:, at * part : (at + 1) * part].astype(F32)


def run_last(other, final, local, basis, close):
    rows = local.shape[0]
    return pl.pallas_call(
        last_kernel,
        in_specs=[VMEM] * (len(close) + 4),
        out_specs=VMEM,
        out_shape=jax.ShapeDtypeStruct((rows, basis.shape[1]), F32),
        compiler_params=limit(6),
        cost_estimate=LIGHT,
        name="last",
    )(other, final, local, basis, *close)


def local(
    rhs_block,
    col_basis,
    row_basis,
    leaf_transfer,
    leaf_coupling,
    inner_transfer,
    inner_coupling,
    tree_transfer,
    tree_coupling,
    diag_blocks,
    near_blocks,
    near_leaves,
):
    width = rhs_block.shape[1]
    count = leaf_transfer.shape[0]
    wide = 2 * (width // count)
    skel = col_basis.shape[0]
    span = lax.axis_size("leaf")
    ranks = lax.axis_size("rhs")
    depth = span.bit_length() - 1
    leaf_tr = leaf_transfer.reshape(count // 2, 2 * skel, skel)
    leaf_cp = leaf_coupling.reshape(count // 2, 2 * skel, skel)
    inner_tr = inner_transfer.reshape(count // 2 - 1, 2 * skel, skel)
    inner_cp = inner_coupling.reshape(count // 2 - 1, 2 * skel, skel)

    far = swapped(rhs_block, "rhs", 2)
    own, tree, coeffs, second, first, block, packet, outward = run_up(
        rhs_block, col_basis, leaf_tr, inner_tr, jnp.transpose(tree_transfer, (1, 2, 0))
    )

    packet = swapped(packet, "leaf", 1)
    mats = run_pick(depth, tree)
    pairs = [(i, i + 1) for i in range(1, span - 1, 2)]
    outward = lax.ppermute(outward, "leaf", pairs + [(j, i) for i, j in pairs])
    current, other = run_first_lift(block, packet, mats, [])
    others = [other]

    def step(current, beside, width=skel):
        bit = len(others)
        others.append(swapped(current, "leaf", 1 << bit))
        return run_lift(bit, current, others[-1], mats, beside, width)

    local_part, reach, tree = run_prep(
        coeffs,
        second,
        first,
        leaf_tr,
        leaf_cp,
        inner_tr,
        inner_cp,
        jnp.transpose(tree_coupling, (1, 2, 0)),
        current,
    )
    current = step(current, [reach])
    turn = run_turn(depth, mats, tree, current)
    edge = run_join([(packet, 2 * skel, wide), (outward, 0, wide)], [current])
    edge_far = swapped(edge, "rhs", 2)
    current = step(current, [turn])
    joined = run_join(
        [(own, 0, width), (far, 0, width), (edge, 0, 2 * wide), (edge_far, 0, 2 * wide)], [current]
    )
    relay = swapped(joined, "rhs", 1)
    current = step(current, [joined])
    close = run_near(
        near_leaves.T, own, far, edge, edge_far, relay, diag_blocks, near_blocks, current
    )
    current = step(current, close[:1])
    close = [close[0]] + [swapped(close[k], "rhs", k) for k in range(1, ranks)]
    leaf_part, final = run_settle(others, turn, reach, local_part)
    other = swapped(current, "leaf", 1 << len(others))
    return run_last(other, final, leaf_part, row_basis, close)


def solution(mesh):
    in_specs = (
        P("rhs", "leaf"),
        P(None, "leaf"),
        P(None, "leaf"),
        P("leaf", None, None),
        P("leaf", None, None),
        P("leaf", None, None, None),
        P("leaf", None, None, None),
        P(),
        P(),
        P("leaf", "rhs", None),
        P("leaf", None, "rhs", None),
        P("leaf", None),
    )
    out_specs = P("rhs", "leaf")
    return jax.shard_map(local, mesh=mesh, in_specs=in_specs, out_specs=out_specs, check_vma=False)
```

time: 55.3 us -> 47.1 us (0.85)
  the two profiles are of different devices: /device:TPU:2 before, /device:TPU:1 now
where the time goes in v2:
time: 47.1 us; the launch traced here: 47 us
  starting transfers between devices  31.7 us (67%)
  Pallas kernels  12.1 us (26%)
  waiting for transfers between devices  3.08 us (7%)
    ppermute x12, starting transfers between devices, swapped(): return lax.ppermute(x, axis, [(i, i ^ bit) for i in range(count)])  31 us
    ppermute x12, waiting for transfers between devices, swapped(): return lax.ppermute(x, axis, [(i, i ^ bit) for i in range(count)])  3.07 us
    pallas_call x1, Pallas kernels, run_prep(): pl.pallas_call(prep_kernel, in_specs=[VMEM] * 3 + [ANY] * 6, out_specs=[V...  2.42 us
    pallas_call x1, Pallas kernels, run_up(): pl.pallas_call(up_kernel, in_specs=[ANY] * 5, out_specs=[VMEM] * 8, out_s...  2.34 us
    pallas_call x1, Pallas kernels, run_near(): pl.pallas_call(near_kernel, in_specs=[pl.BlockSpec(memory_space=pltpu.SME...  1.66 us
    pallas_call x1, Pallas kernels, run_turn(): pl.pallas_call(functools.partial(turn_kernel, depth), in_specs=[VMEM] * 2...  1.48 us
    pallas_call x1, Pallas kernels, run_last(): pl.pallas_call(last_kernel, in_specs=[VMEM] * (len(close) + 4), out_specs...  1.4 us
  transfers between devices with their start and end apart: 13, of which 2 were waited for; matrix products, arithmetic and copies ran while one was open for 0% of the time, Pallas kernels for 18%

profile of v2, /device:TPU:1, one launch (start us, length us, event | category | flops | bytes accessed | tf_op | source)
XLA Modules:
  0.0 47.0 jit_solution(1866826113999428637)
XLA Ops:
  0.0 2.3 %up.1 = (bf16[32,4096]{1,0:T(8,128)(2,1)S(1)}, f32[64,64,126]{2,1,0:T(8,128)S(1)}, f32[32,512]{1,0:T(8,128)S(1)}, f32[32,256]{1,0:T(8,128)S(1)}, f32[32,128]{1,0...) custom-call(bf16[32,4096]{1,0:T(8,128)(2,1)} %rhs_hbm.1, ...), custom_call_target="tpu_custom_call" | custom-call | tf_op jit(solution)/shard_map/up/pallas_call | solution.py:122
  2.3 2.2 %collective-permute-start = (bf16[32,1152]{1,0:T(8,128)(2,1)S(1)}, bf16[32,1152]{1,0:T(8,128)(2,1)S(1)}, u32[]{:S(2)}, u32[]{:S(2)}) collective-permute-start(bf16[32,1152]{1,0:T(8,128)(2,1)S(1)} %get-tuple-element.25), channel_id=1, source_target_pairs={{0,4},{4,0},{8,12},{12,8},{16,20},{20,16},{24,28},{28,24},{32,36},... | collective-permute-start | bytes 221192 | tf_op jit(solution)/shard_map/ppermute | solution.py:36
  4.6 2.7 %collective-permute-start.4 = (bf16[32,4096]{1,0:T(8,128)(2,1)S(1)}, bf16[32,4096]{1,0:T(8,128)(2,1)S(1)}, u32[]{:S(2)}, u32[]{:S(2)}) collective-permute-start(bf16[32,4096]{1,0:T(8,128)(2,1)S(1)} %copy-done.4), channel_id=1, source_target_pairs={{0,2},{1,3},{2,0},{3,1},{4,6},{5,7},{6,4},{7,5},{8,10},{9,11},{10,... | collective-permute-start | bytes 786440 | tf_op jit(solution)/shard_map/ppermute | solution.py:36
  7.3 0.7 %collective-permute-start.5 = (bf16[32,1024]{1,0:T(8,128)(2,1)S(1)}, bf16[32,1024]{1,0:T(8,128)(2,1)S(1)}, u32[]{:S(2)}, u32[]{:S(2)}) collective-permute-start(bf16[32,1024]{1,0:T(8,128)(2,1)S(1)} %get-tuple-element.34), channel_id=1, source_target_pairs={{4,8},{12,16},{20,24},{28,32},{36,40},{44,48},{52,56},{60,64},{68,... | collective-permute-start | bytes 196616 | tf_op jit(solution)/shard_map/ppermute | solution.py:501
  8.0 0.8 %pick.1.mats = f32[5,128,64]{2,1,0:T(8,128)S(1)} custom-call(f32[64,64,126]{2,1,0:T(8,128)S(1)} %get-tuple-element.26.tree), custom_call_target="tpu_custom_call" | custom-call | tf_op jit(solution)/shard_map/pick/pallas_call | solution.py:202
  8.7 0.3 lift.5
  9.0 3.9 %collective-permute-start.1 = (f32[32,64]{1,0:T(8,128)S(1)}, f32[32,64]{1,0:T(8,128)S(1)}, u32[]{:S(2)}, u32[]{:S(2)}) collective-permute-start(f32[32,64]{1,0:T(8,128)S(1)} %get-tuple-element.27.after.current), channel_id=1, source_target_pairs={{0,8},{4,12},{8,0},{12,4},{16,24},{20,28},{24,16},{28,20},{32,40},... | collective-permute-start | bytes 24584 | tf_op jit(solution)/shard_map/ppermute | solution.py:36
  12.9 2.4 %prep.1 = (f32[32,512]{1,0:T(8,128)S(1)}, f32[512,64]{1,0:T(8,128)S(1)}, f32[64,64,126]{2,1,0:T(8,128)S(1)}) custom-call(f32[32,512]{1,0:T(8,128)S(1)} %get-tuple-element.28.coeffs, f32[32,256]{1,0:T(8,128)S(1)} %get-tuple-element.29.second, f32[32,128]{1,0:T(8,128)S(1)} %get-tuple-element.30.first, f32[32,64]{1,0:T(8,128)S(1)} %get-tuple-element.27.after.current, ...), custom_call_target="tpu_custom_call" | custom-call | tf_op jit(solution)/shard_map/prep/pallas_call | solution.py:315
  15.6 0.3 collective-permute-start.6
  15.9 2.4 %collective-permute-start.2 = (f32[32,64]{1,0:T(8,128)S(1)}, f32[32,64]{1,0:T(8,128)S(1)}, u32[]{:S(2)}, u32[]{:S(2)}) collective-permute-start(f32[32,64]{1,0:T(8,128)S(1)} %lift.6.after.current.refs_2_), channel_id=1, source_target_pairs={{0,16},{4,20},{8,24},{12,28},{16,0},{20,4},{24,8},{28,12},{32,48},... | collective-permute-start | bytes 24584 | tf_op jit(solution)/shard_map/ppermute | solution.py:36
  18.3 1.5 %turn.1.rest_0_.refs_5_ = f32[6,64,64]{2,1,0:T(8,128)S(1)} custom-call(f32[5,128,64]{2,1,0:T(8,128)S(1)} %pick.1.mats, f32[64,64,126]{2,1,0:T(8,128)S(1)} %get-tuple-element.32.tree, f32[32,64]{1,0:T(8,128)S(1)} %lift.6.after.current.refs_2_), custom_call_target="tpu_custom_call" | custom-call | tf_op jit(solution)/shard_map/turn/pallas_call | solution.py:347
  19.8 0.2 lift.7.refs_4_.current
  20.0 3.0 %collective-permute-start.3 = (f32[32,64]{1,0:T(8,128)S(1)}, f32[32,64]{1,0:T(8,128)S(1)}, u32[]{:S(2)}, u32[]{:S(2)}) collective-permute-start(f32[32,64]{1,0:T(8,128)S(1)} %lift.7.refs_4_.current), channel_id=1, source_target_pairs={{0,32},{4,36},{8,40},{12,44},{16,48},{20,52},{24,56},{28,60},{32,0... | collective-permute-start | bytes 24584 | tf_op jit(solution)/shard_map/ppermute | solution.py:36
  23.3 3.6 %collective-permute-start.8 = (bf16[32,12288]{1,0:T(8,128)(2,1)S(1)}, bf16[32,12288]{1,0:T(8,128)(2,1)S(1)}, u32[]{:S(2)}, u32[]{:S(2)}) collective-permute-start(bf16[32,12288]{1,0:T(8,128)(2,1)S(1)} %join.3.rest_0_), channel_id=1, source_target_pairs={{0,1},{1,0},{2,3},{3,2},{4,5},{5,4},{6,7},{7,6},{8,9},{9,8},{10,11... | collective-permute-start | bytes 2359304 | tf_op jit(solution)/shard_map/ppermute | solution.py:36
  27.1 6.0 %collective-permute-start.7 = (f32[32,64]{1,0:T(8,128)S(1)}, f32[32,64]{1,0:T(8,128)S(1)}, u32[]{:S(2)}, u32[]{:S(2)}) collective-permute-start(f32[32,64]{1,0:T(8,128)S(1)} %lift.8.after.current), channel_id=1, source_target_pairs={{0,64},{4,68},{8,72},{12,76},{16,80},{20,84},{24,88},{28,92},{32,9... | collective-permute-start | bytes 24584 | tf_op jit(solution)/shard_map/ppermute | solution.py:36
  33.1 1.7 %near.2 = (f32[32,1024]{1,0:T(8,128)S(1)}, bf16[32,1024]{1,0:T(8,128)(2,1)S(1)}, bf16[32,1024]{1,0:T(8,128)(2,1)S(1)}, bf16[32,1024]{1,0:T(8,128)(2,1)S(1)}) custom-call(s32[2,8]{1,0:T(2,128)S(1)} %bitcast.7, bf16[32,4096]{1,0:T(8,128)(2,1)S(1)} %get-tuple-element.33.refs_0_.own, bf16[32,4096]{1,0:T(8,128)(2,1)S(1)} %collective-permute-done.4.refs_1_.far, ...), custom_call_target="tpu_custom_call" | custom-call | tf_op jit(solution)/shard_map/near/pallas_call | solution.py:399
  34.8 2.3 %collective-permute-start.10 = (bf16[32,1024]{1,0:T(8,128)(2,1)S(1)}, bf16[32,1024]{1,0:T(8,128)(2,1)S(1)}, u32[]{:S(2)}, u32[]{:S(2)}) collective-permute-start(bf16[32,1024]{1,0:T(8,128)(2,1)S(1)} %get-tuple-element.40), channel_id=1, source_target_pairs={{0,1},{1,0},{2,3},{3,2},{4,5},{5,4},{6,7},{7,6},{8,9},{9,8},{10,11... | collective-permute-start | bytes 196616 | tf_op jit(solution)/shard_map/ppermute | solution.py:36
  37.1 2.8 %collective-permute-start.11 = (bf16[32,1024]{1,0:T(8,128)(2,1)S(1)}, bf16[32,1024]{1,0:T(8,128)(2,1)S(1)}, u32[]{:S(2)}, u32[]{:S(2)}) collective-permute-start(bf16[32,1024]{1,0:T(8,128)(2,1)S(1)} %get-tuple-element.41), channel_id=1, source_target_pairs={{0,2},{1,3},{2,0},{3,1},{4,6},{5,7},{6,4},{7,5},{8,10},{9,11},{10,... | collective-permute-start | bytes 196616 | tf_op jit(solution)/shard_map/ppermute | solution.py:36
  39.9 0.5 %collective-permute-start.12 = (bf16[32,1024]{1,0:T(8,128)(2,1)S(1)}, bf16[32,1024]{1,0:T(8,128)(2,1)S(1)}, u32[]{:S(2)}, u32[]{:S(2)}) collective-permute-start(bf16[32,1024]{1,0:T(8,128)(2,1)S(1)} %get-tuple-element.42), channel_id=1, source_target_pairs={{0,3},{1,2},{2,1},{3,0},{4,7},{5,6},{6,5},{7,4},{8,11},{9,10},{10,... | collective-permute-start | bytes 196616 | tf_op jit(solution)/shard_map/ppermute | solution.py:36
  40.5 1.2 %collective-permute-start.9 = (f32[32,64]{1,0:T(8,128)S(1)}, f32[32,64]{1,0:T(8,128)S(1)}, u32[]{:S(2)}, u32[]{:S(2)}) collective-permute-start(f32[32,64]{1,0:T(8,128)S(1)} %lift.9), channel_id=1, source_target_pairs={{0,128},{4,132},{8,136},{12,140},{16,144},{20,148},{24,152},{28,15... | collective-permute-start | bytes 24584 | tf_op jit(solution)/shard_map/ppermute | solution.py:36
  41.8 0.8 %settle.1 = (f32[32,512]{1,0:T(8,128)S(1)}, f32[512,64]{1,0:T(8,128)S(1)}) custom-call(f32[32,64]{1,0:T(8,128)S(1)} %get-tuple-element.36.refs_0_, f32[32,64]{1,0:T(8,128)S(1)} %collective-permute-done.1.other.refs_1_, f32[32,64]{1,0:T(8,128)S(1)} %collective-permute-done.2.other.refs_2_, f32[32,64]{1,0:T(8,128)S(1)} %collective-permute-done.3.other.refs_3_, ...), custom_call_target="tpu_custom_call" | custom-call | tf_op jit(solution)/shard_map/settle/pallas_call | solution.py:424
  42.6 1.4 %collective-permute-done.9.other = f32[32,64]{1,0:T(8,128)S(1)} collective-permute-done((f32[32,64]{1,0:T(8,128)S(1)}, f32[32,64]{1,0:T(8,128)S(1)}, u32[]{:S(2)}, u32[]{:S(2)}) %collective-permute-start.9) | collective-permute-done | bytes 8224 | tf_op jit(solution)/shard_map/ppermute | solution.py:36
  44.0 1.6 %collective-permute-done.12.rest_3_ = bf16[32,1024]{1,0:T(8,128)(2,1)S(1)} collective-permute-done((bf16[32,1024]{1,0:T(8,128)(2,1)S(1)}, bf16[32,1024]{1,0:T(8,128)(2,1)S(1)}, u32[]{:S(2)}, u32[]{:S(2)}) %collective-permute-start.12) | collective-permute-done | bytes 65568 | tf_op jit(solution)/shard_map/ppermute | solution.py:36
  45.6 1.4 %last.1 = f32[32,4096]{1,0:T(8,128)} custom-call(f32[32,64]{1,0:T(8,128)S(1)} %collective-permute-done.9.other, f32[512,64]{1,0:T(8,128)S(1)} %get-tuple-element.38.final, f32[32,512]{1,0:T(8,128)S(1)} %get-tuple-element.39.local, bf16[64,4096]{1,0:T(8,128)(2,1)S(1)} %copy-done.2, f32[32,1024]{1,0:T(8,128)S(1)} %get-tuple-element.35.rest_0_, ...), custom_call_target="tpu_custom_call" | custom-call | tf_op jit(solution)/shard_map/last/pallas_call | solution.py:456
  (26 shorter events, 0.9 us)
Async XLA Ops:
  0.0 4.6 %copy-start.4 = (bf16[32,4096]{1,0:T(8,128)(2,1)S(1)}, bf16[32,4096]{1,0:T(8,128)(2,1)}, u32[]{:S(2)}) copy-start(bf16[32,4096]{1,0:T(8,128)(2,1)} %rhs_hbm.1) | copy-start | bytes 786436
  2.3 6.4 %collective-permute-start = (bf16[32,1152]{1,0:T(8,128)(2,1)S(1)}, bf16[32,1152]{1,0:T(8,128)(2,1)S(1)}, u32[]{:S(2)}, u32[]{:S(2)}) collective-permute-start(bf16[32,1152]{1,0:T(8,128)(2,1)S(1)} %get-tuple-element.25), channel_id=1, source_target_pairs={{0,4},{4,0},{8,12},{12,8},{16,20},{20,16},{24,28},{28,24},{32,36},... | collective-permute-start | bytes 221192 | tf_op jit(solution)/shard_map/ppermute | solution.py:36
  4.6 18.5 %collective-permute-start.4 = (bf16[32,4096]{1,0:T(8,128)(2,1)S(1)}, bf16[32,4096]{1,0:T(8,128)(2,1)S(1)}, u32[]{:S(2)}, u32[]{:S(2)}) collective-permute-start(bf16[32,4096]{1,0:T(8,128)(2,1)S(1)} %copy-done.4), channel_id=1, source_target_pairs={{0,2},{1,3},{2,0},{3,1},{4,6},{5,7},{6,4},{7,5},{8,10},{9,11},{10,... | collective-permute-start | bytes 786440 | tf_op jit(solution)/shard_map/ppermute | solution.py:36
  7.3 8.2 %collective-permute-start.5 = (bf16[32,1024]{1,0:T(8,128)(2,1)S(1)}, bf16[32,1024]{1,0:T(8,128)(2,1)S(1)}, u32[]{:S(2)}, u32[]{:S(2)}) collective-permute-start(bf16[32,1024]{1,0:T(8,128)(2,1)S(1)} %get-tuple-element.34), channel_id=1, source_target_pairs={{4,8},{12,16},{20,24},{28,32},{36,40},{44,48},{52,56},{60,64},{68,... | collective-permute-start | bytes 196616 | tf_op jit(solution)/shard_map/ppermute | solution.py:501
  9.0 6.3 %collective-permute-start.1 = (f32[32,64]{1,0:T(8,128)S(1)}, f32[32,64]{1,0:T(8,128)S(1)}, u32[]{:S(2)}, u32[]{:S(2)}) collective-permute-start(f32[32,64]{1,0:T(8,128)S(1)} %get-tuple-element.27.after.current), channel_id=1, source_target_pairs={{0,8},{4,12},{8,0},{12,4},{16,24},{20,28},{24,16},{28,20},{32,40},... | collective-permute-start | bytes 24584 | tf_op jit(solution)/shard_map/ppermute | solution.py:36
  15.6 7.4 %collective-permute-start.6 = (bf16[32,2048]{1,0:T(8,128)(2,1)S(1)}, bf16[32,2048]{1,0:T(8,128)(2,1)S(1)}, u32[]{:S(2)}, u32[]{:S(2)}) collective-permute-start(bf16[32,2048]{1,0:T(8,128)(2,1)S(1)} %join.2.refs_2_.edge), channel_id=1, source_target_pairs={{0,2},{1,3},{2,0},{3,1},{4,6},{5,7},{6,4},{7,5},{8,10},{9,11},{10,... | collective-permute-start | bytes 393224 | tf_op jit(solution)/shard_map/ppermute | solution.py:36
  15.9 3.9 %collective-permute-start.2 = (f32[32,64]{1,0:T(8,128)S(1)}, f32[32,64]{1,0:T(8,128)S(1)}, u32[]{:S(2)}, u32[]{:S(2)}) collective-permute-start(f32[32,64]{1,0:T(8,128)S(1)} %lift.6.after.current.refs_2_), channel_id=1, source_target_pairs={{0,16},{4,20},{8,24},{12,28},{16,0},{20,4},{24,8},{28,12},{32,48},... | collective-permute-start | bytes 24584 | tf_op jit(solution)/shard_map/ppermute | solution.py:36
  20.0 6.9 %collective-permute-start.3 = (f32[32,64]{1,0:T(8,128)S(1)}, f32[32,64]{1,0:T(8,128)S(1)}, u32[]{:S(2)}, u32[]{:S(2)}) collective-permute-start(f32[32,64]{1,0:T(8,128)S(1)} %lift.7.refs_4_.current), channel_id=1, source_target_pairs={{0,32},{4,36},{8,40},{12,44},{16,48},{20,52},{24,56},{28,60},{32,0... | collective-permute-start | bytes 24584 | tf_op jit(solution)/shard_map/ppermute | solution.py:36
  23.2 9.9 %copy-start = (bf16[8,2,128,512]{3,2,1,0:T(8,128)(2,1)S(1)}, bf16[8,2,128,512]{3,2,1,0:T(8,128)(2,1)}, u32[]{:S(2)}) copy-start(bf16[8,2,128,512]{3,2,1,0:T(8,128)(2,1)} %near.3) | copy-start | bytes 6291460
  23.2 9.9 %copy-start.1 = (bf16[8,128,512]{2,1,0:T(8,128)(2,1)S(1)}, bf16[8,128,512]{2,1,0:T(8,128)(2,1)}, u32[]{:S(2)}) copy-start(bf16[8,128,512]{2,1,0:T(8,128)(2,1)} %diag.1) | copy-start | bytes 3145732
  23.2 9.9 %copy-start.3 = (s32[8,2]{0,1:T(2,128)S(1)}, s32[8,2]{0,1:T(2,128)}, u32[]{:S(2)}) copy-start(s32[8,2]{0,1:T(2,128)} %param.23) | copy-start | bytes 196
  23.3 9.9 %collective-permute-start.8 = (bf16[32,12288]{1,0:T(8,128)(2,1)S(1)}, bf16[32,12288]{1,0:T(8,128)(2,1)S(1)}, u32[]{:S(2)}, u32[]{:S(2)}) collective-permute-start(bf16[32,12288]{1,0:T(8,128)(2,1)S(1)} %join.3.rest_0_), channel_id=1, source_target_pairs={{0,1},{1,0},{2,3},{3,2},{4,5},{5,4},{6,7},{7,6},{8,9},{9,8},{10,11... | collective-permute-start | bytes 2359304 | tf_op jit(solution)/shard_map/ppermute | solution.py:36
  27.1 13.3 %collective-permute-start.7 = (f32[32,64]{1,0:T(8,128)S(1)}, f32[32,64]{1,0:T(8,128)S(1)}, u32[]{:S(2)}, u32[]{:S(2)}) collective-permute-start(f32[32,64]{1,0:T(8,128)S(1)} %lift.8.after.current), channel_id=1, source_target_pairs={{0,64},{4,68},{8,72},{12,76},{16,80},{20,84},{24,88},{28,92},{32,9... | collective-permute-start | bytes 24584 | tf_op jit(solution)/shard_map/ppermute | solution.py:36
  34.8 9.2 %collective-permute-start.10 = (bf16[32,1024]{1,0:T(8,128)(2,1)S(1)}, bf16[32,1024]{1,0:T(8,128)(2,1)S(1)}, u32[]{:S(2)}, u32[]{:S(2)}) collective-permute-start(bf16[32,1024]{1,0:T(8,128)(2,1)S(1)} %get-tuple-element.40), channel_id=1, source_target_pairs={{0,1},{1,0},{2,3},{3,2},{4,5},{5,4},{6,7},{7,6},{8,9},{9,8},{10,11... | collective-permute-start | bytes 196616 | tf_op jit(solution)/shard_map/ppermute | solution.py:36
  37.1 6.9 %collective-permute-start.11 = (bf16[32,1024]{1,0:T(8,128)(2,1)S(1)}, bf16[32,1024]{1,0:T(8,128)(2,1)S(1)}, u32[]{:S(2)}, u32[]{:S(2)}) collective-permute-start(bf16[32,1024]{1,0:T(8,128)(2,1)S(1)} %get-tuple-element.41), channel_id=1, source_target_pairs={{0,2},{1,3},{2,0},{3,1},{4,6},{5,7},{6,4},{7,5},{8,10},{9,11},{10,... | collective-permute-start | bytes 196616 | tf_op jit(solution)/shard_map/ppermute | solution.py:36
  39.9 5.7 %collective-permute-start.12 = (bf16[32,1024]{1,0:T(8,128)(2,1)S(1)}, bf16[32,1024]{1,0:T(8,128)(2,1)S(1)}, u32[]{:S(2)}, u32[]{:S(2)}) collective-permute-start(bf16[32,1024]{1,0:T(8,128)(2,1)S(1)} %get-tuple-element.42), channel_id=1, source_target_pairs={{0,3},{1,2},{2,1},{3,0},{4,7},{5,6},{6,5},{7,4},{8,11},{9,10},{10,... | collective-permute-start | bytes 196616 | tf_op jit(solution)/shard_map/ppermute | solution.py:36
  40.3 5.3 %copy-start.2 = (bf16[64,4096]{1,0:T(8,128)(2,1)S(1)}, bf16[64,4096]{1,0:T(8,128)(2,1)}, u32[]{:S(2)}) copy-start(bf16[64,4096]{1,0:T(8,128)(2,1)} %basis.1) | copy-start | bytes 1572868
  40.5 3.5 %collective-permute-start.9 = (f32[32,64]{1,0:T(8,128)S(1)}, f32[32,64]{1,0:T(8,128)S(1)}, u32[]{:S(2)}, u32[]{:S(2)}) collective-permute-start(f32[32,64]{1,0:T(8,128)S(1)} %lift.9), channel_id=1, source_target_pairs={{0,128},{4,132},{8,136},{12,140},{16,144},{20,148},{24,152},{28,15... | collective-permute-start | bytes 24584 | tf_op jit(solution)/shard_map/ppermute | solution.py:36

commit v3 on v2

--- a/solution.py
+++ b/solution.py
@@ -7,16 +7,20 @@
 from jax.experimental.pallas import tpu as pltpu
 from jax.sharding import PartitionSpec as P
 
-HIGH = lax.Precision.HIGHEST
 F32 = jnp.float32
 BF16 = jnp.bfloat16
 VMEM = pl.BlockSpec(memory_space=pltpu.VMEM)
 ANY = pl.BlockSpec(memory_space=pl.ANY)
-LIGHT = pl.CostEstimate(flops=0, bytes_accessed=0, transcendentals=0)
-HEAVY = pl.CostEstimate(flops=20_000_000_000, bytes_accessed=60_000_000, transcendentals=0)
-MIDDLE = pl.CostEstimate(flops=0, bytes_accessed=11_000_000, transcendentals=0)
 PLAIN = (((1,), (0,)), ((), ()))
 TURNED = (((1,), (1,)), ((), ()))
+
+
+def work(flops):
+    return pl.CostEstimate(flops=flops, bytes_accessed=0, transcendentals=0)
+
+
+LIFT_WORK = (20_000_000_000, 500_000_000, 2_500_000_000, 20_000_000_000, 20_000_000_000)
+LIGHT = work(0)
 
 
 def halves(x):
@@ -226,7 +230,7 @@
         out_specs=[VMEM] * 2,
         out_shape=[pltpu.VMEM(current.shape, F32)] * 2,
         compiler_params=limit(1),
-        cost_estimate=HEAVY,
+        cost_estimate=work(LIFT_WORK[0]),
         name="lift",
     )(current, packet, mats, *after)
 
@@ -247,7 +251,7 @@
         out_specs=VMEM,
         out_shape=pltpu.VMEM((current.shape[0], width), F32),
         compiler_params=limit(1),
-        cost_estimate=(HEAVY, LIGHT, MIDDLE, HEAVY, HEAVY)[bit],
+        cost_estimate=work(LIFT_WORK[bit]),
         name="lift",
     )(current, other, mats, *after)
 
@@ -356,7 +360,7 @@
     )(mats, tree, after)
 
 
-def near_kernel(index, own, far, edge, edge_far, relay, diag, near, after, *rest):
+def near_kernel(index, own, mate, far, edge, edge_far, relay, diag, near, after, *rest):
     del after
     outs, grid = rest[:4], rest[4]
     rows, width = own.shape
@@ -371,11 +375,11 @@
         grid[target] = source[:, start : start + length]
 
     place(own, 0, width, 0, wide)
-    place(relay, 0, width, 1, wide)
+    place(mate, 0, width, 1, wide)
     place(far, 0, width, 2, wide)
-    place(relay, width, width, 3, wide)
+    place(relay, 0, width, 3, wide)
     for group, (source, start) in enumerate(
-        ((edge, 0), (relay, 2 * width), (edge_far, 0), (relay, 2 * width + 2 * wide))
+        ((edge, 0), (relay, width), (edge_far, 0), (relay, width + 2 * wide))
     ):
         place(source, start, wide, group, inner)
         place(source, start + wide, wide, group, outer)
@@ -393,12 +397,12 @@
             out[:, leaf * part : (leaf + 1) * part] = block.astype(out.dtype)
 
 
-def run_near(index, own, far, edge, edge_far, relay, diag, near, after):
+def run_near(index, own, mate, far, edge, edge_far, relay, diag, near, after):
     rows, width = own.shape
     count, part, size = diag.shape
     return pl.pallas_call(
         near_kernel,
-        in_specs=[pl.BlockSpec(memory_space=pltpu.SMEM)] + [VMEM] * 7 + [ANY],
+        in_specs=[pl.BlockSpec(memory_space=pltpu.SMEM)] + [VMEM] * 8 + [ANY],
         out_specs=[VMEM] * 4,
         out_shape=[pltpu.VMEM((rows, count * part), F32)]
         + [pltpu.VMEM((rows, count * part), BF16)] * 3,
@@ -406,7 +410,7 @@
         compiler_params=limit(12),
         cost_estimate=LIGHT,
         name="near",
-    )(index, own, far, edge, edge_far, relay, diag, near, after)
+    )(index, own, mate, far, edge, edge_far, relay, diag, near, after)
 
 
 def settle_kernel(*refs):
@@ -432,36 +436,49 @@
     )(*others, turn, reach, local)
 
 
-def last_kernel(other, final, local, basis, *rest):
-    close, out = rest[:-1], rest[-1]
+def last_kernel(groups, other, final, local, basis, *rest):
+    close, (out_hbm, out, sems) = rest[:-3], rest[-3:]
     skel = other.shape[1]
     count = local.shape[1] // skel
     size = basis.shape[1] // count
     part = close[0].shape[1] // count
     leaf = (local[...] + dot3(other[...], final[...], TURNED)).astype(BF16)
     place = lax.axis_index("rhs")
+    copies = []
     for at in range(count):
         span = slice(at * size, (at + 1) * size)
         out[:, span] = lax.dot_general(
             leaf[:, at * skel : (at + 1) * skel], basis[:, span], PLAIN, preferred_element_type=F32
         )
-        for group, block in enumerate(close):
+        for group, block in zip(groups, close):
             column = pl.multiple_of(at * size + (place ^ group) * part, part)
             here = pl.ds(column, part)
             out[:, here] = out[:, here] + block[:, at * part : (at + 1) * part].astype(F32)
+        if at % 2:
+            here = pl.ds((at - 1) * size, 2 * size)
+            copy = pltpu.make_async_copy(out.at[:, here], out_hbm.at[:, here], sems.at[at // 2])
+            copy.start()
+            copies.append(copy)
+    for copy in copies:
+        copy.wait()
 
 
 def run_last(other, final, local, basis, close):
     rows = local.shape[0]
-    return pl.pallas_call(
-        last_kernel,
+    groups = list(close)
+    return pl.pallas_call(
+        functools.partial(last_kernel, groups),
         in_specs=[VMEM] * (len(close) + 4),
-        out_specs=VMEM,
+        out_specs=ANY,
         out_shape=jax.ShapeDtypeStruct((rows, basis.shape[1]), F32),
+        scratch_shapes=[
+            pltpu.VMEM((rows, basis.shape[1]), F32),
+            pltpu.SemaphoreType.DMA((local.shape[1] // other.shape[1] // 2,)),
+        ],
         compiler_params=limit(6),
         cost_estimate=LIGHT,
         name="last",
-    )(other, final, local, basis, *close)
+    )(other, final, local, basis, *close.values())
 
 
 def local(
@@ -491,6 +508,7 @@
     inner_cp = inner_coupling.reshape(count // 2 - 1, 2 * skel, skel)
 
     far = swapped(rhs_block, "rhs", 2)
+    mate = swapped(rhs_block, "rhs", 1)
     own, tree, coeffs, second, first, block, packet, outward = run_up(
         rhs_block, col_basis, leaf_tr, inner_tr, jnp.transpose(tree_transfer, (1, 2, 0))
     )
@@ -519,20 +537,20 @@
         current,
     )
     current = step(current, [reach])
-    turn = run_turn(depth, mats, tree, current)
     edge = run_join([(packet, 2 * skel, wide), (outward, 0, wide)], [current])
     edge_far = swapped(edge, "rhs", 2)
-    current = step(current, [turn])
+    current = step(current, [edge])
+    turn = run_turn(depth, mats, tree, current)
     joined = run_join(
-        [(own, 0, width), (far, 0, width), (edge, 0, 2 * wide), (edge_far, 0, 2 * wide)], [current]
+        [(far, 0, width), (edge, 0, 2 * wide), (edge_far, 0, 2 * wide)], [current]
     )
     relay = swapped(joined, "rhs", 1)
-    current = step(current, [joined])
+    current = step(current, [joined, turn])
     close = run_near(
-        near_leaves.T, own, far, edge, edge_far, relay, diag_blocks, near_blocks, current
+        near_leaves.T, own, mate, far, edge, edge_far, relay, diag_blocks, near_blocks, current
     )
     current = step(current, close[:1])
-    close = [close[0]] + [swapped(close[k], "rhs", k) for k in range(1, ranks)]
+    close = {k: swapped(close[k], "rhs", k) if k else close[0] for k in (0, 2, 3, 1)}
     leaf_part, final = run_settle(others, turn, reach, local_part)
     other = swapped(current, "leaf", 1 << len(others))
     return run_last(other, final, leaf_part, row_basis, close)

time: 47.1 us -> 43.5 us (0.924)
  starting transfers between devices: 31.7 us -> 28 us
    ppermute x12 -> x13, starting transfers between devices: 31 us -> 27.4 us  [swapped(): return lax.ppermute(x, axis, [(i, i ^ bit) for i in range(count)])]
    ppermute x12 -> x13, waiting for transfers between devices: 3.07 us -> 3.28 us  [swapped(): return lax.ppermute(x, axis, [(i, i ^ bit) for i in range(count)])]
  transfers between devices with their start and end apart: 13 -> 14, of which waited for: 2 -> 4; matrix products, arithmetic and copies ran while one was open for 0% -> 0% of each run, Pallas kernels for 18% -> 19%
where the time goes in v3:
time: 43.5 us; the launch traced here: 43.4 us
  starting transfers between devices  28 us (64%)
  Pallas kernels  11.9 us (27%)
  waiting for transfers between devices  3.28 us (8%)
    ppermute x13, starting transfers between devices, swapped(): return lax.ppermute(x, axis, [(i, i ^ bit) for i in range(count)])  27.4 us
    ppermute x13, waiting for transfers between devices, swapped(): return lax.ppermute(x, axis, [(i, i ^ bit) for i in range(count)])  3.28 us
    pallas_call x1, Pallas kernels, run_prep(): pl.pallas_call(prep_kernel, in_specs=[VMEM] * 3 + [ANY] * 6, out_specs=[V...  2.43 us
    pallas_call x1, Pallas kernels, run_up(): pl.pallas_call(up_kernel, in_specs=[ANY] * 5, out_specs=[VMEM] * 8, out_s...  2.3 us
    pallas_call x1, Pallas kernels, run_near(): pl.pallas_call(near_kernel, in_specs=[pl.BlockSpec(memory_space=pltpu.SME...  1.66 us
    pallas_call x1, Pallas kernels, run_turn(): pl.pallas_call(functools.partial(turn_kernel, depth), in_specs=[VMEM] * 2...  1.48 us
    pallas_call x1, Pallas kernels, run_last(): pl.pallas_call(functools.partial(last_kernel, groups), in_specs=[VMEM] *...  1.3 us
  transfers between devices with their start and end apart: 14, of which 4 were waited for; matrix products, arithmetic and copies ran while one was open for 0% of the time, Pallas kernels for 19%

profile of v3, /device:TPU:1, one launch (start us, length us, event | category | flops | bytes accessed | tf_op | source)
XLA Modules:
  0.0 43.4 jit_solution(2057404827080824566)
XLA Ops:
  0.0 2.3 %up.1 = (bf16[32,4096]{1,0:T(8,128)(2,1)S(1)}, f32[64,64,126]{2,1,0:T(8,128)S(1)}, f32[32,512]{1,0:T(8,128)S(1)}, f32[32,256]{1,0:T(8,128)S(1)}, f32[32,128]{1,0...) custom-call(bf16[32,4096]{1,0:T(8,128)(2,1)} %rhs_hbm.1, ...), custom_call_target="tpu_custom_call" | custom-call | tf_op jit(solution)/shard_map/up/pallas_call | solution.py:126
  2.3 2.2 %collective-permute-start = (bf16[32,1152]{1,0:T(8,128)(2,1)S(1)}, bf16[32,1152]{1,0:T(8,128)(2,1)S(1)}, u32[]{:S(2)}, u32[]{:S(2)}) collective-permute-start(bf16[32,1152]{1,0:T(8,128)(2,1)S(1)} %get-tuple-element.25), channel_id=1, source_target_pairs={{0,4},{4,0},{8,12},{12,8},{16,20},{20,16},{24,28},{28,24},{32,36},... | collective-permute-start | bytes 221192 | tf_op jit(solution)/shard_map/ppermute | solution.py:40
  4.5 0.7 %collective-permute-start.3 = (bf16[32,1024]{1,0:T(8,128)(2,1)S(1)}, bf16[32,1024]{1,0:T(8,128)(2,1)S(1)}, u32[]{:S(2)}, u32[]{:S(2)}) collective-permute-start(bf16[32,1024]{1,0:T(8,128)(2,1)S(1)} %get-tuple-element.32), channel_id=1, source_target_pairs={{4,8},{12,16},{20,24},{28,32},{36,40},{44,48},{52,56},{60,64},{68,... | collective-permute-start | bytes 196616 | tf_op jit(solution)/shard_map/ppermute | solution.py:519
  5.2 0.8 %pick.1.mats = f32[5,128,64]{2,1,0:T(8,128)S(1)} custom-call(f32[64,64,126]{2,1,0:T(8,128)S(1)} %get-tuple-element.26.tree), custom_call_target="tpu_custom_call" | custom-call | tf_op jit(solution)/shard_map/pick/pallas_call | solution.py:206
  6.0 0.3 collective-permute-done.packet.refs_0_
  6.3 0.3 lift.5
  6.5 3.6 %collective-permute-start.1 = (f32[32,64]{1,0:T(8,128)S(1)}, f32[32,64]{1,0:T(8,128)S(1)}, u32[]{:S(2)}, u32[]{:S(2)}) collective-permute-start(f32[32,64]{1,0:T(8,128)S(1)} %get-tuple-element.27.after.current), channel_id=1, source_target_pairs={{0,8},{4,12},{8,0},{12,4},{16,24},{20,28},{24,16},{28,20},{32,40},... | collective-permute-start | bytes 24584 | tf_op jit(solution)/shard_map/ppermute | solution.py:40
  10.1 2.7 %collective-permute-start.5 = (bf16[32,4096]{1,0:T(8,128)(2,1)S(1)}, bf16[32,4096]{1,0:T(8,128)(2,1)S(1)}, u32[]{:S(2)}, u32[]{:S(2)}) collective-permute-start(bf16[32,4096]{1,0:T(8,128)(2,1)S(1)} %copy-done.4), channel_id=1, source_target_pairs={{0,2},{1,3},{2,0},{3,1},{4,6},{5,7},{6,4},{7,5},{8,10},{9,11},{10,... | collective-permute-start | bytes 786440 | tf_op jit(solution)/shard_map/ppermute | solution.py:40
  12.9 2.4 %prep.1 = (f32[32,512]{1,0:T(8,128)S(1)}, f32[512,64]{1,0:T(8,128)S(1)}, f32[64,64,126]{2,1,0:T(8,128)S(1)}) custom-call(f32[32,512]{1,0:T(8,128)S(1)} %get-tuple-element.28.coeffs, f32[32,256]{1,0:T(8,128)S(1)} %get-tuple-element.29.second, f32[32,128]{1,0:T(8,128)S(1)} %get-tuple-element.30.first, f32[32,64]{1,0:T(8,128)S(1)} %get-tuple-element.27.after.current, ...), custom_call_target="tpu_custom_call" | custom-call | tf_op jit(solution)/shard_map/prep/pallas_call | solution.py:319
  15.5 1.7 %collective-permute-start.2 = (f32[32,64]{1,0:T(8,128)S(1)}, f32[32,64]{1,0:T(8,128)S(1)}, u32[]{:S(2)}, u32[]{:S(2)}) collective-permute-start(f32[32,64]{1,0:T(8,128)S(1)} %lift.6.refs_2_.current), channel_id=1, source_target_pairs={{0,16},{4,20},{8,24},{12,28},{16,0},{20,4},{24,8},{28,12},{32,48},... | collective-permute-start | bytes 24584 | tf_op jit(solution)/shard_map/ppermute | solution.py:40
  17.2 0.8 %collective-permute-start.6 = (bf16[32,2048]{1,0:T(8,128)(2,1)S(1)}, bf16[32,2048]{1,0:T(8,128)(2,1)S(1)}, u32[]{:S(2)}, u32[]{:S(2)}) collective-permute-start(bf16[32,2048]{1,0:T(8,128)(2,1)S(1)} %join.2.rest_0_.refs_1_.edge), channel_id=1, source_target_pairs={{0,2},{1,3},{2,0},{3,1},{4,6},{5,7},{6,4},{7,5},{8,10},{9,11},{10,... | collective-permute-start | bytes 393224 | tf_op jit(solution)/shard_map/ppermute | solution.py:40
  18.1 0.5 %collective-permute-done.2.other.refs_2_ = f32[32,64]{1,0:T(8,128)S(1)} collective-permute-done((f32[32,64]{1,0:T(8,128)S(1)}, f32[32,64]{1,0:T(8,128)S(1)}, u32[]{:S(2)}, u32[]{:S(2)}) %collective-permute-start.2) | collective-permute-done | bytes 8224 | tf_op jit(solution)/shard_map/ppermute | solution.py:40
  18.8 3.0 %collective-permute-start.4 = (f32[32,64]{1,0:T(8,128)S(1)}, f32[32,64]{1,0:T(8,128)S(1)}, u32[]{:S(2)}, u32[]{:S(2)}) collective-permute-start(f32[32,64]{1,0:T(8,128)S(1)} %lift.7.refs_3_.after.current), channel_id=1, source_target_pairs={{0,32},{4,36},{8,40},{12,44},{16,48},{20,52},{24,56},{28,60},{32,0... | collective-permute-start | bytes 24584 | tf_op jit(solution)/shard_map/ppermute | solution.py:40
  21.8 2.8 %collective-permute-start.8 = (bf16[32,4096]{1,0:T(8,128)(2,1)S(1)}, bf16[32,4096]{1,0:T(8,128)(2,1)S(1)}, u32[]{:S(2)}, u32[]{:S(2)}) collective-permute-start(bf16[32,4096]{1,0:T(8,128)(2,1)S(1)} %copy-done.4), channel_id=1, source_target_pairs={{0,1},{1,0},{2,3},{3,2},{4,5},{5,4},{6,7},{7,6},{8,9},{9,8},{10,11... | collective-permute-start | bytes 786440 | tf_op jit(solution)/shard_map/ppermute | solution.py:40
  24.6 1.5 %turn.1.rest_1_.refs_5_ = f32[6,64,64]{2,1,0:T(8,128)S(1)} custom-call(f32[5,128,64]{2,1,0:T(8,128)S(1)} %pick.1.mats, f32[64,64,126]{2,1,0:T(8,128)S(1)} %get-tuple-element.33.tree, f32[32,64]{1,0:T(8,128)S(1)} %lift.7.refs_3_.after.current), custom_call_target="tpu_custom_call" | custom-call | tf_op jit(solution)/shard_map/turn/pallas_call | solution.py:351
  26.6 5.8 %collective-permute-start.7 = (f32[32,64]{1,0:T(8,128)S(1)}, f32[32,64]{1,0:T(8,128)S(1)}, u32[]{:S(2)}, u32[]{:S(2)}) collective-permute-start(f32[32,64]{1,0:T(8,128)S(1)} %lift.8.after.current), channel_id=1, source_target_pairs={{0,64},{4,68},{8,72},{12,76},{16,80},{20,84},{24,88},{28,92},{32,9... | collective-permute-start | bytes 24584 | tf_op jit(solution)/shard_map/ppermute | solution.py:40
  32.5 1.7 %near.2 = (f32[32,1024]{1,0:T(8,128)S(1)}, bf16[32,1024]{1,0:T(8,128)(2,1)S(1)}, bf16[32,1024]{1,0:T(8,128)(2,1)S(1)}, bf16[32,1024]{1,0:T(8,128)(2,1)S(1)}) custom-call(s32[2,8]{1,0:T(2,128)S(1)} %bitcast.7, bf16[32,4096]{1,0:T(8,128)(2,1)S(1)} %get-tuple-element.34.own, bf16[32,4096]{1,0:T(8,128)(2,1)S(1)} %collective-permute-done.8.mate, ...), custom_call_target="tpu_custom_call" | custom-call | tf_op jit(solution)/shard_map/near/pallas_call | solution.py:403
  34.1 1.9 %collective-permute-start.11 = (bf16[32,1024]{1,0:T(8,128)(2,1)S(1)}, bf16[32,1024]{1,0:T(8,128)(2,1)S(1)}, u32[]{:S(2)}, u32[]{:S(2)}) collective-permute-start(bf16[32,1024]{1,0:T(8,128)(2,1)S(1)} %get-tuple-element.40), channel_id=1, source_target_pairs={{0,2},{1,3},{2,0},{3,1},{4,6},{5,7},{6,4},{7,5},{8,10},{9,11},{10,... | collective-permute-start | bytes 196616 | tf_op jit(solution)/shard_map/ppermute | solution.py:40
  36.1 2.2 %collective-permute-start.12 = (bf16[32,1024]{1,0:T(8,128)(2,1)S(1)}, bf16[32,1024]{1,0:T(8,128)(2,1)S(1)}, u32[]{:S(2)}, u32[]{:S(2)}) collective-permute-start(bf16[32,1024]{1,0:T(8,128)(2,1)S(1)} %get-tuple-element.41), channel_id=1, source_target_pairs={{0,3},{1,2},{2,1},{3,0},{4,7},{5,6},{6,5},{7,4},{8,11},{9,10},{10,... | collective-permute-start | bytes 196616 | tf_op jit(solution)/shard_map/ppermute | solution.py:40
  38.5 0.3 collective-permute-start.10
  38.9 0.8 %settle.1 = (f32[32,512]{1,0:T(8,128)S(1)}, f32[512,64]{1,0:T(8,128)S(1)}) custom-call(f32[32,64]{1,0:T(8,128)S(1)} %get-tuple-element.36.refs_0_, f32[32,64]{1,0:T(8,128)S(1)} %collective-permute-done.1.other.refs_1_, f32[32,64]{1,0:T(8,128)S(1)} %collective-permute-done.2.other.refs_2_, f32[32,64]{1,0:T(8,128)S(1)} %collective-permute-done.4.other.refs_3_, ...), custom_call_target="tpu_custom_call" | custom-call | tf_op jit(solution)/shard_map/settle/pallas_call | solution.py:428
  39.6 1.8 %collective-permute-done.10.other = f32[32,64]{1,0:T(8,128)S(1)} collective-permute-done((f32[32,64]{1,0:T(8,128)S(1)}, f32[32,64]{1,0:T(8,128)S(1)}, u32[]{:S(2)}, u32[]{:S(2)}) %collective-permute-start.10) | collective-permute-done | bytes 8224 | tf_op jit(solution)/shard_map/ppermute | solution.py:40
  41.4 0.6 %collective-permute-done.12.rest_2_ = bf16[32,1024]{1,0:T(8,128)(2,1)S(1)} collective-permute-done((bf16[32,1024]{1,0:T(8,128)(2,1)S(1)}, bf16[32,1024]{1,0:T(8,128)(2,1)S(1)}, u32[]{:S(2)}, u32[]{:S(2)}) %collective-permute-start.12) | collective-permute-done | bytes 65568 | tf_op jit(solution)/shard_map/ppermute | solution.py:40
  42.1 1.3 %last.1 = f32[32,4096]{1,0:T(8,128)} custom-call(f32[32,64]{1,0:T(8,128)S(1)} %collective-permute-done.10.other, f32[512,64]{1,0:T(8,128)S(1)} %get-tuple-element.38.final, f32[32,512]{1,0:T(8,128)S(1)} %get-tuple-element.39.local, bf16[64,4096]{1,0:T(8,128)(2,1)S(1)} %copy-done.2, f32[32,1024]{1,0:T(8,128)S(1)} %get-tuple-element.35.rest_0_, ...), custom_call_target="tpu_custom_call" | custom-call | tf_op jit(solution)/shard_map/last/pallas_call | solution.py:469
  (28 shorter events, 1.1 us)
Async XLA Ops:
  2.3 4.0 %collective-permute-start = (bf16[32,1152]{1,0:T(8,128)(2,1)S(1)}, bf16[32,1152]{1,0:T(8,128)(2,1)S(1)}, u32[]{:S(2)}, u32[]{:S(2)}) collective-permute-start(bf16[32,1152]{1,0:T(8,128)(2,1)S(1)} %get-tuple-element.25), channel_id=1, source_target_pairs={{0,4},{4,0},{8,12},{12,8},{16,20},{20,16},{24,28},{28,24},{32,36},... | collective-permute-start | bytes 221192 | tf_op jit(solution)/shard_map/ppermute | solution.py:40
  4.5 12.7 %collective-permute-start.3 = (bf16[32,1024]{1,0:T(8,128)(2,1)S(1)}, bf16[32,1024]{1,0:T(8,128)(2,1)S(1)}, u32[]{:S(2)}, u32[]{:S(2)}) collective-permute-start(bf16[32,1024]{1,0:T(8,128)(2,1)S(1)} %get-tuple-element.32), channel_id=1, source_target_pairs={{4,8},{12,16},{20,24},{28,32},{36,40},{44,48},{52,56},{60,64},{68,... | collective-permute-start | bytes 196616 | tf_op jit(solution)/shard_map/ppermute | solution.py:519
  6.3 3.9 %copy-start.4 = (bf16[32,4096]{1,0:T(8,128)(2,1)S(1)}, bf16[32,4096]{1,0:T(8,128)(2,1)}, u32[]{:S(2)}) copy-start(bf16[32,4096]{1,0:T(8,128)(2,1)} %rhs_hbm.1) | copy-start | bytes 786436
  6.5 8.8 %collective-permute-start.1 = (f32[32,64]{1,0:T(8,128)S(1)}, f32[32,64]{1,0:T(8,128)S(1)}, u32[]{:S(2)}, u32[]{:S(2)}) collective-permute-start(f32[32,64]{1,0:T(8,128)S(1)} %get-tuple-element.27.after.current), channel_id=1, source_target_pairs={{0,8},{4,12},{8,0},{12,4},{16,24},{20,28},{24,16},{28,20},{32,40},... | collective-permute-start | bytes 24584 | tf_op jit(solution)/shard_map/ppermute | solution.py:40
  10.1 16.0 %collective-permute-start.5 = (bf16[32,4096]{1,0:T(8,128)(2,1)S(1)}, bf16[32,4096]{1,0:T(8,128)(2,1)S(1)}, u32[]{:S(2)}, u32[]{:S(2)}) collective-permute-start(bf16[32,4096]{1,0:T(8,128)(2,1)S(1)} %copy-done.4), channel_id=1, source_target_pairs={{0,2},{1,3},{2,0},{3,1},{4,6},{5,7},{6,4},{7,5},{8,10},{9,11},{10,... | collective-permute-start | bytes 786440 | tf_op jit(solution)/shard_map/ppermute | solution.py:40
  15.5 3.1 %collective-permute-start.2 = (f32[32,64]{1,0:T(8,128)S(1)}, f32[32,64]{1,0:T(8,128)S(1)}, u32[]{:S(2)}, u32[]{:S(2)}) collective-permute-start(f32[32,64]{1,0:T(8,128)S(1)} %lift.6.refs_2_.current), channel_id=1, source_target_pairs={{0,16},{4,20},{8,24},{12,28},{16,0},{20,4},{24,8},{28,12},{32,48},... | collective-permute-start | bytes 24584 | tf_op jit(solution)/shard_map/ppermute | solution.py:40
  17.2 8.9 %collective-permute-start.6 = (bf16[32,2048]{1,0:T(8,128)(2,1)S(1)}, bf16[32,2048]{1,0:T(8,128)(2,1)S(1)}, u32[]{:S(2)}, u32[]{:S(2)}) collective-permute-start(bf16[32,2048]{1,0:T(8,128)(2,1)S(1)} %join.2.rest_0_.refs_1_.edge), channel_id=1, source_target_pairs={{0,2},{1,3},{2,0},{3,1},{4,6},{5,7},{6,4},{7,5},{8,10},{9,11},{10,... | collective-permute-start | bytes 393224 | tf_op jit(solution)/shard_map/ppermute | solution.py:40
  18.8 7.6 %collective-permute-start.4 = (f32[32,64]{1,0:T(8,128)S(1)}, f32[32,64]{1,0:T(8,128)S(1)}, u32[]{:S(2)}, u32[]{:S(2)}) collective-permute-start(f32[32,64]{1,0:T(8,128)S(1)} %lift.7.refs_3_.after.current), channel_id=1, source_target_pairs={{0,32},{4,36},{8,40},{12,44},{16,48},{20,52},{24,56},{28,60},{32,0... | collective-permute-start | bytes 24584 | tf_op jit(solution)/shard_map/ppermute | solution.py:40
  21.8 10.7 %collective-permute-start.8 = (bf16[32,4096]{1,0:T(8,128)(2,1)S(1)}, bf16[32,4096]{1,0:T(8,128)(2,1)S(1)}, u32[]{:S(2)}, u32[]{:S(2)}) collective-permute-start(bf16[32,4096]{1,0:T(8,128)(2,1)S(1)} %copy-done.4), channel_id=1, source_target_pairs={{0,1},{1,0},{2,3},{3,2},{4,5},{5,4},{6,7},{7,6},{8,9},{9,8},{10,11... | collective-permute-start | bytes 786440 | tf_op jit(solution)/shard_map/ppermute | solution.py:40
  26.3 6.2 %copy-start = (bf16[8,2,128,512]{3,2,1,0:T(8,128)(2,1)S(1)}, bf16[8,2,128,512]{3,2,1,0:T(8,128)(2,1)}, u32[]{:S(2)}) copy-start(bf16[8,2,128,512]{3,2,1,0:T(8,128)(2,1)} %near.3) | copy-start | bytes 6291460
  26.3 6.2 %copy-start.1 = (bf16[8,128,512]{2,1,0:T(8,128)(2,1)S(1)}, bf16[8,128,512]{2,1,0:T(8,128)(2,1)}, u32[]{:S(2)}) copy-start(bf16[8,128,512]{2,1,0:T(8,128)(2,1)} %diag.1) | copy-start | bytes 3145732
  26.3 6.2 %copy-start.3 = (s32[8,2]{0,1:T(2,128)S(1)}, s32[8,2]{0,1:T(2,128)}, u32[]{:S(2)}) copy-start(s32[8,2]{0,1:T(2,128)} %param.23) | copy-start | bytes 196
  26.3 6.1 %collective-permute-start.9 = (bf16[32,8192]{1,0:T(8,128)(2,1)S(1)}, bf16[32,8192]{1,0:T(8,128)(2,1)S(1)}, u32[]{:S(2)}, u32[]{:S(2)}) collective-permute-start(bf16[32,8192]{1,0:T(8,128)(2,1)S(1)} %join.3.rest_0_), channel_id=1, source_target_pairs={{0,1},{1,0},{2,3},{3,2},{4,5},{5,4},{6,7},{7,6},{8,9},{9,8},{10,11... | collective-permute-start | bytes 1572872 | tf_op jit(solution)/shard_map/ppermute | solution.py:40
  26.6 11.7 %collective-permute-start.7 = (f32[32,64]{1,0:T(8,128)S(1)}, f32[32,64]{1,0:T(8,128)S(1)}, u32[]{:S(2)}, u32[]{:S(2)}) collective-permute-start(f32[32,64]{1,0:T(8,128)S(1)} %lift.8.after.current), channel_id=1, source_target_pairs={{0,64},{4,68},{8,72},{12,76},{16,80},{20,84},{24,88},{28,92},{32,9... | collective-permute-start | bytes 24584 | tf_op jit(solution)/shard_map/ppermute | solution.py:40
  34.1 7.3 %collective-permute-start.11 = (bf16[32,1024]{1,0:T(8,128)(2,1)S(1)}, bf16[32,1024]{1,0:T(8,128)(2,1)S(1)}, u32[]{:S(2)}, u32[]{:S(2)}) collective-permute-start(bf16[32,1024]{1,0:T(8,128)(2,1)S(1)} %get-tuple-element.40), channel_id=1, source_target_pairs={{0,2},{1,3},{2,0},{3,1},{4,6},{5,7},{6,4},{7,5},{8,10},{9,11},{10,... | collective-permute-start | bytes 196616 | tf_op jit(solution)/shard_map/ppermute | solution.py:40
  36.1 6.0 %collective-permute-start.12 = (bf16[32,1024]{1,0:T(8,128)(2,1)S(1)}, bf16[32,1024]{1,0:T(8,128)(2,1)S(1)}, u32[]{:S(2)}, u32[]{:S(2)}) collective-permute-start(bf16[32,1024]{1,0:T(8,128)(2,1)S(1)} %get-tuple-element.41), channel_id=1, source_target_pairs={{0,3},{1,2},{2,1},{3,0},{4,7},{5,6},{6,5},{7,4},{8,11},{9,10},{10,... | collective-permute-start | bytes 196616 | tf_op jit(solution)/shard_map/ppermute | solution.py:40
  38.3 3.8 %collective-permute-start.13 = (bf16[32,1024]{1,0:T(8,128)(2,1)S(1)}, bf16[32,1024]{1,0:T(8,128)(2,1)S(1)}, u32[]{:S(2)}, u32[]{:S(2)}) collective-permute-start(bf16[32,1024]{1,0:T(8,128)(2,1)S(1)} %get-tuple-element.42), channel_id=1, source_target_pairs={{0,1},{1,0},{2,3},{3,2},{4,5},{5,4},{6,7},{7,6},{8,9},{9,8},{10,11... | collective-permute-start | bytes 196616 | tf_op jit(solution)/shard_map/ppermute | solution.py:40
  38.3 3.7 %copy-start.2 = (bf16[64,4096]{1,0:T(8,128)(2,1)S(1)}, bf16[64,4096]{1,0:T(8,128)(2,1)}, u32[]{:S(2)}) copy-start(bf16[64,4096]{1,0:T(8,128)(2,1)} %basis.1) | copy-start | bytes 1572868
  38.5 2.9 %collective-permute-start.10 = (f32[32,64]{1,0:T(8,128)S(1)}, f32[32,64]{1,0:T(8,128)S(1)}, u32[]{:S(2)}, u32[]{:S(2)}) collective-permute-start(f32[32,64]{1,0:T(8,128)S(1)} %lift.9), channel_id=1, source_target_pairs={{0,128},{4,132},{8,136},{12,140},{16,144},{20,148},{24,152},{28,15... | collective-permute-start | bytes 24584 | tf_op jit(solution)/shard_map/ppermute | solution.py:40

commit v4 on v3

--- a/solution.py
+++ b/solution.py
@@ -76,26 +76,21 @@
     inner_tr,
     sems,
 ):
-    half = rhs.shape[1] // 2
     size = rhs.shape[1] // 8
     wide = 2 * size
-    pairs = []
-    for side in range(2):
-        span = pl.ds(side * half, half)
-        pairs += [(rhs_hbm.at[:, span], rhs.at[:, span]), (cols_hbm.at[:, span], cols.at[:, span])]
-    pairs += [(leaf_hbm, leaf_tr), (inner_hbm, inner_tr), (tree_hbm, tree)]
+    pairs = [(rhs_hbm, rhs), (cols_hbm, cols), (leaf_hbm, leaf_tr), (inner_hbm, inner_tr), (tree_hbm, tree)]
     copies = fetched(pairs, sems)
     parts = []
     for leaf in range(8):
-        if leaf % 4 == 0:
-            copies[leaf // 2].wait()
-            copies[leaf // 2 + 1].wait()
+        if leaf == 0:
+            copies[0].wait()
+            copies[1].wait()
         span = slice(leaf * size, (leaf + 1) * size)
         parts.append(
             lax.dot_general(rhs[:, span], cols[:, span], TURNED, preferred_element_type=F32)
         )
-    copies[4].wait()
-    copies[5].wait()
+    copies[2].wait()
+    copies[3].wait()
     ups = []
     for pair in range(4):
         both = jnp.concatenate(parts[2 * pair : 2 * pair + 2], axis=1)
@@ -115,7 +110,7 @@
     outer_side = pl.multiple_of(odd * (rhs.shape[1] - wide), wide)
     packet[:, 128:] = rhs[:, pl.ds(inner_side, wide)]
     outward[...] = rhs[:, pl.ds(outer_side, wide)]
-    copies[6].wait()
+    copies[4].wait()
 
 
 def run_up(rhs, cols, leaf_tr, inner_tr, tree_tr):
@@ -138,7 +133,7 @@
             pltpu.VMEM((rows, wide), BF16),
         ],
         scratch_shapes=[pltpu.VMEM(x.shape, x.dtype) for x in tables]
-        + [pltpu.SemaphoreType.DMA((7,))],
+        + [pltpu.SemaphoreType.DMA((5,))],
         compiler_params=limit(8),
         cost_estimate=LIGHT,
         name="up",
@@ -265,10 +260,8 @@
     leaf_cp_hbm,
     inner_tr_hbm,
     inner_cp_hbm,
-    tree_hbm,
     local_ref,
     reach_ref,
-    tree,
     leaf_tr,
     leaf_cp,
     inner_tr,
@@ -282,7 +275,6 @@
             (inner_tr_hbm, inner_tr),
             (leaf_cp_hbm, leaf_cp),
             (leaf_tr_hbm, leaf_tr),
-            (tree_hbm, tree),
         ],
         sems,
     )
@@ -292,7 +284,7 @@
         b = dot3(values[:, :64], table[64:], TURNED)
         return jnp.concatenate([a, b], axis=1)
 
-    for copy in copies[:4]:
+    for copy in copies:
         copy.wait()
     tops = coupled(first[...], inner_cp[0])
     mids = []
@@ -309,27 +301,25 @@
         if pair % 2 == 0:
             reach_mid = dot3(inner_tr[1 + side], reach_top[side * 64 : (side + 1) * 64])
         reach_ref[pair * 128 : (pair + 1) * 128, :] = dot3(leaf_tr[pair], reach_mid[low : low + 64])
-    copies[4].wait()
-
-
-def run_prep(coeffs, second, first, leaf_tr, leaf_cp, inner_tr, inner_cp, tree_cp, after):
+
+
+def run_prep(coeffs, second, first, leaf_tr, leaf_cp, inner_tr, inner_cp, after):
     rows = coeffs.shape[0]
     skel = first.shape[1] // 2
     tables = (leaf_tr, leaf_cp, inner_tr, inner_cp)
     return pl.pallas_call(
         prep_kernel,
-        in_specs=[VMEM] * 3 + [ANY] * 6,
-        out_specs=[VMEM] * 3,
+        in_specs=[VMEM] * 3 + [ANY] * 5,
+        out_specs=[VMEM] * 2,
         out_shape=[
             pltpu.VMEM((rows, 8 * skel), F32),
             pltpu.VMEM((8 * skel, skel), F32),
-            pltpu.VMEM(tree_cp.shape, F32),
         ],
-        scratch_shapes=[pltpu.VMEM(x.shape, F32) for x in tables] + [pltpu.SemaphoreType.DMA((5,))],
+        scratch_shapes=[pltpu.VMEM(x.shape, F32) for x in tables] + [pltpu.SemaphoreType.DMA((4,))],
         compiler_params=limit(6),
         cost_estimate=LIGHT,
         name="prep",
-    )(coeffs, second, first, after, *map(in_hbm, (*tables, tree_cp)))
+    )(coeffs, second, first, after, *map(in_hbm, tables))
 
 
 def turn_kernel(depth, mats, tree, after, out, picked):
@@ -525,7 +515,7 @@
         others.append(swapped(current, "leaf", 1 << bit))
         return run_lift(bit, current, others[-1], mats, beside, width)
 
-    local_part, reach, tree = run_prep(
+    local_part, reach = run_prep(
         coeffs,
         second,
         first,
@@ -533,14 +523,13 @@
         leaf_cp,
         inner_tr,
         inner_cp,
-        jnp.transpose(tree_coupling, (1, 2, 0)),
         current,
     )
     current = step(current, [reach])
     edge = run_join([(packet, 2 * skel, wide), (outward, 0, wide)], [current])
     edge_far = swapped(edge, "rhs", 2)
     current = step(current, [edge])
-    turn = run_turn(depth, mats, tree, current)
+    turn = run_turn(depth, mats, jnp.transpose(tree_coupling, (1, 2, 0)), current)
     joined = run_join(
         [(far, 0, width), (edge, 0, 2 * wide), (edge_far, 0, 2 * wide)], [current]
     )
@@ -550,7 +539,7 @@
         near_leaves.T, own, mate, far, edge, edge_far, relay, diag_blocks, near_blocks, current
     )
     current = step(current, close[:1])
-    close = {k: swapped(close[k], "rhs", k) if k else close[0] for k in (0, 2, 3, 1)}
+    close = {k: swapped(close[k], "rhs", k) if k else close[0] for k in (0, 3, 2, 1)}
     leaf_part, final = run_settle(others, turn, reach, local_part)
     other = swapped(current, "leaf", 1 << len(others))
     return run_last(other, final, leaf_part, row_basis, close)

time: 43.5 us -> 42.7 us (0.982)
  waiting for transfers between devices: 3.28 us -> 2.77 us
    ppermute x13, waiting for transfers between devices: 3.28 us -> 2.77 us  [swapped(): return lax.ppermute(x, axis, [(i, i ^ bit) for i in range(count)])]
where the time goes in v4:
time: 42.7 us; the launch traced here: 42.5 us
  starting transfers between devices  27.7 us (65%)
  Pallas kernels  11.8 us (28%)
  waiting for transfers between devices  2.77 us (6%)
    ppermute x13, starting transfers between devices, swapped(): return lax.ppermute(x, axis, [(i, i ^ bit) for i in range(count)])  27.1 us
    ppermute x13, waiting for transfers between devices, swapped(): return lax.ppermute(x, axis, [(i, i ^ bit) for i in range(count)])  2.77 us
    pallas_call x1, Pallas kernels, run_prep(): pl.pallas_call(prep_kernel, in_specs=[VMEM] * 3 + [ANY] * 5, out_specs=[V...  2.41 us
    pallas_call x1, Pallas kernels, run_up(): pl.pallas_call(up_kernel, in_specs=[ANY] * 5, out_specs=[VMEM] * 8, out_s...  2.25 us
    pallas_call x1, Pallas kernels, run_near(): pl.pallas_call(near_kernel, in_specs=[pl.BlockSpec(memory_space=pltpu.SME...  1.66 us
    pallas_call x1, Pallas kernels, run_turn(): pl.pallas_call(functools.partial(turn_kernel, depth), in_specs=[VMEM] * 2...  1.48 us
    pallas_call x1, Pallas kernels, run_last(): pl.pallas_call(functools.partial(last_kernel, groups), in_specs=[VMEM] *...  1.3 us
  transfers between devices with their start and end apart: 14, of which 4 were waited for; matrix products, arithmetic and copies ran while one was open for 0% of the time, Pallas kernels for 19%

profile of v4, /device:TPU:1, one launch (start us, length us, event | category | flops | bytes accessed | tf_op | source)
XLA Modules:
  0.0 42.5 jit_solution(9501589443636743309)
XLA Ops:
  0.0 2.3 %up.1 = (bf16[32,4096]{1,0:T(8,128)(2,1)S(1)}, f32[64,64,126]{2,1,0:T(8,128)S(1)}, f32[32,512]{1,0:T(8,128)S(1)}, f32[32,256]{1,0:T(8,128)S(1)}, f32[32,128]{1,0...) custom-call(bf16[32,4096]{1,0:T(8,128)(2,1)} %rhs_hbm.1, ...), custom_call_target="tpu_custom_call" | custom-call | tf_op jit(solution)/shard_map/up/pallas_call | solution.py:121
  2.3 2.2 %collective-permute-start = (bf16[32,1152]{1,0:T(8,128)(2,1)S(1)}, bf16[32,1152]{1,0:T(8,128)(2,1)S(1)}, u32[]{:S(2)}, u32[]{:S(2)}) collective-permute-start(bf16[32,1152]{1,0:T(8,128)(2,1)S(1)} %get-tuple-element.24), channel_id=1, source_target_pairs={{0,4},{4,0},{8,12},{12,8},{16,20},{20,16},{24,28},{28,24},{32,36},... | collective-permute-start | bytes 221192 | tf_op jit(solution)/shard_map/ppermute | solution.py:40
  4.5 0.7 %collective-permute-start.3 = (bf16[32,1024]{1,0:T(8,128)(2,1)S(1)}, bf16[32,1024]{1,0:T(8,128)(2,1)S(1)}, u32[]{:S(2)}, u32[]{:S(2)}) collective-permute-start(bf16[32,1024]{1,0:T(8,128)(2,1)S(1)} %get-tuple-element.31), channel_id=1, source_target_pairs={{4,8},{12,16},{20,24},{28,32},{36,40},{44,48},{52,56},{60,64},{68,... | collective-permute-start | bytes 196616 | tf_op jit(solution)/shard_map/ppermute | solution.py:509
  5.1 0.8 %pick.1.mats = f32[5,128,64]{2,1,0:T(8,128)S(1)} custom-call(f32[64,64,126]{2,1,0:T(8,128)S(1)} %get-tuple-element.25.tree), custom_call_target="tpu_custom_call" | custom-call | tf_op jit(solution)/shard_map/pick/pallas_call | solution.py:201
  5.9 0.3 collective-permute-done.packet.refs_0_
  6.2 0.3 lift.5
  6.5 3.6 %collective-permute-start.1 = (f32[32,64]{1,0:T(8,128)S(1)}, f32[32,64]{1,0:T(8,128)S(1)}, u32[]{:S(2)}, u32[]{:S(2)}) collective-permute-start(f32[32,64]{1,0:T(8,128)S(1)} %get-tuple-element.26.after.current), channel_id=1, source_target_pairs={{0,8},{4,12},{8,0},{12,4},{16,24},{20,28},{24,16},{28,20},{32,40},... | collective-permute-start | bytes 24584 | tf_op jit(solution)/shard_map/ppermute | solution.py:40
  10.1 2.7 %collective-permute-start.5 = (bf16[32,4096]{1,0:T(8,128)(2,1)S(1)}, bf16[32,4096]{1,0:T(8,128)(2,1)S(1)}, u32[]{:S(2)}, u32[]{:S(2)}) collective-permute-start(bf16[32,4096]{1,0:T(8,128)(2,1)S(1)} %copy-done.5), channel_id=1, source_target_pairs={{0,2},{1,3},{2,0},{3,1},{4,6},{5,7},{6,4},{7,5},{8,10},{9,11},{10,... | collective-permute-start | bytes 786440 | tf_op jit(solution)/shard_map/ppermute | solution.py:40
  12.8 2.4 %prep.1 = (f32[32,512]{1,0:T(8,128)S(1)}, f32[512,64]{1,0:T(8,128)S(1)}) custom-call(f32[32,512]{1,0:T(8,128)S(1)} %get-tuple-element.27.coeffs, f32[32,256]{1,0:T(8,128)S(1)} %get-tuple-element.28.second, f32[32,128]{1,0:T(8,128)S(1)} %get-tuple-element.29.first, f32[32,64]{1,0:T(8,128)S(1)} %get-tuple-element.26.after.current, f32[4,128,64]{2,1,0:T(8,128)} %bitcast.11, ...), custom_call_target="tpu_custom_call" | custom-call | tf_op jit(solution)/shard_map/prep/pallas_call | solution.py:310
  15.5 1.7 %collective-permute-start.2 = (f32[32,64]{1,0:T(8,128)S(1)}, f32[32,64]{1,0:T(8,128)S(1)}, u32[]{:S(2)}, u32[]{:S(2)}) collective-permute-start(f32[32,64]{1,0:T(8,128)S(1)} %lift.6.refs_2_.current), channel_id=1, source_target_pairs={{0,16},{4,20},{8,24},{12,28},{16,0},{20,4},{24,8},{28,12},{32,48},... | collective-permute-start | bytes 24584 | tf_op jit(solution)/shard_map/ppermute | solution.py:40
  17.2 0.9 %collective-permute-start.6 = (bf16[32,2048]{1,0:T(8,128)(2,1)S(1)}, bf16[32,2048]{1,0:T(8,128)(2,1)S(1)}, u32[]{:S(2)}, u32[]{:S(2)}) collective-permute-start(bf16[32,2048]{1,0:T(8,128)(2,1)S(1)} %join.2.rest_0_.refs_1_.edge), channel_id=1, source_target_pairs={{0,2},{1,3},{2,0},{3,1},{4,6},{5,7},{6,4},{7,5},{8,10},{9,11},{10,... | collective-permute-start | bytes 393224 | tf_op jit(solution)/shard_map/ppermute | solution.py:40
  18.0 0.5 %collective-permute-done.2.other.refs_2_ = f32[32,64]{1,0:T(8,128)S(1)} collective-permute-done((f32[32,64]{1,0:T(8,128)S(1)}, f32[32,64]{1,0:T(8,128)S(1)}, u32[]{:S(2)}, u32[]{:S(2)}) %collective-permute-start.2) | collective-permute-done | bytes 8224 | tf_op jit(solution)/shard_map/ppermute | solution.py:40
  18.7 3.0 %collective-permute-start.4 = (f32[32,64]{1,0:T(8,128)S(1)}, f32[32,64]{1,0:T(8,128)S(1)}, u32[]{:S(2)}, u32[]{:S(2)}) collective-permute-start(f32[32,64]{1,0:T(8,128)S(1)} %lift.7.refs_3_.after.current), channel_id=1, source_target_pairs={{0,32},{4,36},{8,40},{12,44},{16,48},{20,52},{24,56},{28,60},{32,0... | collective-permute-start | bytes 24584 | tf_op jit(solution)/shard_map/ppermute | solution.py:40
  21.7 2.8 %collective-permute-start.8 = (bf16[32,4096]{1,0:T(8,128)(2,1)S(1)}, bf16[32,4096]{1,0:T(8,128)(2,1)S(1)}, u32[]{:S(2)}, u32[]{:S(2)}) collective-permute-start(bf16[32,4096]{1,0:T(8,128)(2,1)S(1)} %copy-done.5), channel_id=1, source_target_pairs={{0,1},{1,0},{2,3},{3,2},{4,5},{5,4},{6,7},{7,6},{8,9},{9,8},{10,11... | collective-permute-start | bytes 786440 | tf_op jit(solution)/shard_map/ppermute | solution.py:40
  24.6 1.5 %turn.1.rest_1_.refs_5_ = f32[6,64,64]{2,1,0:T(8,128)S(1)} custom-call(f32[5,128,64]{2,1,0:T(8,128)S(1)} %pick.1.mats, f32[64,64,126]{2,1,0:T(8,128)S(1)} %bitcast.7, f32[32,64]{1,0:T(8,128)S(1)} %lift.7.refs_3_.after.current), custom_call_target="tpu_custom_call" | custom-call | tf_op jit(solution)/shard_map/turn/pallas_call | solution.py:341
  26.6 5.8 %collective-permute-start.7 = (f32[32,64]{1,0:T(8,128)S(1)}, f32[32,64]{1,0:T(8,128)S(1)}, u32[]{:S(2)}, u32[]{:S(2)}) collective-permute-start(f32[32,64]{1,0:T(8,128)S(1)} %lift.8.after.current), channel_id=1, source_target_pairs={{0,64},{4,68},{8,72},{12,76},{16,80},{20,84},{24,88},{28,92},{32,9... | collective-permute-start | bytes 24584 | tf_op jit(solution)/shard_map/ppermute | solution.py:40
  32.4 1.7 %near.2 = (f32[32,1024]{1,0:T(8,128)S(1)}, bf16[32,1024]{1,0:T(8,128)(2,1)S(1)}, bf16[32,1024]{1,0:T(8,128)(2,1)S(1)}, bf16[32,1024]{1,0:T(8,128)(2,1)S(1)}) custom-call(s32[2,8]{1,0:T(2,128)S(1)} %bitcast.8, bf16[32,4096]{1,0:T(8,128)(2,1)S(1)} %get-tuple-element.32.own, bf16[32,4096]{1,0:T(8,128)(2,1)S(1)} %collective-permute-done.8.mate, ...), custom_call_target="tpu_custom_call" | custom-call | tf_op jit(solution)/shard_map/near/pallas_call | solution.py:393
  34.1 2.1 %collective-permute-start.11 = (bf16[32,1024]{1,0:T(8,128)(2,1)S(1)}, bf16[32,1024]{1,0:T(8,128)(2,1)S(1)}, u32[]{:S(2)}, u32[]{:S(2)}) collective-permute-start(bf16[32,1024]{1,0:T(8,128)(2,1)S(1)} %get-tuple-element.38), channel_id=1, source_target_pairs={{0,3},{1,2},{2,1},{3,0},{4,7},{5,6},{6,5},{7,4},{8,11},{9,10},{10,... | collective-permute-start | bytes 196616 | tf_op jit(solution)/shard_map/ppermute | solution.py:40
  36.2 1.7 %collective-permute-start.12 = (bf16[32,1024]{1,0:T(8,128)(2,1)S(1)}, bf16[32,1024]{1,0:T(8,128)(2,1)S(1)}, u32[]{:S(2)}, u32[]{:S(2)}) collective-permute-start(bf16[32,1024]{1,0:T(8,128)(2,1)S(1)} %get-tuple-element.39), channel_id=1, source_target_pairs={{0,2},{1,3},{2,0},{3,1},{4,6},{5,7},{6,4},{7,5},{8,10},{9,11},{10,... | collective-permute-start | bytes 196616 | tf_op jit(solution)/shard_map/ppermute | solution.py:40
  38.0 0.2 lift.9
  38.2 0.3 collective-permute-start.10
  38.5 0.8 %settle.1 = (f32[32,512]{1,0:T(8,128)S(1)}, f32[512,64]{1,0:T(8,128)S(1)}) custom-call(f32[32,64]{1,0:T(8,128)S(1)} %get-tuple-element.34.refs_0_, f32[32,64]{1,0:T(8,128)S(1)} %collective-permute-done.1.other.refs_1_, f32[32,64]{1,0:T(8,128)S(1)} %collective-permute-done.2.other.refs_2_, f32[32,64]{1,0:T(8,128)S(1)} %collective-permute-done.4.other.refs_3_, ...), custom_call_target="tpu_custom_call" | custom-call | tf_op jit(solution)/shard_map/settle/pallas_call | solution.py:418
  39.3 1.8 %collective-permute-done.10.other = f32[32,64]{1,0:T(8,128)S(1)} collective-permute-done((f32[32,64]{1,0:T(8,128)S(1)}, f32[32,64]{1,0:T(8,128)S(1)}, u32[]{:S(2)}, u32[]{:S(2)}) %collective-permute-start.10) | collective-permute-done | bytes 8224 | tf_op jit(solution)/shard_map/ppermute | solution.py:40
  41.2 1.3 %last.1 = f32[32,4096]{1,0:T(8,128)} custom-call(f32[32,64]{1,0:T(8,128)S(1)} %collective-permute-done.10.other, f32[512,64]{1,0:T(8,128)S(1)} %get-tuple-element.36.final, f32[32,512]{1,0:T(8,128)S(1)} %get-tuple-element.37.local, bf16[64,4096]{1,0:T(8,128)(2,1)S(1)} %copy-done.3, f32[32,1024]{1,0:T(8,128)S(1)} %get-tuple-element.33.rest_0_, ...), custom_call_target="tpu_custom_call" | custom-call | tf_op jit(solution)/shard_map/last/pallas_call | solution.py:459
  (30 shorter events, 1.0 us)
Async XLA Ops:
  2.3 4.0 %collective-permute-start = (bf16[32,1152]{1,0:T(8,128)(2,1)S(1)}, bf16[32,1152]{1,0:T(8,128)(2,1)S(1)}, u32[]{:S(2)}, u32[]{:S(2)}) collective-permute-start(bf16[32,1152]{1,0:T(8,128)(2,1)S(1)} %get-tuple-element.24), channel_id=1, source_target_pairs={{0,4},{4,0},{8,12},{12,8},{16,20},{20,16},{24,28},{28,24},{32,36},... | collective-permute-start | bytes 221192 | tf_op jit(solution)/shard_map/ppermute | solution.py:40
  4.5 12.6 %collective-permute-start.3 = (bf16[32,1024]{1,0:T(8,128)(2,1)S(1)}, bf16[32,1024]{1,0:T(8,128)(2,1)S(1)}, u32[]{:S(2)}, u32[]{:S(2)}) collective-permute-start(bf16[32,1024]{1,0:T(8,128)(2,1)S(1)} %get-tuple-element.31), channel_id=1, source_target_pairs={{4,8},{12,16},{20,24},{28,32},{36,40},{44,48},{52,56},{60,64},{68,... | collective-permute-start | bytes 196616 | tf_op jit(solution)/shard_map/ppermute | solution.py:509
  6.2 3.9 %copy-start.5 = (bf16[32,4096]{1,0:T(8,128)(2,1)S(1)}, bf16[32,4096]{1,0:T(8,128)(2,1)}, u32[]{:S(2)}) copy-start(bf16[32,4096]{1,0:T(8,128)(2,1)} %rhs_hbm.1) | copy-start | bytes 786436
  6.5 8.8 %collective-permute-start.1 = (f32[32,64]{1,0:T(8,128)S(1)}, f32[32,64]{1,0:T(8,128)S(1)}, u32[]{:S(2)}, u32[]{:S(2)}) collective-permute-start(f32[32,64]{1,0:T(8,128)S(1)} %get-tuple-element.26.after.current), channel_id=1, source_target_pairs={{0,8},{4,12},{8,0},{12,4},{16,24},{20,28},{24,16},{28,20},{32,40},... | collective-permute-start | bytes 24584 | tf_op jit(solution)/shard_map/ppermute | solution.py:40
  10.1 16.0 %collective-permute-start.5 = (bf16[32,4096]{1,0:T(8,128)(2,1)S(1)}, bf16[32,4096]{1,0:T(8,128)(2,1)S(1)}, u32[]{:S(2)}, u32[]{:S(2)}) collective-permute-start(bf16[32,4096]{1,0:T(8,128)(2,1)S(1)} %copy-done.5), channel_id=1, source_target_pairs={{0,2},{1,3},{2,0},{3,1},{4,6},{5,7},{6,4},{7,5},{8,10},{9,11},{10,... | collective-permute-start | bytes 786440 | tf_op jit(solution)/shard_map/ppermute | solution.py:40
  15.5 3.1 %collective-permute-start.2 = (f32[32,64]{1,0:T(8,128)S(1)}, f32[32,64]{1,0:T(8,128)S(1)}, u32[]{:S(2)}, u32[]{:S(2)}) collective-permute-start(f32[32,64]{1,0:T(8,128)S(1)} %lift.6.refs_2_.current), channel_id=1, source_target_pairs={{0,16},{4,20},{8,24},{12,28},{16,0},{20,4},{24,8},{28,12},{32,48},... | collective-permute-start | bytes 24584 | tf_op jit(solution)/shard_map/ppermute | solution.py:40
  17.2 7.4 %copy-start = (f32[126,64,64]{0,2,1:T(8,128)S(1)}, f32[126,64,64]{0,2,1:T(8,128)}, u32[]{:S(2)}) copy-start(f32[126,64,64]{0,2,1:T(8,128)} %param.20) | copy-start | bytes 6193156
  17.2 8.9 %collective-permute-start.6 = (bf16[32,2048]{1,0:T(8,128)(2,1)S(1)}, bf16[32,2048]{1,0:T(8,128)(2,1)S(1)}, u32[]{:S(2)}, u32[]{:S(2)}) collective-permute-start(bf16[32,2048]{1,0:T(8,128)(2,1)S(1)} %join.2.rest_0_.refs_1_.edge), channel_id=1, source_target_pairs={{0,2},{1,3},{2,0},{3,1},{4,6},{5,7},{6,4},{7,5},{8,10},{9,11},{10,... | collective-permute-start | bytes 393224 | tf_op jit(solution)/shard_map/ppermute | solution.py:40
  18.7 7.6 %collective-permute-start.4 = (f32[32,64]{1,0:T(8,128)S(1)}, f32[32,64]{1,0:T(8,128)S(1)}, u32[]{:S(2)}, u32[]{:S(2)}) collective-permute-start(f32[32,64]{1,0:T(8,128)S(1)} %lift.7.refs_3_.after.current), channel_id=1, source_target_pairs={{0,32},{4,36},{8,40},{12,44},{16,48},{20,52},{24,56},{28,60},{32,0... | collective-permute-start | bytes 24584 | tf_op jit(solution)/shard_map/ppermute | solution.py:40
  21.7 10.7 %collective-permute-start.8 = (bf16[32,4096]{1,0:T(8,128)(2,1)S(1)}, bf16[32,4096]{1,0:T(8,128)(2,1)S(1)}, u32[]{:S(2)}, u32[]{:S(2)}) collective-permute-start(bf16[32,4096]{1,0:T(8,128)(2,1)S(1)} %copy-done.5), channel_id=1, source_target_pairs={{0,1},{1,0},{2,3},{3,2},{4,5},{5,4},{6,7},{7,6},{8,9},{9,8},{10,11... | collective-permute-start | bytes 786440 | tf_op jit(solution)/shard_map/ppermute | solution.py:40
  26.2 6.2 %copy-start.1 = (bf16[8,2,128,512]{3,2,1,0:T(8,128)(2,1)S(1)}, bf16[8,2,128,512]{3,2,1,0:T(8,128)(2,1)}, u32[]{:S(2)}) copy-start(bf16[8,2,128,512]{3,2,1,0:T(8,128)(2,1)} %near.3) | copy-start | bytes 6291460
  26.2 6.2 %copy-start.2 = (bf16[8,128,512]{2,1,0:T(8,128)(2,1)S(1)}, bf16[8,128,512]{2,1,0:T(8,128)(2,1)}, u32[]{:S(2)}) copy-start(bf16[8,128,512]{2,1,0:T(8,128)(2,1)} %diag.1) | copy-start | bytes 3145732
  26.2 6.2 %copy-start.4 = (s32[8,2]{0,1:T(2,128)S(1)}, s32[8,2]{0,1:T(2,128)}, u32[]{:S(2)}) copy-start(s32[8,2]{0,1:T(2,128)} %param.23) | copy-start | bytes 196
  26.3 6.1 %collective-permute-start.9 = (bf16[32,8192]{1,0:T(8,128)(2,1)S(1)}, bf16[32,8192]{1,0:T(8,128)(2,1)S(1)}, u32[]{:S(2)}, u32[]{:S(2)}) collective-permute-start(bf16[32,8192]{1,0:T(8,128)(2,1)S(1)} %join.3.rest_0_), channel_id=1, source_target_pairs={{0,1},{1,0},{2,3},{3,2},{4,5},{5,4},{6,7},{7,6},{8,9},{9,8},{10,11... | collective-permute-start | bytes 1572872 | tf_op jit(solution)/shard_map/ppermute | solution.py:40
  26.6 11.4 %collective-permute-start.7 = (f32[32,64]{1,0:T(8,128)S(1)}, f32[32,64]{1,0:T(8,128)S(1)}, u32[]{:S(2)}, u32[]{:S(2)}) collective-permute-start(f32[32,64]{1,0:T(8,128)S(1)} %lift.8.after.current), channel_id=1, source_target_pairs={{0,64},{4,68},{8,72},{12,76},{16,80},{20,84},{24,88},{28,92},{32,9... | collective-permute-start | bytes 24584 | tf_op jit(solution)/shard_map/ppermute | solution.py:40
  34.1 7.0 %collective-permute-start.11 = (bf16[32,1024]{1,0:T(8,128)(2,1)S(1)}, bf16[32,1024]{1,0:T(8,128)(2,1)S(1)}, u32[]{:S(2)}, u32[]{:S(2)}) collective-permute-start(bf16[32,1024]{1,0:T(8,128)(2,1)S(1)} %get-tuple-element.38), channel_id=1, source_target_pairs={{0,3},{1,2},{2,1},{3,0},{4,7},{5,6},{6,5},{7,4},{8,11},{9,10},{10,... | collective-permute-start | bytes 196616 | tf_op jit(solution)/shard_map/ppermute | solution.py:40
  36.2 5.0 %collective-permute-start.12 = (bf16[32,1024]{1,0:T(8,128)(2,1)S(1)}, bf16[32,1024]{1,0:T(8,128)(2,1)S(1)}, u32[]{:S(2)}, u32[]{:S(2)}) collective-permute-start(bf16[32,1024]{1,0:T(8,128)(2,1)S(1)} %get-tuple-element.39), channel_id=1, source_target_pairs={{0,2},{1,3},{2,0},{3,1},{4,6},{5,7},{6,4},{7,5},{8,10},{9,11},{10,... | collective-permute-start | bytes 196616 | tf_op jit(solution)/shard_map/ppermute | solution.py:40
  38.0 3.3 %collective-permute-start.13 = (bf16[32,1024]{1,0:T(8,128)(2,1)S(1)}, bf16[32,1024]{1,0:T(8,128)(2,1)S(1)}, u32[]{:S(2)}, u32[]{:S(2)}) collective-permute-start(bf16[32,1024]{1,0:T(8,128)(2,1)S(1)} %get-tuple-element.40), channel_id=1, source_target_pairs={{0,1},{1,0},{2,3},{3,2},{4,5},{5,4},{6,7},{7,6},{8,9},{9,8},{10,11... | collective-permute-start | bytes 196616 | tf_op jit(solution)/shard_map/ppermute | solution.py:40
  38.0 3.3 %copy-start.3 = (bf16[64,4096]{1,0:T(8,128)(2,1)S(1)}, bf16[64,4096]{1,0:T(8,128)(2,1)}, u32[]{:S(2)}) copy-start(bf16[64,4096]{1,0:T(8,128)(2,1)} %basis.1) | copy-start | bytes 1572868
  38.2 2.9 %collective-permute-start.10 = (f32[32,64]{1,0:T(8,128)S(1)}, f32[32,64]{1,0:T(8,128)S(1)}, u32[]{:S(2)}, u32[]{:S(2)}) collective-permute-start(f32[32,64]{1,0:T(8,128)S(1)} %lift.9), channel_id=1, source_target_pairs={{0,128},{4,132},{8,136},{12,140},{16,144},{20,148},{24,152},{28,15... | collective-permute-start | bytes 24584 | tf_op jit(solution)/shard_map/ppermute | solution.py:40

commit v5 on v4

--- a/solution.py
+++ b/solution.py
@@ -280,9 +280,9 @@
     )
 
     def coupled(values, table):
-        a = dot3(values[:, 64:], table[:64], TURNED)
-        b = dot3(values[:, :64], table[64:], TURNED)
-        return jnp.concatenate([a, b], axis=1)
+        rows = values.shape[0]
+        both = dot3(jnp.concatenate([values[:, 64:], values[:, :64]], axis=0), table, TURNED)
+        return jnp.concatenate([both[:rows, :64], both[rows:, 64:]], axis=1)
 
     for copy in copies:
         copy.wait()

time: 42.7 us -> 42.7 us (level)
  transfers between devices with their start and end apart: 14 -> 14, of which waited for: 4 -> 3; matrix products, arithmetic and copies ran while one was open for 0% -> 0% of each run, Pallas kernels for 19% -> 20%
where the time goes in v5:
time: 42.7 us; the launch traced here: 42.5 us
  starting transfers between devices  27.6 us (65%)
  Pallas kernels  11.9 us (28%)
  waiting for transfers between devices  2.73 us (6%)
    ppermute x13, starting transfers between devices, swapped(): return lax.ppermute(x, axis, [(i, i ^ bit) for i in range(count)])  27 us
    ppermute x13, waiting for transfers between devices, swapped(): return lax.ppermute(x, axis, [(i, i ^ bit) for i in range(count)])  2.73 us
    pallas_call x1, Pallas kernels, run_prep(): pl.pallas_call(prep_kernel, in_specs=[VMEM] * 3 + [ANY] * 5, out_specs=[V...  2.5 us
    pallas_call x1, Pallas kernels, run_up(): pl.pallas_call(up_kernel, in_specs=[ANY] * 5, out_specs=[VMEM] * 8, out_s...  2.25 us
    pallas_call x1, Pallas kernels, run_near(): pl.pallas_call(near_kernel, in_specs=[pl.BlockSpec(memory_space=pltpu.SME...  1.66 us
    pallas_call x1, Pallas kernels, run_turn(): pl.pallas_call(functools.partial(turn_kernel, depth), in_specs=[VMEM] * 2...  1.48 us
    pallas_call x1, Pallas kernels, run_last(): pl.pallas_call(functools.partial(last_kernel, groups), in_specs=[VMEM] *...  1.3 us
  transfers between devices with their start and end apart: 14, of which 3 were waited for; matrix products, arithmetic and copies ran while one was open for 0% of the time, Pallas kernels for 20%

profile of v5, /device:TPU:1, one launch (start us, length us, event | category | flops | bytes accessed | tf_op | source)
XLA Modules:
  0.0 42.5 jit_solution(13009651936838363223)
XLA Ops:
  0.0 2.3 %up.1 = (bf16[32,4096]{1,0:T(8,128)(2,1)S(1)}, f32[64,64,126]{2,1,0:T(8,128)S(1)}, f32[32,512]{1,0:T(8,128)S(1)}, f32[32,256]{1,0:T(8,128)S(1)}, f32[32,128]{1,0...) custom-call(bf16[32,4096]{1,0:T(8,128)(2,1)} %rhs_hbm.1, ...), custom_call_target="tpu_custom_call" | custom-call | tf_op jit(solution)/shard_map/up/pallas_call | solution.py:121
  2.3 2.2 %collective-permute-start = (bf16[32,1152]{1,0:T(8,128)(2,1)S(1)}, bf16[32,1152]{1,0:T(8,128)(2,1)S(1)}, u32[]{:S(2)}, u32[]{:S(2)}) collective-permute-start(bf16[32,1152]{1,0:T(8,128)(2,1)S(1)} %get-tuple-element.24), channel_id=1, source_target_pairs={{0,4},{4,0},{8,12},{12,8},{16,20},{20,16},{24,28},{28,24},{32,36},... | collective-permute-start | bytes 221192 | tf_op jit(solution)/shard_map/ppermute | solution.py:40
  4.5 0.7 %collective-permute-start.3 = (bf16[32,1024]{1,0:T(8,128)(2,1)S(1)}, bf16[32,1024]{1,0:T(8,128)(2,1)S(1)}, u32[]{:S(2)}, u32[]{:S(2)}) collective-permute-start(bf16[32,1024]{1,0:T(8,128)(2,1)S(1)} %get-tuple-element.31), channel_id=1, source_target_pairs={{4,8},{12,16},{20,24},{28,32},{36,40},{44,48},{52,56},{60,64},{68,... | collective-permute-start | bytes 196616 | tf_op jit(solution)/shard_map/ppermute | solution.py:509
  5.1 0.8 %pick.1.mats = f32[5,128,64]{2,1,0:T(8,128)S(1)} custom-call(f32[64,64,126]{2,1,0:T(8,128)S(1)} %get-tuple-element.25.tree), custom_call_target="tpu_custom_call" | custom-call | tf_op jit(solution)/shard_map/pick/pallas_call | solution.py:201
  5.9 0.3 collective-permute-done.packet.refs_0_
  6.2 0.3 lift.5
  6.5 3.6 %collective-permute-start.1 = (f32[32,64]{1,0:T(8,128)S(1)}, f32[32,64]{1,0:T(8,128)S(1)}, u32[]{:S(2)}, u32[]{:S(2)}) collective-permute-start(f32[32,64]{1,0:T(8,128)S(1)} %get-tuple-element.26.after.current), channel_id=1, source_target_pairs={{0,8},{4,12},{8,0},{12,4},{16,24},{20,28},{24,16},{28,20},{32,40},... | collective-permute-start | bytes 24584 | tf_op jit(solution)/shard_map/ppermute | solution.py:40
  10.1 2.7 %collective-permute-start.5 = (bf16[32,4096]{1,0:T(8,128)(2,1)S(1)}, bf16[32,4096]{1,0:T(8,128)(2,1)S(1)}, u32[]{:S(2)}, u32[]{:S(2)}) collective-permute-start(bf16[32,4096]{1,0:T(8,128)(2,1)S(1)} %copy-done.5), channel_id=1, source_target_pairs={{0,2},{1,3},{2,0},{3,1},{4,6},{5,7},{6,4},{7,5},{8,10},{9,11},{10,... | collective-permute-start | bytes 786440 | tf_op jit(solution)/shard_map/ppermute | solution.py:40
  12.8 2.5 %prep.1 = (f32[32,512]{1,0:T(8,128)S(1)}, f32[512,64]{1,0:T(8,128)S(1)}) custom-call(f32[32,512]{1,0:T(8,128)S(1)} %get-tuple-element.27.coeffs, f32[32,256]{1,0:T(8,128)S(1)} %get-tuple-element.28.second, f32[32,128]{1,0:T(8,128)S(1)} %get-tuple-element.29.first, f32[32,64]{1,0:T(8,128)S(1)} %get-tuple-element.26.after.current, f32[4,128,64]{2,1,0:T(8,128)} %bitcast.11, ...), custom_call_target="tpu_custom_call" | custom-call | tf_op jit(solution)/shard_map/prep/pallas_call | solution.py:310
  15.5 1.7 %collective-permute-start.2 = (f32[32,64]{1,0:T(8,128)S(1)}, f32[32,64]{1,0:T(8,128)S(1)}, u32[]{:S(2)}, u32[]{:S(2)}) collective-permute-start(f32[32,64]{1,0:T(8,128)S(1)} %lift.6.refs_2_.current), channel_id=1, source_target_pairs={{0,16},{4,20},{8,24},{12,28},{16,0},{20,4},{24,8},{28,12},{32,48},... | collective-permute-start | bytes 24584 | tf_op jit(solution)/shard_map/ppermute | solution.py:40
  17.3 0.8 %collective-permute-start.6 = (bf16[32,2048]{1,0:T(8,128)(2,1)S(1)}, bf16[32,2048]{1,0:T(8,128)(2,1)S(1)}, u32[]{:S(2)}, u32[]{:S(2)}) collective-permute-start(bf16[32,2048]{1,0:T(8,128)(2,1)S(1)} %join.2.rest_0_.refs_1_.edge), channel_id=1, source_target_pairs={{0,2},{1,3},{2,0},{3,1},{4,6},{5,7},{6,4},{7,5},{8,10},{9,11},{10,... | collective-permute-start | bytes 393224 | tf_op jit(solution)/shard_map/ppermute | solution.py:40
  18.0 0.6 %collective-permute-done.2.other.refs_2_ = f32[32,64]{1,0:T(8,128)S(1)} collective-permute-done((f32[32,64]{1,0:T(8,128)S(1)}, f32[32,64]{1,0:T(8,128)S(1)}, u32[]{:S(2)}, u32[]{:S(2)}) %collective-permute-start.2) | collective-permute-done | bytes 8224 | tf_op jit(solution)/shard_map/ppermute | solution.py:40
  18.8 3.0 %collective-permute-start.4 = (f32[32,64]{1,0:T(8,128)S(1)}, f32[32,64]{1,0:T(8,128)S(1)}, u32[]{:S(2)}, u32[]{:S(2)}) collective-permute-start(f32[32,64]{1,0:T(8,128)S(1)} %lift.7.refs_3_.after.current), channel_id=1, source_target_pairs={{0,32},{4,36},{8,40},{12,44},{16,48},{20,52},{24,56},{28,60},{32,0... | collective-permute-start | bytes 24584 | tf_op jit(solution)/shard_map/ppermute | solution.py:40
  21.8 2.8 %collective-permute-start.8 = (bf16[32,4096]{1,0:T(8,128)(2,1)S(1)}, bf16[32,4096]{1,0:T(8,128)(2,1)S(1)}, u32[]{:S(2)}, u32[]{:S(2)}) collective-permute-start(bf16[32,4096]{1,0:T(8,128)(2,1)S(1)} %copy-done.5), channel_id=1, source_target_pairs={{0,1},{1,0},{2,3},{3,2},{4,5},{5,4},{6,7},{7,6},{8,9},{9,8},{10,11... | collective-permute-start | bytes 786440 | tf_op jit(solution)/shard_map/ppermute | solution.py:40
  24.7 1.5 %turn.1.rest_1_.refs_5_ = f32[6,64,64]{2,1,0:T(8,128)S(1)} custom-call(f32[5,128,64]{2,1,0:T(8,128)S(1)} %pick.1.mats, f32[64,64,126]{2,1,0:T(8,128)S(1)} %bitcast.7, f32[32,64]{1,0:T(8,128)S(1)} %lift.7.refs_3_.after.current), custom_call_target="tpu_custom_call" | custom-call | tf_op jit(solution)/shard_map/turn/pallas_call | solution.py:341
  26.6 5.8 %collective-permute-start.7 = (f32[32,64]{1,0:T(8,128)S(1)}, f32[32,64]{1,0:T(8,128)S(1)}, u32[]{:S(2)}, u32[]{:S(2)}) collective-permute-start(f32[32,64]{1,0:T(8,128)S(1)} %lift.8.after.current), channel_id=1, source_target_pairs={{0,64},{4,68},{8,72},{12,76},{16,80},{20,84},{24,88},{28,92},{32,9... | collective-permute-start | bytes 24584 | tf_op jit(solution)/shard_map/ppermute | solution.py:40
  32.5 1.7 %near.2 = (f32[32,1024]{1,0:T(8,128)S(1)}, bf16[32,1024]{1,0:T(8,128)(2,1)S(1)}, bf16[32,1024]{1,0:T(8,128)(2,1)S(1)}, bf16[32,1024]{1,0:T(8,128)(2,1)S(1)}) custom-call(s32[2,8]{1,0:T(2,128)S(1)} %bitcast.8, bf16[32,4096]{1,0:T(8,128)(2,1)S(1)} %get-tuple-element.32.own, bf16[32,4096]{1,0:T(8,128)(2,1)S(1)} %collective-permute-done.8.mate, ...), custom_call_target="tpu_custom_call" | custom-call | tf_op jit(solution)/shard_map/near/pallas_call | solution.py:393
  34.2 2.1 %collective-permute-start.11 = (bf16[32,1024]{1,0:T(8,128)(2,1)S(1)}, bf16[32,1024]{1,0:T(8,128)(2,1)S(1)}, u32[]{:S(2)}, u32[]{:S(2)}) collective-permute-start(bf16[32,1024]{1,0:T(8,128)(2,1)S(1)} %get-tuple-element.38), channel_id=1, source_target_pairs={{0,3},{1,2},{2,1},{3,0},{4,7},{5,6},{6,5},{7,4},{8,11},{9,10},{10,... | collective-permute-start | bytes 196616 | tf_op jit(solution)/shard_map/ppermute | solution.py:40
  36.2 1.8 %collective-permute-start.12 = (bf16[32,1024]{1,0:T(8,128)(2,1)S(1)}, bf16[32,1024]{1,0:T(8,128)(2,1)S(1)}, u32[]{:S(2)}, u32[]{:S(2)}) collective-permute-start(bf16[32,1024]{1,0:T(8,128)(2,1)S(1)} %get-tuple-element.39), channel_id=1, source_target_pairs={{0,2},{1,3},{2,0},{3,1},{4,6},{5,7},{6,4},{7,5},{8,10},{9,11},{10,... | collective-permute-start | bytes 196616 | tf_op jit(solution)/shard_map/ppermute | solution.py:40
  38.1 0.2 lift.9
  38.3 0.3 collective-permute-start.10
  38.6 0.8 %settle.1 = (f32[32,512]{1,0:T(8,128)S(1)}, f32[512,64]{1,0:T(8,128)S(1)}) custom-call(f32[32,64]{1,0:T(8,128)S(1)} %get-tuple-element.34.refs_0_, f32[32,64]{1,0:T(8,128)S(1)} %collective-permute-done.1.other.refs_1_, f32[32,64]{1,0:T(8,128)S(1)} %collective-permute-done.2.other.refs_2_, f32[32,64]{1,0:T(8,128)S(1)} %collective-permute-done.4.other.refs_3_, ...), custom_call_target="tpu_custom_call" | custom-call | tf_op jit(solution)/shard_map/settle/pallas_call | solution.py:418
  39.4 1.8 %collective-permute-done.10.other = f32[32,64]{1,0:T(8,128)S(1)} collective-permute-done((f32[32,64]{1,0:T(8,128)S(1)}, f32[32,64]{1,0:T(8,128)S(1)}, u32[]{:S(2)}, u32[]{:S(2)}) %collective-permute-start.10) | collective-permute-done | bytes 8224 | tf_op jit(solution)/shard_map/ppermute | solution.py:40
  41.2 1.3 %last.1 = f32[32,4096]{1,0:T(8,128)} custom-call(f32[32,64]{1,0:T(8,128)S(1)} %collective-permute-done.10.other, f32[512,64]{1,0:T(8,128)S(1)} %get-tuple-element.36.final, f32[32,512]{1,0:T(8,128)S(1)} %get-tuple-element.37.local, bf16[64,4096]{1,0:T(8,128)(2,1)S(1)} %copy-done.3, f32[32,1024]{1,0:T(8,128)S(1)} %get-tuple-element.33.rest_0_, ...), custom_call_target="tpu_custom_call" | custom-call | tf_op jit(solution)/shard_map/last/pallas_call | solution.py:459
  (30 shorter events, 0.9 us)
Async XLA Ops:
  2.3 4.0 %collective-permute-start = (bf16[32,1152]{1,0:T(8,128)(2,1)S(1)}, bf16[32,1152]{1,0:T(8,128)(2,1)S(1)}, u32[]{:S(2)}, u32[]{:S(2)}) collective-permute-start(bf16[32,1152]{1,0:T(8,128)(2,1)S(1)} %get-tuple-element.24), channel_id=1, source_target_pairs={{0,4},{4,0},{8,12},{12,8},{16,20},{20,16},{24,28},{28,24},{32,36},... | collective-permute-start | bytes 221192 | tf_op jit(solution)/shard_map/ppermute | solution.py:40
  4.5 12.7 %collective-permute-start.3 = (bf16[32,1024]{1,0:T(8,128)(2,1)S(1)}, bf16[32,1024]{1,0:T(8,128)(2,1)S(1)}, u32[]{:S(2)}, u32[]{:S(2)}) collective-permute-start(bf16[32,1024]{1,0:T(8,128)(2,1)S(1)} %get-tuple-element.31), channel_id=1, source_target_pairs={{4,8},{12,16},{20,24},{28,32},{36,40},{44,48},{52,56},{60,64},{68,... | collective-permute-start | bytes 196616 | tf_op jit(solution)/shard_map/ppermute | solution.py:509
  6.2 3.9 %copy-start.5 = (bf16[32,4096]{1,0:T(8,128)(2,1)S(1)}, bf16[32,4096]{1,0:T(8,128)(2,1)}, u32[]{:S(2)}) copy-start(bf16[32,4096]{1,0:T(8,128)(2,1)} %rhs_hbm.1) | copy-start | bytes 786436
  6.5 8.9 %collective-permute-start.1 = (f32[32,64]{1,0:T(8,128)S(1)}, f32[32,64]{1,0:T(8,128)S(1)}, u32[]{:S(2)}, u32[]{:S(2)}) collective-permute-start(f32[32,64]{1,0:T(8,128)S(1)} %get-tuple-element.26.after.current), channel_id=1, source_target_pairs={{0,8},{4,12},{8,0},{12,4},{16,24},{20,28},{24,16},{28,20},{32,40},... | collective-permute-start | bytes 24584 | tf_op jit(solution)/shard_map/ppermute | solution.py:40
  10.1 16.1 %collective-permute-start.5 = (bf16[32,4096]{1,0:T(8,128)(2,1)S(1)}, bf16[32,4096]{1,0:T(8,128)(2,1)S(1)}, u32[]{:S(2)}, u32[]{:S(2)}) collective-permute-start(bf16[32,4096]{1,0:T(8,128)(2,1)S(1)} %copy-done.5), channel_id=1, source_target_pairs={{0,2},{1,3},{2,0},{3,1},{4,6},{5,7},{6,4},{7,5},{8,10},{9,11},{10,... | collective-permute-start | bytes 786440 | tf_op jit(solution)/shard_map/ppermute | solution.py:40
  15.5 3.1 %collective-permute-start.2 = (f32[32,64]{1,0:T(8,128)S(1)}, f32[32,64]{1,0:T(8,128)S(1)}, u32[]{:S(2)}, u32[]{:S(2)}) collective-permute-start(f32[32,64]{1,0:T(8,128)S(1)} %lift.6.refs_2_.current), channel_id=1, source_target_pairs={{0,16},{4,20},{8,24},{12,28},{16,0},{20,4},{24,8},{28,12},{32,48},... | collective-permute-start | bytes 24584 | tf_op jit(solution)/shard_map/ppermute | solution.py:40
  17.3 7.4 %copy-start = (f32[126,64,64]{0,2,1:T(8,128)S(1)}, f32[126,64,64]{0,2,1:T(8,128)}, u32[]{:S(2)}) copy-start(f32[126,64,64]{0,2,1:T(8,128)} %param.20) | copy-start | bytes 6193156
  17.3 8.9 %collective-permute-start.6 = (bf16[32,2048]{1,0:T(8,128)(2,1)S(1)}, bf16[32,2048]{1,0:T(8,128)(2,1)S(1)}, u32[]{:S(2)}, u32[]{:S(2)}) collective-permute-start(bf16[32,2048]{1,0:T(8,128)(2,1)S(1)} %join.2.rest_0_.refs_1_.edge), channel_id=1, source_target_pairs={{0,2},{1,3},{2,0},{3,1},{4,6},{5,7},{6,4},{7,5},{8,10},{9,11},{10,... | collective-permute-start | bytes 393224 | tf_op jit(solution)/shard_map/ppermute | solution.py:40
  18.8 7.6 %collective-permute-start.4 = (f32[32,64]{1,0:T(8,128)S(1)}, f32[32,64]{1,0:T(8,128)S(1)}, u32[]{:S(2)}, u32[]{:S(2)}) collective-permute-start(f32[32,64]{1,0:T(8,128)S(1)} %lift.7.refs_3_.after.current), channel_id=1, source_target_pairs={{0,32},{4,36},{8,40},{12,44},{16,48},{20,52},{24,56},{28,60},{32,0... | collective-permute-start | bytes 24584 | tf_op jit(solution)/shard_map/ppermute | solution.py:40
  21.8 10.7 %collective-permute-start.8 = (bf16[32,4096]{1,0:T(8,128)(2,1)S(1)}, bf16[32,4096]{1,0:T(8,128)(2,1)S(1)}, u32[]{:S(2)}, u32[]{:S(2)}) collective-permute-start(bf16[32,4096]{1,0:T(8,128)(2,1)S(1)} %copy-done.5), channel_id=1, source_target_pairs={{0,1},{1,0},{2,3},{3,2},{4,5},{5,4},{6,7},{7,6},{8,9},{9,8},{10,11... | collective-permute-start | bytes 786440 | tf_op jit(solution)/shard_map/ppermute | solution.py:40
  26.3 6.2 %copy-start.1 = (bf16[8,2,128,512]{3,2,1,0:T(8,128)(2,1)S(1)}, bf16[8,2,128,512]{3,2,1,0:T(8,128)(2,1)}, u32[]{:S(2)}) copy-start(bf16[8,2,128,512]{3,2,1,0:T(8,128)(2,1)} %near.3) | copy-start | bytes 6291460
  26.3 6.2 %copy-start.2 = (bf16[8,128,512]{2,1,0:T(8,128)(2,1)S(1)}, bf16[8,128,512]{2,1,0:T(8,128)(2,1)}, u32[]{:S(2)}) copy-start(bf16[8,128,512]{2,1,0:T(8,128)(2,1)} %diag.1) | copy-start | bytes 3145732
  26.3 6.2 %copy-start.4 = (s32[8,2]{0,1:T(2,128)S(1)}, s32[8,2]{0,1:T(2,128)}, u32[]{:S(2)}) copy-start(s32[8,2]{0,1:T(2,128)} %param.23) | copy-start | bytes 196
  26.3 6.1 %collective-permute-start.9 = (bf16[32,8192]{1,0:T(8,128)(2,1)S(1)}, bf16[32,8192]{1,0:T(8,128)(2,1)S(1)}, u32[]{:S(2)}, u32[]{:S(2)}) collective-permute-start(bf16[32,8192]{1,0:T(8,128)(2,1)S(1)} %join.3.rest_0_), channel_id=1, source_target_pairs={{0,1},{1,0},{2,3},{3,2},{4,5},{5,4},{6,7},{7,6},{8,9},{9,8},{10,11... | collective-permute-start | bytes 1572872 | tf_op jit(solution)/shard_map/ppermute | solution.py:40
  26.6 11.4 %collective-permute-start.7 = (f32[32,64]{1,0:T(8,128)S(1)}, f32[32,64]{1,0:T(8,128)S(1)}, u32[]{:S(2)}, u32[]{:S(2)}) collective-permute-start(f32[32,64]{1,0:T(8,128)S(1)} %lift.8.after.current), channel_id=1, source_target_pairs={{0,64},{4,68},{8,72},{12,76},{16,80},{20,84},{24,88},{28,92},{32,9... | collective-permute-start | bytes 24584 | tf_op jit(solution)/shard_map/ppermute | solution.py:40
  34.2 7.0 %collective-permute-start.11 = (bf16[32,1024]{1,0:T(8,128)(2,1)S(1)}, bf16[32,1024]{1,0:T(8,128)(2,1)S(1)}, u32[]{:S(2)}, u32[]{:S(2)}) collective-permute-start(bf16[32,1024]{1,0:T(8,128)(2,1)S(1)} %get-tuple-element.38), channel_id=1, source_target_pairs={{0,3},{1,2},{2,1},{3,0},{4,7},{5,6},{6,5},{7,4},{8,11},{9,10},{10,... | collective-permute-start | bytes 196616 | tf_op jit(solution)/shard_map/ppermute | solution.py:40
  36.2 5.0 %collective-permute-start.12 = (bf16[32,1024]{1,0:T(8,128)(2,1)S(1)}, bf16[32,1024]{1,0:T(8,128)(2,1)S(1)}, u32[]{:S(2)}, u32[]{:S(2)}) collective-permute-start(bf16[32,1024]{1,0:T(8,128)(2,1)S(1)} %get-tuple-element.39), channel_id=1, source_target_pairs={{0,2},{1,3},{2,0},{3,1},{4,6},{5,7},{6,4},{7,5},{8,10},{9,11},{10,... | collective-permute-start | bytes 196616 | tf_op jit(solution)/shard_map/ppermute | solution.py:40
  38.1 3.1 %collective-permute-start.13 = (bf16[32,1024]{1,0:T(8,128)(2,1)S(1)}, bf16[32,1024]{1,0:T(8,128)(2,1)S(1)}, u32[]{:S(2)}, u32[]{:S(2)}) collective-permute-start(bf16[32,1024]{1,0:T(8,128)(2,1)S(1)} %get-tuple-element.40), channel_id=1, source_target_pairs={{0,1},{1,0},{2,3},{3,2},{4,5},{5,4},{6,7},{7,6},{8,9},{9,8},{10,11... | collective-permute-start | bytes 196616 | tf_op jit(solution)/shard_map/ppermute | solution.py:40
  38.1 3.1 %copy-start.3 = (bf16[64,4096]{1,0:T(8,128)(2,1)S(1)}, bf16[64,4096]{1,0:T(8,128)(2,1)}, u32[]{:S(2)}) copy-start(bf16[64,4096]{1,0:T(8,128)(2,1)} %basis.1) | copy-start | bytes 1572868
  38.3 2.9 %collective-permute-start.10 = (f32[32,64]{1,0:T(8,128)S(1)}, f32[32,64]{1,0:T(8,128)S(1)}, u32[]{:S(2)}, u32[]{:S(2)}) collective-permute-start(f32[32,64]{1,0:T(8,128)S(1)} %lift.9), channel_id=1, source_target_pairs={{0,128},{4,132},{8,136},{12,140},{16,144},{20,148},{24,152},{28,15... | collective-permute-start | bytes 24584 | tf_op jit(solution)/shard_map/ppermute | solution.py:40

commit v6 on v5

--- a/solution.py
+++ b/solution.py
@@ -172,7 +172,7 @@
     dot = functools.partial(
         lax.dot_general, select, dimension_numbers=TURNED, preferred_element_type=F32
     )
-    group = 4
+    group = 8
     for k in range(0, skel, group):
         top, low = halves(table[k : k + group].reshape(group * skel, nodes))
         rows = dot(top) + dot(low)

time: 42.7 us -> 42.7 us (level)
  no operation moved by 1% of the time
where the time goes in v6:
time: 42.7 us; the launch traced here: 42.5 us
  starting transfers between devices  27.6 us (65%)
  Pallas kernels  11.9 us (28%)
  waiting for transfers between devices  2.73 us (6%)
    ppermute x13, starting transfers between devices, swapped(): return lax.ppermute(x, axis, [(i, i ^ bit) for i in range(count)])  27 us
    ppermute x13, waiting for transfers between devices, swapped(): return lax.ppermute(x, axis, [(i, i ^ bit) for i in range(count)])  2.73 us
    pallas_call x1, Pallas kernels, run_prep(): pl.pallas_call(prep_kernel, in_specs=[VMEM] * 3 + [ANY] * 5, out_specs=[V...  2.5 us
    pallas_call x1, Pallas kernels, run_up(): pl.pallas_call(up_kernel, in_specs=[ANY] * 5, out_specs=[VMEM] * 8, out_s...  2.25 us
    pallas_call x1, Pallas kernels, run_near(): pl.pallas_call(near_kernel, in_specs=[pl.BlockSpec(memory_space=pltpu.SME...  1.66 us
    pallas_call x1, Pallas kernels, run_turn(): pl.pallas_call(functools.partial(turn_kernel, depth), in_specs=[VMEM] * 2...  1.48 us
    pallas_call x1, Pallas kernels, run_last(): pl.pallas_call(functools.partial(last_kernel, groups), in_specs=[VMEM] *...  1.3 us
  transfers between devices with their start and end apart: 14, of which 3 were waited for; matrix products, arithmetic and copies ran while one was open for 0% of the time, Pallas kernels for 20%

profile of v6, /device:TPU:1, one launch (start us, length us, event | category | flops | bytes accessed | tf_op | source)
XLA Modules:
  0.0 42.5 jit_solution(3527009121595478038)
XLA Ops:
  0.0 2.3 %up.1 = (bf16[32,4096]{1,0:T(8,128)(2,1)S(1)}, f32[64,64,126]{2,1,0:T(8,128)S(1)}, f32[32,512]{1,0:T(8,128)S(1)}, f32[32,256]{1,0:T(8,128)S(1)}, f32[32,128]{1,0...) custom-call(bf16[32,4096]{1,0:T(8,128)(2,1)} %rhs_hbm.1, ...), custom_call_target="tpu_custom_call" | custom-call | tf_op jit(solution)/shard_map/up/pallas_call | solution.py:121
  2.3 2.2 %collective-permute-start = (bf16[32,1152]{1,0:T(8,128)(2,1)S(1)}, bf16[32,1152]{1,0:T(8,128)(2,1)S(1)}, u32[]{:S(2)}, u32[]{:S(2)}) collective-permute-start(bf16[32,1152]{1,0:T(8,128)(2,1)S(1)} %get-tuple-element.24), channel_id=1, source_target_pairs={{0,4},{4,0},{8,12},{12,8},{16,20},{20,16},{24,28},{28,24},{32,36},... | collective-permute-start | bytes 221192 | tf_op jit(solution)/shard_map/ppermute | solution.py:40
  4.5 0.7 %collective-permute-start.3 = (bf16[32,1024]{1,0:T(8,128)(2,1)S(1)}, bf16[32,1024]{1,0:T(8,128)(2,1)S(1)}, u32[]{:S(2)}, u32[]{:S(2)}) collective-permute-start(bf16[32,1024]{1,0:T(8,128)(2,1)S(1)} %get-tuple-element.31), channel_id=1, source_target_pairs={{4,8},{12,16},{20,24},{28,32},{36,40},{44,48},{52,56},{60,64},{68,... | collective-permute-start | bytes 196616 | tf_op jit(solution)/shard_map/ppermute | solution.py:509
  5.1 0.8 %pick.1.mats = f32[5,128,64]{2,1,0:T(8,128)S(1)} custom-call(f32[64,64,126]{2,1,0:T(8,128)S(1)} %get-tuple-element.25.tree), custom_call_target="tpu_custom_call" | custom-call | tf_op jit(solution)/shard_map/pick/pallas_call | solution.py:201
  5.9 0.3 collective-permute-done.packet.refs_0_
  6.2 0.3 lift.5
  6.5 3.6 %collective-permute-start.1 = (f32[32,64]{1,0:T(8,128)S(1)}, f32[32,64]{1,0:T(8,128)S(1)}, u32[]{:S(2)}, u32[]{:S(2)}) collective-permute-start(f32[32,64]{1,0:T(8,128)S(1)} %get-tuple-element.26.after.current), channel_id=1, source_target_pairs={{0,8},{4,12},{8,0},{12,4},{16,24},{20,28},{24,16},{28,20},{32,40},... | collective-permute-start | bytes 24584 | tf_op jit(solution)/shard_map/ppermute | solution.py:40
  10.1 2.7 %collective-permute-start.5 = (bf16[32,4096]{1,0:T(8,128)(2,1)S(1)}, bf16[32,4096]{1,0:T(8,128)(2,1)S(1)}, u32[]{:S(2)}, u32[]{:S(2)}) collective-permute-start(bf16[32,4096]{1,0:T(8,128)(2,1)S(1)} %copy-done.5), channel_id=1, source_target_pairs={{0,2},{1,3},{2,0},{3,1},{4,6},{5,7},{6,4},{7,5},{8,10},{9,11},{10,... | collective-permute-start | bytes 786440 | tf_op jit(solution)/shard_map/ppermute | solution.py:40
  12.8 2.5 %prep.1 = (f32[32,512]{1,0:T(8,128)S(1)}, f32[512,64]{1,0:T(8,128)S(1)}) custom-call(f32[32,512]{1,0:T(8,128)S(1)} %get-tuple-element.27.coeffs, f32[32,256]{1,0:T(8,128)S(1)} %get-tuple-element.28.second, f32[32,128]{1,0:T(8,128)S(1)} %get-tuple-element.29.first, f32[32,64]{1,0:T(8,128)S(1)} %get-tuple-element.26.after.current, f32[4,128,64]{2,1,0:T(8,128)} %bitcast.11, ...), custom_call_target="tpu_custom_call" | custom-call | tf_op jit(solution)/shard_map/prep/pallas_call | solution.py:310
  15.5 1.7 %collective-permute-start.2 = (f32[32,64]{1,0:T(8,128)S(1)}, f32[32,64]{1,0:T(8,128)S(1)}, u32[]{:S(2)}, u32[]{:S(2)}) collective-permute-start(f32[32,64]{1,0:T(8,128)S(1)} %lift.6.refs_2_.current), channel_id=1, source_target_pairs={{0,16},{4,20},{8,24},{12,28},{16,0},{20,4},{24,8},{28,12},{32,48},... | collective-permute-start | bytes 24584 | tf_op jit(solution)/shard_map/ppermute | solution.py:40
  17.3 0.8 %collective-permute-start.6 = (bf16[32,2048]{1,0:T(8,128)(2,1)S(1)}, bf16[32,2048]{1,0:T(8,128)(2,1)S(1)}, u32[]{:S(2)}, u32[]{:S(2)}) collective-permute-start(bf16[32,2048]{1,0:T(8,128)(2,1)S(1)} %join.2.rest_0_.refs_1_.edge), channel_id=1, source_target_pairs={{0,2},{1,3},{2,0},{3,1},{4,6},{5,7},{6,4},{7,5},{8,10},{9,11},{10,... | collective-permute-start | bytes 393224 | tf_op jit(solution)/shard_map/ppermute | solution.py:40
  18.0 0.6 %collective-permute-done.2.other.refs_2_ = f32[32,64]{1,0:T(8,128)S(1)} collective-permute-done((f32[32,64]{1,0:T(8,128)S(1)}, f32[32,64]{1,0:T(8,128)S(1)}, u32[]{:S(2)}, u32[]{:S(2)}) %collective-permute-start.2) | collective-permute-done | bytes 8224 | tf_op jit(solution)/shard_map/ppermute | solution.py:40
  18.8 3.0 %collective-permute-start.4 = (f32[32,64]{1,0:T(8,128)S(1)}, f32[32,64]{1,0:T(8,128)S(1)}, u32[]{:S(2)}, u32[]{:S(2)}) collective-permute-start(f32[32,64]{1,0:T(8,128)S(1)} %lift.7.refs_3_.after.current), channel_id=1, source_target_pairs={{0,32},{4,36},{8,40},{12,44},{16,48},{20,52},{24,56},{28,60},{32,0... | collective-permute-start | bytes 24584 | tf_op jit(solution)/shard_map/ppermute | solution.py:40
  21.8 2.8 %collective-permute-start.8 = (bf16[32,4096]{1,0:T(8,128)(2,1)S(1)}, bf16[32,4096]{1,0:T(8,128)(2,1)S(1)}, u32[]{:S(2)}, u32[]{:S(2)}) collective-permute-start(bf16[32,4096]{1,0:T(8,128)(2,1)S(1)} %copy-done.5), channel_id=1, source_target_pairs={{0,1},{1,0},{2,3},{3,2},{4,5},{5,4},{6,7},{7,6},{8,9},{9,8},{10,11... | collective-permute-start | bytes 786440 | tf_op jit(solution)/shard_map/ppermute | solution.py:40
  24.7 1.5 %turn.1.rest_1_.refs_5_ = f32[6,64,64]{2,1,0:T(8,128)S(1)} custom-call(f32[5,128,64]{2,1,0:T(8,128)S(1)} %pick.1.mats, f32[64,64,126]{2,1,0:T(8,128)S(1)} %bitcast.7, f32[32,64]{1,0:T(8,128)S(1)} %lift.7.refs_3_.after.current), custom_call_target="tpu_custom_call" | custom-call | tf_op jit(solution)/shard_map/turn/pallas_call | solution.py:341
  26.6 5.8 %collective-permute-start.7 = (f32[32,64]{1,0:T(8,128)S(1)}, f32[32,64]{1,0:T(8,128)S(1)}, u32[]{:S(2)}, u32[]{:S(2)}) collective-permute-start(f32[32,64]{1,0:T(8,128)S(1)} %lift.8.after.current), channel_id=1, source_target_pairs={{0,64},{4,68},{8,72},{12,76},{16,80},{20,84},{24,88},{28,92},{32,9... | collective-permute-start | bytes 24584 | tf_op jit(solution)/shard_map/ppermute | solution.py:40
  32.5 1.7 %near.2 = (f32[32,1024]{1,0:T(8,128)S(1)}, bf16[32,1024]{1,0:T(8,128)(2,1)S(1)}, bf16[32,1024]{1,0:T(8,128)(2,1)S(1)}, bf16[32,1024]{1,0:T(8,128)(2,1)S(1)}) custom-call(s32[2,8]{1,0:T(2,128)S(1)} %bitcast.8, bf16[32,4096]{1,0:T(8,128)(2,1)S(1)} %get-tuple-element.32.own, bf16[32,4096]{1,0:T(8,128)(2,1)S(1)} %collective-permute-done.8.mate, ...), custom_call_target="tpu_custom_call" | custom-call | tf_op jit(solution)/shard_map/near/pallas_call | solution.py:393
  34.2 2.1 %collective-permute-start.11 = (bf16[32,1024]{1,0:T(8,128)(2,1)S(1)}, bf16[32,1024]{1,0:T(8,128)(2,1)S(1)}, u32[]{:S(2)}, u32[]{:S(2)}) collective-permute-start(bf16[32,1024]{1,0:T(8,128)(2,1)S(1)} %get-tuple-element.38), channel_id=1, source_target_pairs={{0,3},{1,2},{2,1},{3,0},{4,7},{5,6},{6,5},{7,4},{8,11},{9,10},{10,... | collective-permute-start | bytes 196616 | tf_op jit(solution)/shard_map/ppermute | solution.py:40
  36.2 1.8 %collective-permute-start.12 = (bf16[32,1024]{1,0:T(8,128)(2,1)S(1)}, bf16[32,1024]{1,0:T(8,128)(2,1)S(1)}, u32[]{:S(2)}, u32[]{:S(2)}) collective-permute-start(bf16[32,1024]{1,0:T(8,128)(2,1)S(1)} %get-tuple-element.39), channel_id=1, source_target_pairs={{0,2},{1,3},{2,0},{3,1},{4,6},{5,7},{6,4},{7,5},{8,10},{9,11},{10,... | collective-permute-start | bytes 196616 | tf_op jit(solution)/shard_map/ppermute | solution.py:40
  38.1 0.2 lift.9
  38.3 0.3 collective-permute-start.10
  38.6 0.8 %settle.1 = (f32[32,512]{1,0:T(8,128)S(1)}, f32[512,64]{1,0:T(8,128)S(1)}) custom-call(f32[32,64]{1,0:T(8,128)S(1)} %get-tuple-element.34.refs_0_, f32[32,64]{1,0:T(8,128)S(1)} %collective-permute-done.1.other.refs_1_, f32[32,64]{1,0:T(8,128)S(1)} %collective-permute-done.2.other.refs_2_, f32[32,64]{1,0:T(8,128)S(1)} %collective-permute-done.4.other.refs_3_, ...), custom_call_target="tpu_custom_call" | custom-call | tf_op jit(solution)/shard_map/settle/pallas_call | solution.py:418
  39.4 1.8 %collective-permute-done.10.other = f32[32,64]{1,0:T(8,128)S(1)} collective-permute-done((f32[32,64]{1,0:T(8,128)S(1)}, f32[32,64]{1,0:T(8,128)S(1)}, u32[]{:S(2)}, u32[]{:S(2)}) %collective-permute-start.10) | collective-permute-done | bytes 8224 | tf_op jit(solution)/shard_map/ppermute | solution.py:40
  41.2 1.3 %last.1 = f32[32,4096]{1,0:T(8,128)} custom-call(f32[32,64]{1,0:T(8,128)S(1)} %collective-permute-done.10.other, f32[512,64]{1,0:T(8,128)S(1)} %get-tuple-element.36.final, f32[32,512]{1,0:T(8,128)S(1)} %get-tuple-element.37.local, bf16[64,4096]{1,0:T(8,128)(2,1)S(1)} %copy-done.3, f32[32,1024]{1,0:T(8,128)S(1)} %get-tuple-element.33.rest_0_, ...), custom_call_target="tpu_custom_call" | custom-call | tf_op jit(solution)/shard_map/last/pallas_call | solution.py:459
  (30 shorter events, 0.9 us)
Async XLA Ops:
  2.3 4.0 %collective-permute-start = (bf16[32,1152]{1,0:T(8,128)(2,1)S(1)}, bf16[32,1152]{1,0:T(8,128)(2,1)S(1)}, u32[]{:S(2)}, u32[]{:S(2)}) collective-permute-start(bf16[32,1152]{1,0:T(8,128)(2,1)S(1)} %get-tuple-element.24), channel_id=1, source_target_pairs={{0,4},{4,0},{8,12},{12,8},{16,20},{20,16},{24,28},{28,24},{32,36},... | collective-permute-start | bytes 221192 | tf_op jit(solution)/shard_map/ppermute | solution.py:40
  4.5 12.7 %collective-permute-start.3 = (bf16[32,1024]{1,0:T(8,128)(2,1)S(1)}, bf16[32,1024]{1,0:T(8,128)(2,1)S(1)}, u32[]{:S(2)}, u32[]{:S(2)}) collective-permute-start(bf16[32,1024]{1,0:T(8,128)(2,1)S(1)} %get-tuple-element.31), channel_id=1, source_target_pairs={{4,8},{12,16},{20,24},{28,32},{36,40},{44,48},{52,56},{60,64},{68,... | collective-permute-start | bytes 196616 | tf_op jit(solution)/shard_map/ppermute | solution.py:509
  6.2 3.9 %copy-start.5 = (bf16[32,4096]{1,0:T(8,128)(2,1)S(1)}, bf16[32,4096]{1,0:T(8,128)(2,1)}, u32[]{:S(2)}) copy-start(bf16[32,4096]{1,0:T(8,128)(2,1)} %rhs_hbm.1) | copy-start | bytes 786436
  6.5 8.9 %collective-permute-start.1 = (f32[32,64]{1,0:T(8,128)S(1)}, f32[32,64]{1,0:T(8,128)S(1)}, u32[]{:S(2)}, u32[]{:S(2)}) collective-permute-start(f32[32,64]{1,0:T(8,128)S(1)} %get-tuple-element.26.after.current), channel_id=1, source_target_pairs={{0,8},{4,12},{8,0},{12,4},{16,24},{20,28},{24,16},{28,20},{32,40},... | collective-permute-start | bytes 24584 | tf_op jit(solution)/shard_map/ppermute | solution.py:40
  10.1 16.1 %collective-permute-start.5 = (bf16[32,4096]{1,0:T(8,128)(2,1)S(1)}, bf16[32,4096]{1,0:T(8,128)(2,1)S(1)}, u32[]{:S(2)}, u32[]{:S(2)}) collective-permute-start(bf16[32,4096]{1,0:T(8,128)(2,1)S(1)} %copy-done.5), channel_id=1, source_target_pairs={{0,2},{1,3},{2,0},{3,1},{4,6},{5,7},{6,4},{7,5},{8,10},{9,11},{10,... | collective-permute-start | bytes 786440 | tf_op jit(solution)/shard_map/ppermute | solution.py:40
  15.5 3.1 %collective-permute-start.2 = (f32[32,64]{1,0:T(8,128)S(1)}, f32[32,64]{1,0:T(8,128)S(1)}, u32[]{:S(2)}, u32[]{:S(2)}) collective-permute-start(f32[32,64]{1,0:T(8,128)S(1)} %lift.6.refs_2_.current), channel_id=1, source_target_pairs={{0,16},{4,20},{8,24},{12,28},{16,0},{20,4},{24,8},{28,12},{32,48},... | collective-permute-start | bytes 24584 | tf_op jit(solution)/shard_map/ppermute | solution.py:40
  17.3 7.4 %copy-start = (f32[126,64,64]{0,2,1:T(8,128)S(1)}, f32[126,64,64]{0,2,1:T(8,128)}, u32[]{:S(2)}) copy-start(f32[126,64,64]{0,2,1:T(8,128)} %param.20) | copy-start | bytes 6193156
  17.3 8.9 %collective-permute-start.6 = (bf16[32,2048]{1,0:T(8,128)(2,1)S(1)}, bf16[32,2048]{1,0:T(8,128)(2,1)S(1)}, u32[]{:S(2)}, u32[]{:S(2)}) collective-permute-start(bf16[32,2048]{1,0:T(8,128)(2,1)S(1)} %join.2.rest_0_.refs_1_.edge), channel_id=1, source_target_pairs={{0,2},{1,3},{2,0},{3,1},{4,6},{5,7},{6,4},{7,5},{8,10},{9,11},{10,... | collective-permute-start | bytes 393224 | tf_op jit(solution)/shard_map/ppermute | solution.py:40
  18.8 7.6 %collective-permute-start.4 = (f32[32,64]{1,0:T(8,128)S(1)}, f32[32,64]{1,0:T(8,128)S(1)}, u32[]{:S(2)}, u32[]{:S(2)}) collective-permute-start(f32[32,64]{1,0:T(8,128)S(1)} %lift.7.refs_3_.after.current), channel_id=1, source_target_pairs={{0,32},{4,36},{8,40},{12,44},{16,48},{20,52},{24,56},{28,60},{32,0... | collective-permute-start | bytes 24584 | tf_op jit(solution)/shard_map/ppermute | solution.py:40
  21.8 10.7 %collective-permute-start.8 = (bf16[32,4096]{1,0:T(8,128)(2,1)S(1)}, bf16[32,4096]{1,0:T(8,128)(2,1)S(1)}, u32[]{:S(2)}, u32[]{:S(2)}) collective-permute-start(bf16[32,4096]{1,0:T(8,128)(2,1)S(1)} %copy-done.5), channel_id=1, source_target_pairs={{0,1},{1,0},{2,3},{3,2},{4,5},{5,4},{6,7},{7,6},{8,9},{9,8},{10,11... | collective-permute-start | bytes 786440 | tf_op jit(solution)/shard_map/ppermute | solution.py:40
  26.3 6.2 %copy-start.1 = (bf16[8,2,128,512]{3,2,1,0:T(8,128)(2,1)S(1)}, bf16[8,2,128,512]{3,2,1,0:T(8,128)(2,1)}, u32[]{:S(2)}) copy-start(bf16[8,2,128,512]{3,2,1,0:T(8,128)(2,1)} %near.3) | copy-start | bytes 6291460
  26.3 6.2 %copy-start.2 = (bf16[8,128,512]{2,1,0:T(8,128)(2,1)S(1)}, bf16[8,128,512]{2,1,0:T(8,128)(2,1)}, u32[]{:S(2)}) copy-start(bf16[8,128,512]{2,1,0:T(8,128)(2,1)} %diag.1) | copy-start | bytes 3145732
  26.3 6.2 %copy-start.4 = (s32[8,2]{0,1:T(2,128)S(1)}, s32[8,2]{0,1:T(2,128)}, u32[]{:S(2)}) copy-start(s32[8,2]{0,1:T(2,128)} %param.23) | copy-start | bytes 196
  26.3 6.1 %collective-permute-start.9 = (bf16[32,8192]{1,0:T(8,128)(2,1)S(1)}, bf16[32,8192]{1,0:T(8,128)(2,1)S(1)}, u32[]{:S(2)}, u32[]{:S(2)}) collective-permute-start(bf16[32,8192]{1,0:T(8,128)(2,1)S(1)} %join.3.rest_0_), channel_id=1, source_target_pairs={{0,1},{1,0},{2,3},{3,2},{4,5},{5,4},{6,7},{7,6},{8,9},{9,8},{10,11... | collective-permute-start | bytes 1572872 | tf_op jit(solution)/shard_map/ppermute | solution.py:40
  26.6 11.4 %collective-permute-start.7 = (f32[32,64]{1,0:T(8,128)S(1)}, f32[32,64]{1,0:T(8,128)S(1)}, u32[]{:S(2)}, u32[]{:S(2)}) collective-permute-start(f32[32,64]{1,0:T(8,128)S(1)} %lift.8.after.current), channel_id=1, source_target_pairs={{0,64},{4,68},{8,72},{12,76},{16,80},{20,84},{24,88},{28,92},{32,9... | collective-permute-start | bytes 24584 | tf_op jit(solution)/shard_map/ppermute | solution.py:40
  34.2 7.0 %collective-permute-start.11 = (bf16[32,1024]{1,0:T(8,128)(2,1)S(1)}, bf16[32,1024]{1,0:T(8,128)(2,1)S(1)}, u32[]{:S(2)}, u32[]{:S(2)}) collective-permute-start(bf16[32,1024]{1,0:T(8,128)(2,1)S(1)} %get-tuple-element.38), channel_id=1, source_target_pairs={{0,3},{1,2},{2,1},{3,0},{4,7},{5,6},{6,5},{7,4},{8,11},{9,10},{10,... | collective-permute-start | bytes 196616 | tf_op jit(solution)/shard_map/ppermute | solution.py:40
  36.2 5.0 %collective-permute-start.12 = (bf16[32,1024]{1,0:T(8,128)(2,1)S(1)}, bf16[32,1024]{1,0:T(8,128)(2,1)S(1)}, u32[]{:S(2)}, u32[]{:S(2)}) collective-permute-start(bf16[32,1024]{1,0:T(8,128)(2,1)S(1)} %get-tuple-element.39), channel_id=1, source_target_pairs={{0,2},{1,3},{2,0},{3,1},{4,6},{5,7},{6,4},{7,5},{8,10},{9,11},{10,... | collective-permute-start | bytes 196616 | tf_op jit(solution)/shard_map/ppermute | solution.py:40
  38.1 3.1 %collective-permute-start.13 = (bf16[32,1024]{1,0:T(8,128)(2,1)S(1)}, bf16[32,1024]{1,0:T(8,128)(2,1)S(1)}, u32[]{:S(2)}, u32[]{:S(2)}) collective-permute-start(bf16[32,1024]{1,0:T(8,128)(2,1)S(1)} %get-tuple-element.40), channel_id=1, source_target_pairs={{0,1},{1,0},{2,3},{3,2},{4,5},{5,4},{6,7},{7,6},{8,9},{9,8},{10,11... | collective-permute-start | bytes 196616 | tf_op jit(solution)/shard_map/ppermute | solution.py:40
  38.1 3.1 %copy-start.3 = (bf16[64,4096]{1,0:T(8,128)(2,1)S(1)}, bf16[64,4096]{1,0:T(8,128)(2,1)}, u32[]{:S(2)}) copy-start(bf16[64,4096]{1,0:T(8,128)(2,1)} %basis.1) | copy-start | bytes 1572868
  38.3 2.9 %collective-permute-start.10 = (f32[32,64]{1,0:T(8,128)S(1)}, f32[32,64]{1,0:T(8,128)S(1)}, u32[]{:S(2)}, u32[]{:S(2)}) collective-permute-start(f32[32,64]{1,0:T(8,128)S(1)} %lift.9), channel_id=1, source_target_pairs={{0,128},{4,132},{8,136},{12,140},{16,144},{20,148},{24,152},{28,15... | collective-permute-start | bytes 24584 | tf_op jit(solution)/shard_map/ppermute | solution.py:40
